TPU v7x, 512 devices: a whole 4x4x16 slice. The times are simulated.
512 devices in a mesh: img: 16 (over z_lo, core), txt: 32 (over y, z_hi, x).
Axes of the slice: x: 4, y: 4, z: 16 (z_hi: 2, z_lo: 8; z = z_hi * 8 + z_lo), core: 2. Of those that a mesh axis runs over, the one named last changes fastest.
Arguments:
- image_feats: bfloat16 [8192, 768], P(('img', 'txt')), may hold values from -6 to 6
- text_feats: bfloat16 [8192, 512], P(('txt', 'img')), may hold values from -6 to 6
- teacher_img: bfloat16 [8192, 1024], P(('img', 'txt')), may hold values from -60 to 60, as said below
- teacher_txt: bfloat16 [8192, 1024], P(('txt', 'img')), may hold values from -60 to 60, as said below
- proj_img: bfloat16 [768, 512], replicated, may hold values from -0.21875 to 0.21875
- proj_txt: bfloat16 [512, 512], replicated, may hold values from -0.25 to 0.25
Outputs:
- loss: float32 [], replicated
- grad_img: float32 [768, 512], replicated
- grad_txt: float32 [512, 512], replicated
Inputs may be any that keep to these rules, and one draw needn't show every extreme that they name: `teacher_img`: raw teacher embeddings, rows of various scales. `teacher_txt`: raw teacher embeddings, rows of various scales.
All inputs are finite; a program needn't handle non-finite values.
Results may differ from a plain program's by a relative error of at most 0.0077.
Values may be sent and summed in bfloat16 or wider, within the bound.
No kernel may reach another device: no remote copies, remote signals or barrier semaphores. Data moves between devices by JAX's collectives and lax.ppermute only.
A program may use at most 64 MiB of HBM per device.

v0:
```python
import jax
import jax.numpy as jnp
from jax import lax
from jax.sharding import PartitionSpec as P

EPS = 1e-06
TEACHER_SCALE = 100.0
STUDENT_SCALE = 50.0


def project(feats, weight):
    u = jnp.dot(feats, weight, preferred_element_type=jnp.float32)
    inv = lax.rsqrt(jnp.sum(u * u, axis=1, keepdims=True) + EPS)
    return (u * inv, inv)


def normed(raw):
    x = raw.astype(jnp.float32)
    return (x * lax.rsqrt(jnp.sum(x * x, axis=1, keepdims=True) + EPS)).astype(jnp.bfloat16)


def tangent(grad_rows, embeds, inverse):
    return (grad_rows - embeds * jnp.sum(embeds * grad_rows, 1, keepdims=True)) * inverse


def weight_grad(feats, du_rows):
    return lax.dot_general(
        feats.astype(jnp.float32),
        du_rows,
        (((0,), (0,)), ((), ())),
        precision=lax.Precision.HIGHEST,
    )


def tile_terms(block_q_img, block_q_txt, block_s_img, block_s_txt):
    tl = TEACHER_SCALE * jnp.dot(block_q_img, block_q_txt.T, preferred_element_type=jnp.float32)
    sl = STUDENT_SCALE * jnp.dot(block_s_img, block_s_txt.T, preferred_element_type=jnp.float32)
    rtm, rsm = lax.pmax((tl.max(1), sl.max(1)), "txt")
    rts, rss = lax.psum(
        (jnp.sum(jnp.exp(tl - rtm[:, None]), 1), jnp.sum(jnp.exp(sl - rsm[:, None]), 1)), "txt"
    )
    ctm, csm = lax.pmax((tl.max(0), sl.max(0)), "img")
    cts, css = lax.psum(
        (jnp.sum(jnp.exp(tl - ctm[None, :]), 0), jnp.sum(jnp.exp(sl - csm[None, :]), 0)), "img"
    )
    pt_row = jnp.exp(tl - rtm[:, None]) / rts[:, None]
    ps_row = jnp.exp(sl - rsm[:, None]) / rss[:, None]
    pt_col = jnp.exp(tl - ctm[None, :]) / cts[None, :]
    ps_col = jnp.exp(sl - csm[None, :]) / css[None, :]
    diff = tl - sl
    n_img = lax.axis_size("img")
    n_txt = lax.axis_size("txt")
    local_term = jnp.sum(pt_row * diff) + jnp.sum(pt_col * diff)
    local_term = local_term + jnp.sum(rsm + jnp.log(rss) - rtm - jnp.log(rts)) / n_txt
    local_term = local_term + jnp.sum(csm + jnp.log(css) - ctm - jnp.log(cts)) / n_img
    grad_tile = (0.5 * STUDENT_SCALE * (ps_row - pt_row + (ps_col - pt_col))).astype(jnp.bfloat16)
    part_img = jnp.dot(grad_tile, block_s_txt, preferred_element_type=jnp.float32)
    part_txt = lax.dot_general(
        grad_tile, block_s_img, (((0,), (0,)), ((), ())), preferred_element_type=jnp.float32
    )
    return (part_img, part_txt, local_term)


def shards(image_feats, text_feats, teacher_img, teacher_txt, proj_img, proj_txt):
    e_img, inv_img = project(image_feats, proj_img)
    e_txt, inv_txt = project(text_feats, proj_txt)
    q_img = normed(teacher_img)
    q_txt = normed(teacher_txt)
    feats_img, block_q_img = (
        lax.all_gather(image_feats, "txt", axis=0, tiled=True),
        lax.all_gather(q_img, "txt", axis=0, tiled=True),
    )
    feats_txt, block_q_txt = (
        lax.all_gather(text_feats, "img", axis=0, tiled=True),
        lax.all_gather(q_txt, "img", axis=0, tiled=True),
    )
    block_s_img = project(feats_img, proj_img)[0].astype(jnp.bfloat16)
    block_s_txt = project(feats_txt, proj_txt)[0].astype(jnp.bfloat16)
    part_img, part_txt, local_term = tile_terms(block_q_img, block_q_txt, block_s_img, block_s_txt)
    d_img = lax.psum_scatter(part_img, "txt", scatter_dimension=0, tiled=True)
    d_txt = lax.psum_scatter(part_txt, "img", scatter_dimension=0, tiled=True)
    local_img = weight_grad(image_feats, tangent(d_img, e_img, inv_img))
    local_txt = weight_grad(text_feats, tangent(d_txt, e_txt, inv_txt))
    grad_img, grad_txt, total = lax.psum((local_img, local_txt, local_term), ("img", "txt"))
    batch_total = image_feats.shape[0] * lax.axis_size("img") * lax.axis_size("txt")
    loss = total / (2.0 * batch_total)
    return (loss, grad_img, grad_txt)


def solution(mesh):
    return jax.shard_map(
        shards,
        mesh=mesh,
        in_specs=(
            P(("img", "txt"), None),
            P(("txt", "img"), None),
            P(("img", "txt"), None),
            P(("txt", "img"), None),
            P(),
            P(),
        ),
        out_specs=(P(), P(), P()),
        check_vma=False,
    )
```

profile of v0, /device:TPU:1, one launch (start us, length us, event | category | flops | bytes accessed | tf_op | source)
XLA Modules:
  0.0 1573.5 jit_solution(5948633343243834570)
XLA Ops:
  7.2 0.0 copy-start
  7.2 0.0 copy-start.4
  7.2 0.0 all-gather.2.cloned.1.call-start
  7.2 0.9 fusion.7
  8.2 1.5 fusion.8
  9.6 0.0 all-gather.2.cloned.1.call-update
  9.7 0.0 reduce-scatter.5.cloned.1.call-start
  9.7 0.9 fusion.9
  10.6 38.9 %all_gather.15 = bf16[256,512]{1,0:T(8,128)(2,1)S(1)} all-gather(bf16[16,512]{1,0:T(8,128)(2,1)} %param.7), channel_id=1, replica_groups=mesh['img'=16,'txt'=32] {'img'}, dimensions={0}, use_global_device_ids=true | all-gather | bytes 278528 | tf_op jit(solution)/shard_map/all_gather | solution.py:74
  49.5 1.4 multiply_reduce_fusion.3
  50.9 0.0 copy-done.4
  50.9 0.0 copy-start.6
  50.9 153.7 %all_gather.14 = bf16[512,768]{1,0:T(8,128)(2,1)S(1)} all-gather(bf16[16,768]{1,0:T(8,128)(2,1)S(1)} %copy-done.4), channel_id=1, replica_groups=mesh['img'=16,'txt'=32] {'txt'}, dimensions={0}, use_global_device_ids=true | all-gather | bytes 811008 | tf_op jit(solution)/shard_map/all_gather | solution.py:70
  204.6 0.0 copy-done
  204.6 0.6 multiply_reduce_fusion
  205.3 0.0 copy-done.6
  205.3 0.1 fusion.10
  205.3 47.6 %all_gather.13 = bf16[256,1024]{1,0:T(8,128)(2,1)} all-gather(bf16[16,1024]{1,0:T(8,128)(2,1)S(1)} %fusion.10), channel_id=1, replica_groups=mesh['img'=16,'txt'=32] {'img'}, dimensions={0}, use_global_device_ids=true | all-gather | bytes 557056 | tf_op jit(solution)/shard_map/all_gather | solution.py:75
  253.0 0.5 fusion.26
  253.5 0.0 all-gather.2.cloned.1.call-done
  253.5 1.9 fusion.25
  255.4 132.6 %all-reduce.2 = (f32[512]{0:T(512)S(1)}, f32[512]{0:T(512)S(1)}) all-reduce(f32[512]{0:T(512)S(1)} %get-tuple-element.14, f32[512]{0:T(512)S(1)} %get-tuple-element.28), channel_id=1, replica_groups=mesh['img'=16,'txt'=32] {'txt'}, use_global_device_ids=true, to_apply=%region_3.0 | all-reduce | flops 1024 | bytes 8192 | tf_op jit(solution)/shard_map/pmax | solution.py:38
  388.0 0.2 fusion.24
  388.3 58.5 %all-reduce.3 = (f32[256]{0:T(256)S(1)}, f32[256]{0:T(256)S(1)}) all-reduce(f32[256]{0:T(256)S(1)} %get-tuple-element.13, f32[256]{0:T(256)S(1)} %get-tuple-element.9), channel_id=1, replica_groups=mesh['img'=16,'txt'=32] {'img'}, use_global_device_ids=true, to_apply=%region_10.0 | all-reduce | flops 512 | bytes 4096 | tf_op jit(solution)/shard_map/pmax | solution.py:42
  446.8 0.2 fusion.3
  447.1 45.1 %psum.50 = f32[256]{0:T(256)S(1)} all-reduce(f32[256]{0:T(256)S(1)} %get-tuple-element.11), channel_id=1, replica_groups=mesh['img'=16,'txt'=32] {'img'}, use_global_device_ids=true, to_apply=%region_12.0 | all-reduce | flops 256 | bytes 2048 | tf_op jit(solution)/shard_map/psum | solution.py:43
  492.2 134.4 %all-reduce.1 = (f32[512]{0:T(512)S(1)}, f32[512]{0:T(512)S(1)}) all-reduce(f32[512]{0:T(512)S(1)} %get-tuple-element.12, f32[512]{0:T(512)S(1)} %get-tuple-element.10), channel_id=1, replica_groups=mesh['img'=16,'txt'=32] {'txt'}, use_global_device_ids=true, to_apply=%region_5.0 | all-reduce | flops 1024 | bytes 8192 | tf_op jit(solution)/shard_map/psum | solution.py:39
  626.5 1.0 multiply_reduce_fusion.1
  627.5 59.3 %psum.52 = f32[256]{0:T(256)S(1)} all-reduce(f32[256]{0:T(256)S(1)} %get-tuple-element.8), channel_id=1, replica_groups=mesh['img'=16,'txt'=32] {'img'}, use_global_device_ids=true, to_apply=%region_22.0 | all-reduce | flops 256 | bytes 2048 | tf_op jit(solution)/shard_map/psum | solution.py:43
  686.8 0.4 multiply_convert_fusion.1
  687.3 0.0 copy-start.1
  687.3 0.7 copy-done.1
  688.0 1.1 fusion.6
  689.1 0.0 reduce-scatter.5.cloned.1.call-update
  689.1 0.0 copy-start.2
  689.1 0.0 copy-start.5
  689.1 0.0 reduce-scatter.3.cloned.1.call-start
  689.2 2.3 fusion.23
  691.5 0.0 reduce-scatter.3.cloned.1.call-update
  691.6 0.0 all-reduce.6.cloned.1.call-start
  691.6 0.3 multiply_reduce_fusion.7
  691.9 0.0 copy-done.2
  692.0 0.0 copy-done.5
  692.0 0.3 multiply_reduce_fusion.5
  692.3 80.0 %reduce-scatter.5.cloned.1.call-done = f32[16,512]{1,0:T(8,128)} async-done(((f32[256,512]{1,0:T(8,128)}), f32[16,512]{1,0:T(8,128)}) %reduce-scatter.5.cloned.1.call-update) | async-done | bytes 32784 | tf_op jit(solution)/shard_map/reduce_scatter | solution.py:81
  772.2 0.9 multiply_reduce_fusion.4
  773.2 2.4 convolution_bitcast_fusion.1
  775.6 286.6 %reduce-scatter.3.cloned.1.call-done = f32[16,512]{1,0:T(8,128)} async-done(((f32[512,512]{1,0:T(8,128)}), f32[16,512]{1,0:T(8,128)}) %reduce-scatter.3.cloned.1.call-update) | async-done | bytes 32784 | tf_op jit(solution)/shard_map/reduce_scatter | solution.py:80
  1062.2 0.9 multiply_reduce_fusion.6
  1063.1 2.8 convolution_bitcast_fusion
  1065.9 0.0 all-reduce.6.cloned.1.call-update
  1065.9 0.6 subtract_reduce_fusion
  1068.4 0.6 subtract_reduce_fusion.1
  1069.7 122.1 %psum.53 = f32[]{:T(128)} all-reduce(f32[]{:T(128)S(6)} %add.100), channel_id=1, replica_groups=mesh['img'=16,'txt'=32] {'img','txt'}, use_global_device_ids=true, to_apply=%region_24.0 | all-reduce | flops 1 | bytes 8 | tf_op jit(solution)/shard_map/psum | solution.py:84
  1192.4 369.0 %all-reduce.6.cloned.1.call-done = (f32[768,512]{0,1:T(8,128)}, f32[512,512]{0,1:T(8,128)}) async-done(((f32[768,512]{0,1:T(8,128)}, f32[512,512]{0,1:T(8,128)}), (f32[768,512]{0,1:T(8,128)}, f32[512,512]{0,1:T(8,128)})) %all-reduce.6.cloned.1.call-update) | async-done | bytes 2621456 | tf_op jit(solution)/shard_map/psum | solution.py:84
  1561.4 0.0 copy-start.3
  1561.4 3.1 copy.9
  1564.5 0.0 copy-done.3
  1564.5 1.3 copy.10
  (6 shorter events, 0.0 us)
Async XLA Ops:
  7.2 197.4 %copy-start = (bf16[768,512]{1,0:T(8,128)(2,1)S(1)}, bf16[768,512]{1,0:T(8,128)(2,1)}, u32[]{:S(2)}) copy-start(bf16[768,512]{1,0:T(8,128)(2,1)} %param.10) | copy-start | bytes 2359300
  7.2 43.7 %copy-start.4 = (bf16[16,768]{1,0:T(8,128)(2,1)S(1)}, bf16[16,768]{1,0:T(8,128)(2,1)}, u32[]{:S(2)}) copy-start(bf16[16,768]{1,0:T(8,128)(2,1)} %param.6) | copy-start | bytes 73732
  7.2 246.3 %all-gather.2.cloned.1.call-start = ((), (), s32[]{:S(2)}) async-start(), calls=%async_computation.2 | async-start | bytes 1081344 | tf_op jit(solution)/shard_map/all_gather | solution.py:71
  9.7 762.6 %reduce-scatter.5.cloned.1.call-start = ((), (), s32[]{:S(2)}) async-start(), calls=%async_computation.4 | async-start | bytes 557056 | tf_op jit(solution)/shard_map/reduce_scatter | solution.py:81
  50.9 154.3 %copy-start.6 = (bf16[16,1024]{1,0:T(8,128)(2,1)S(1)}, bf16[16,1024]{1,0:T(8,128)(2,1)}, u32[]{:S(2)}) copy-start(bf16[16,1024]{1,0:T(8,128)(2,1)} %param.9) | copy-start | bytes 98308
  687.3 0.7 copy-start.1
  689.1 2.8 copy-start.2
  689.1 2.8 copy-start.5
  689.1 373.0 %reduce-scatter.3.cloned.1.call-start = ((), (), s32[]{:S(2)}) async-start(), calls=%async_computation.3 | async-start | bytes 1081344 | tf_op jit(solution)/shard_map/reduce_scatter | solution.py:80
  691.6 869.9 %all-reduce.6.cloned.1.call-start = ((), (), s32[]{:S(2)}) async-start(), calls=%async_computation.5 | async-start | bytes 5242880 | tf_op jit(solution)/shard_map/psum | solution.py:84
  1561.4 3.1 copy-start.3
Sparse Core Ops, SparseCore 0:
  12.9 116.0 all-gather.1
  689.2 82.9 reduce-scatter.4
  775.8 286.2 reduce-scatter.2
  1068.0 493.3 all-reduce.5
where the time goes:
time: 1580 us; the launch traced here: 1570 us
  blocking collectives  792 us (50%)
  waiting for transfers between devices  736 us (47%)
  between operations  18.2 us (1%)
    psum x1, waiting for transfers between devices, shards(): lax.psum((local_img, local_txt, local_term), ('img', 'txt'))  369 us
    reduce_scatter x1, waiting for transfers between devices, shards(): d_img = lax.psum_scatter(part_img, 'txt', scatter_dimension=0, tiled=True)  287 us
    all_gather x1, blocking collectives, shards(): lax.all_gather(image_feats, 'txt', axis=0, tiled=True)  154 us
    psum x1, blocking collectives, tile_terms(): lax.psum((jnp.sum(jnp.exp(tl - rtm[:, None]), 1), jnp.sum(jnp.exp(sl - rs...  134 us
    pmax x1, blocking collectives, tile_terms(): rtm, rsm = lax.pmax((tl.max(1), sl.max(1)), 'txt')  133 us
    psum x1, blocking collectives, shards(): lax.psum((local_img, local_txt, local_term), ('img', 'txt'))  122 us
    psum x2, blocking collectives, tile_terms(): lax.psum((jnp.sum(jnp.exp(tl - ctm[None, :]), 0), jnp.sum(jnp.exp(sl - cs...  104 us
    reduce_scatter x1, waiting for transfers between devices, shards(): d_txt = lax.psum_scatter(part_txt, 'img', scatter_dimension=0, tiled=True)  80 us
  transfers between devices with their start and end apart: 4, of which 3 were waited for; matrix products, arithmetic and copies ran while one was open for 1% of the time, Pallas kernels for 0%

commit v1 on v0

v1 whole, which is shorter than its diff:
```python
import jax
import jax.numpy as jnp
from jax import lax
from jax.sharding import Mesh
from jax.sharding import PartitionSpec as P

EPS = 1e-06
TEACHER_SCALE = 100.0
STUDENT_SCALE = 50.0

AXES = ("zl", "core", "y", "zh", "x")
SIZES = (8, 2, 4, 2, 4)
PLANE = ("y", "x")
RING = ("zh", "zl")
TILE = ("core", "y", "x")

BF16 = jnp.bfloat16
F32 = jnp.float32


def project(feats, weight):
    u = jnp.dot(feats, weight, preferred_element_type=F32)
    inv = lax.rsqrt(jnp.sum(u * u, axis=1, keepdims=True) + EPS)
    return (u * inv, inv)


def normed(raw):
    x = raw.astype(F32)
    return (x * lax.rsqrt(jnp.sum(x * x, axis=1, keepdims=True) + EPS)).astype(BF16)


def tangent(grad_rows, embeds, inverse):
    return (grad_rows - embeds * jnp.sum(embeds * grad_rows, 1, keepdims=True)) * inverse


def spread(block, axes):
    count = lax.axis_size(axes)
    copies = jnp.broadcast_to(block[None], (count,) + block.shape)
    return lax.all_to_all(copies, axes, 0, 0, tiled=True)


def swap_cores(block):
    return lax.ppermute(block, "core", [(0, 1), (1, 0)])


def thirds(value):
    hi = value.astype(BF16)
    rest = value - hi.astype(F32)
    mid = rest.astype(BF16)
    low = (rest - mid.astype(F32)).astype(BF16)
    return jnp.stack([hi, mid, low])


def with_loss(rows, value):
    extra = jnp.zeros((8, rows.shape[1]), BF16)
    extra = extra.at[0, :3].set(thirds(value))
    return jnp.concatenate([rows.astype(BF16), extra], 0)


def merge(stats):
    top = jnp.max(stats[:, 0], 0)
    teacher = jnp.sum(stats[:, 1] * jnp.exp(stats[:, 0] - top[None]), 0)
    student = jnp.sum(stats[:, 2], 0)
    return (top, teacher, student)


def shards(image_feats, text_feats, teacher_img, teacher_txt, proj_img, proj_txt):
    core = lax.axis_index("core")
    dt = teacher_img.shape[1]
    pack_img = jnp.concatenate([normed(teacher_img), image_feats], 1)
    pack_txt = jnp.concatenate([normed(teacher_txt), text_feats], 1)
    half_img = spread(pack_img, PLANE)
    half_img = half_img.reshape(-1, pack_img.shape[1])
    half_img, pack_txt = lax.optimization_barrier((half_img, pack_txt))
    other_img = swap_cores(half_img)
    block_txt = lax.all_gather(pack_txt, RING, axis=0, tiled=True)
    block_img = jnp.concatenate([half_img, other_img], 0)
    q_img, feats_img = (block_img[:, :dt], block_img[:, dt:])
    q_txt, feats_txt = (block_txt[:, :dt], block_txt[:, dt:])
    e_img, inv_img = project(feats_img, proj_img)
    e_txt, inv_txt = project(feats_txt, proj_txt)
    s_img = e_img.astype(BF16)
    s_txt = e_txt.astype(BF16)
    rows, cols = (q_img.shape[0], q_txt.shape[0])

    tl = TEACHER_SCALE * jnp.dot(q_img, q_txt.T, preferred_element_type=F32)
    sl = STUDENT_SCALE * jnp.dot(s_img, s_txt.T, preferred_element_type=F32)
    rm = tl.max(1)
    cm = tl.max(0)
    er = jnp.exp(tl - rm[:, None])
    ec = jnp.exp(tl - cm[None, :])
    es = jnp.exp(sl)
    row_stats = jnp.stack([rm, er.sum(1), es.sum(1)]).reshape(3, 2, -1)
    col_stats = jnp.stack([cm, ec.sum(0), es.sum(0)])
    row_stats = jnp.where(core == 0, row_stats, row_stats[:, ::-1])
    row_all = spread(row_stats.reshape(-1, 128), TILE).reshape(-1, 3, rows)
    row_all, col_stats = lax.optimization_barrier((row_all, col_stats))
    col_all = spread(col_stats.reshape(-1, 128), RING).reshape(-1, 3, cols)
    row_top, row_t, row_s = merge(row_all)
    col_top, col_t, col_s = merge(col_all)
    row_lse = jnp.sum(jnp.log(row_s) - row_top - jnp.log(row_t))
    col_lse = jnp.sum(jnp.log(col_s) - col_top - jnp.log(col_t))
    mine = jnp.stack([row_top, 1.0 / row_t, 1.0 / row_s]).reshape(3, 2, -1)
    mine = jnp.where(core == 0, mine, mine[:, ::-1]).reshape(3, rows)
    row_gain = jnp.exp(rm - mine[0]) * mine[1]
    col_gain = jnp.exp(cm - col_top) / col_t
    pt = er * row_gain[:, None] + ec * col_gain[None, :]
    ps = es * mine[2][:, None] + es * (1.0 / col_s)[None, :]
    total = jnp.sum(pt * (tl - sl))
    total = total + row_lse / lax.axis_size(TILE) + col_lse / lax.axis_size(RING)
    g = (0.5 * STUDENT_SCALE * (ps - pt)).astype(BF16)
    d_img = jnp.dot(g, s_txt, preferred_element_type=F32)
    d_txt = lax.dot_general(g, s_img, (((0,), (0,)), ((), ())), preferred_element_type=F32)
    du_img = tangent(d_img, e_img, inv_img).astype(BF16)
    du_txt = tangent(d_txt, e_txt, inv_txt).astype(BF16)
    rows_first = (((0,), (0,)), ((), ()))
    w_img = lax.dot_general(feats_img, du_img, rows_first, preferred_element_type=F32)
    w_txt = lax.dot_general(feats_txt, du_txt, rows_first, preferred_element_type=F32)
    part = jnp.concatenate([w_img.astype(BF16), w_txt.astype(BF16)], 0)

    width = part.shape[1]
    part = part.reshape(2, -1, width)
    part = lax.all_to_all(part, "core", 0, 0, tiled=True).astype(F32).sum(0).astype(BF16)
    part = part.reshape(lax.axis_size(PLANE), -1, width)
    part = lax.all_to_all(part, PLANE, 0, 0, tiled=True).astype(F32).sum(0)
    chunk = part.shape[0]
    part = lax.all_gather(with_loss(part, total), RING).astype(F32)
    chunk_sum = part[:, :chunk].sum(0)
    ring_loss = part[:, chunk, :3].sum()
    full = spread(with_loss(chunk_sum, ring_loss), PLANE)
    full = spread(full, "core").astype(F32)
    full = full.reshape(-1, chunk + 8, width)
    grads = full[:, :chunk].reshape(-1, width)
    batch_total = image_feats.shape[0] * lax.axis_size(AXES)
    loss = full[:, chunk, :3].sum() / (2.0 * batch_total)
    split = image_feats.shape[1]
    return (loss, grads[:split], grads[split:])


def solution(mesh):
    fine = Mesh(mesh.devices.reshape(SIZES), AXES)
    img = P(("zl", "core", "y", "zh", "x"), None)
    txt = P(("y", "zh", "x", "zl", "core"), None)
    return jax.shard_map(
        shards,
        mesh=fine,
        in_specs=(img, txt, img, txt, P(), P()),
        out_specs=(P(), P(), P()),
        check_vma=False,
    )
```

time: 1580 us -> 203 us (0.13)
  blocking collectives: 792 us -> 93.3 us
  waiting for transfers between devices: 736 us -> 40.4 us
  starting transfers between devices: 0.16 us -> 34.4 us
    psum x1 -> x0, waiting for transfers between devices: 369 us -> none  [shards(): lax.psum((local_img, local_txt, local_term), ('img', 'txt'))]
    reduce_scatter x2 -> x0, waiting for transfers between devices: 367 us -> none  [the longest x1 287 us: shards(): d_img = lax.psum_scatter(part_img, 'txt', scatter_dimension=0, tiled=True)]
    psum x4 -> x0, blocking collectives: 361 us -> none  [the longest x1 134 us: tile_terms(): lax.psum((jnp.sum(jnp.exp(tl - rtm[:, None]), 1), jnp.sum(jnp.exp(sl - rs...]
    pmax x2 -> x0, blocking collectives: 191 us -> none  [the longest x1 133 us: tile_terms(): rtm, rsm = lax.pmax((tl.max(1), sl.max(1)), 'txt')]
    all_gather x3 -> x2, blocking collectives: 240 us -> 58.9 us  [the longest x1 33.5 us: shards(): block_txt = lax.all_gather(pack_txt, RING, axis=0, tiled=True)]
    all_to_all x0 -> x4, waiting for transfers between devices: none -> 40.4 us  [the longest x3 30 us: spread(): return lax.all_to_all(copies, axes, 0, 0, tiled=True)]
    all_to_all x0 -> x3, blocking collectives: none -> 34.5 us  [the longest x2 27.4 us: spread(): return lax.all_to_all(copies, axes, 0, 0, tiled=True)]
    all_to_all x0 -> x4, starting transfers between devices: none -> 28.5 us  [the longest x3 24.9 us: spread(): return lax.all_to_all(copies, axes, 0, 0, tiled=True)]
  transfers between devices with their start and end apart: 4 -> 5, of which waited for: 3 -> 4; matrix products, arithmetic and copies ran while one was open for 1% -> 2% of each run, Pallas kernels for 0% -> 0%
where the time goes in v1:
time: 203 us; the launch traced here: 202 us
  blocking collectives  93.3 us (46%)
  waiting for transfers between devices  40.4 us (20%)
  starting transfers between devices  34.4 us (17%)
  other arithmetic  13.3 us (7%)
  local copies, waits for them, and re-layouts  7.53 us (4%)
  matrix products  6.69 us (3%)
  between operations  5.99 us (3%)
    all_gather x1, blocking collectives, shards(): block_txt = lax.all_gather(pack_txt, RING, axis=0, tiled=True)  33.5 us
    all_to_all x3, waiting for transfers between devices, spread(): return lax.all_to_all(copies, axes, 0, 0, tiled=True)  30 us
    all_to_all x2, blocking collectives, spread(): return lax.all_to_all(copies, axes, 0, 0, tiled=True)  27.4 us
    all_gather x1, blocking collectives, shards(): part = lax.all_gather(with_loss(part, total), RING).astype(F32)  25.4 us
    all_to_all x3, starting transfers between devices, spread(): return lax.all_to_all(copies, axes, 0, 0, tiled=True)  24.9 us
    all_to_all x1, waiting for transfers between devices, shards(): part = lax.all_to_all(part, PLANE, 0, 0, tiled=True).astype(F32).sum(0)  10.4 us
    all_to_all x1, blocking collectives, shards(): lax.all_to_all(part, 'core', 0, 0, tiled=True).astype(F32).sum(0)  7.09 us
    ppermute x1, starting transfers between devices, swap_cores(): return lax.ppermute(block, 'core', [(0, 1), (1, 0)])  5.89 us
  transfers between devices with their start and end apart: 5, of which 4 were waited for; matrix products, arithmetic and copies ran while one was open for 2% of the time, Pallas kernels for 0%

profile of v1, /device:TPU:1, one launch (start us, length us, event | category | flops | bytes accessed | tf_op | source)
XLA Modules:
  0.0 201.6 jit_solution(11152624953938027717)
XLA Ops:
  0.6 0.0 copy-start
  0.6 0.0 copy-start.3
  0.7 0.9 fusion.19
  1.6 0.8 fusion.20
  2.5 0.7 pad_maximum_fusion.1
  3.2 1.0 broadcast_in_dim.14
  4.2 7.6 %all-to-all-start = ((bf16[16,16,1792]{2,1,0:T(8,128)(2,1)}), bf16[16,16,1792]{2,1,0:T(8,128)(2,1)S(1)}, u32[]{:S(2)}, u32[]{:S(2)}) async-start(bf16[16,16,1792]{2,1,0:T(8,128)(2,1)} %broadcast_in_dim.14), calls=%async_computation | async-start | bytes 1835008 | tf_op jit(solution)/shard_map/all_to_all | solution.py:39
  11.8 0.0 copy-done.3
  11.8 0.1 fusion.21
  11.9 0.1 fusion.22
  12.0 12.7 %all-to-all-done = bf16[16,16,1792]{2,1,0:T(8,128)(2,1)S(1)} async-done(((bf16[16,16,1792]{2,1,0:T(8,128)(2,1)}), bf16[16,16,1792]{2,1,0:T(8,128)(2,1)S(1)}, u32[]{:S(2)}, u32[]{:S(2)}) %all-to-all-start) | async-done | bytes 917536 | tf_op jit(solution)/shard_map/all_to_all | solution.py:39
  24.8 5.9 %collective-permute-start = (bf16[256,1792]{1,0:T(8,128)(2,1)S(1)}, bf16[256,1792]{1,0:T(8,128)(2,1)S(1)}, u32[]{:S(2)}, u32[]{:S(2)}) collective-permute-start(bf16[256,1792]{1,0:T(8,128)(2,1)S(1)} %bitcast.60), channel_id=1, source_target_pairs={{0,32},{32,0},{1,33},{33,1},{2,34},{34,2},{3,35},{35,3},{4,36},{36... | collective-permute-start | bytes 2752520 | tf_op jit(solution)/shard_map/ppermute | solution.py:43
  30.6 33.5 %all_gather.9 = bf16[256,1536]{1,0:T(8,128)(2,1)S(1)} all-gather(bf16[16,1536]{1,0:T(8,128)(2,1)S(1)} %pad_maximum_fusion.2), channel_id=1, replica_groups=mesh['zl'=8,'core'=2,'y'=4,'zh'=2,'x'=4] {'zh','zl'}, dimensions={0}, use_global_device_ids=true | all-gather | bytes 835584 | tf_op jit(solution)/shard_map/all_gather | solution.py:76
  64.1 0.4 multiply_reduce_fusion.4
  64.5 0.1 constant_dynamic-update-slice_fusion.1
  64.6 0.0 collective-permute-done
  64.6 0.1 constant_dynamic-update-slice_fusion
  64.7 1.4 fusion.32
  66.1 0.6 multiply_reduce_fusion.1
  66.7 0.0 copy-done.1
  66.8 1.3 fusion.10
  68.1 1.2 exponential_reduce_fusion
  69.3 0.1 rev.6
  69.4 0.7 broadcast_in_dim.16
  70.2 10.8 %all-to-all-start.1 = ((f32[32,12,128]{2,1,0:T(8,128)}), f32[32,12,128]{2,1,0:T(8,128)}, u32[]{:S(2)}, u32[]{:S(2)}) async-start(f32[32,12,128]{2,1,0:T(8,128)} %broadcast_in_dim.16), calls=%async_computation.1 | async-start | bytes 524288 | tf_op jit(solution)/shard_map/all_to_all | solution.py:39
  81.0 8.3 %all-to-all-done.1 = f32[32,12,128]{2,1,0:T(8,128)} async-done(((f32[32,12,128]{2,1,0:T(8,128)}), f32[32,12,128]{2,1,0:T(8,128)}, u32[]{:S(2)}, u32[]{:S(2)}) %all-to-all-start.1) | async-done | bytes 196640 | tf_op jit(solution)/shard_map/all_to_all | solution.py:39
  89.3 1.0 reshape.193
  90.3 0.7 copy.13
  91.1 0.1 slice_reduce_fusion.1
  91.2 0.6 broadcast_in_dim.18
  91.8 6.5 %all-to-all-start.2 = ((f32[16,6,128]{2,1,0:T(8,128)}), f32[16,6,128]{2,1,0:T(8,128)S(1)}, u32[]{:S(2)}, u32[]{:S(2)}) async-start(f32[16,6,128]{2,1,0:T(8,128)} %broadcast_in_dim.18), calls=%async_computation.2 | async-start | bytes 131072 | tf_op jit(solution)/shard_map/all_to_all | solution.py:39
  98.4 0.9 slice_reduce_fusion.2
  99.2 0.9 fusion.23
  100.1 0.6 subtract_reduce_fusion
  100.8 0.1 rev.7
  101.0 9.0 %all-to-all-done.2 = f32[16,6,128]{2,1,0:T(8,128)S(1)} async-done(((f32[16,6,128]{2,1,0:T(8,128)}), f32[16,6,128]{2,1,0:T(8,128)S(1)}, u32[]{:S(2)}, u32[]{:S(2)}) %all-to-all-start.2) | async-done | bytes 49184 | tf_op jit(solution)/shard_map/all_to_all | solution.py:39
  110.0 0.1 slice_reduce_fusion.4
  110.1 0.6 subtract_reduce_fusion.1
  110.7 2.3 %fusion.6 = (bf16[512,256]{1,0:T(8,128)(2,1)S(1)}, f32[]{:T(128)}) fusion(f32[512,256]{1,0:T(8,128)} %get-tuple-element.62, f32[512,256]{1,0:T(8,128)} %get-tuple-element.63, f32[256]{0:T(256)S(1)} %get-tuple-element.53, f32[512]{0:T(512)S(1)} %exponential_multiply_fusion, f32[256]{0:T(256)S(1)} %get-tuple-element.57, f32[512]{0:T(512)S(1)} %bitcast.64, ...), kind=kLoop, calls=%fused_computation.18 | loop fusion | flops 1703935 | bytes 1319940 | tf_op jit(solution)/shard_map/convert_element_type | solution.py:111
  113.0 0.4 multiply_reduce_fusion.3
  113.4 0.4 multiply_reduce_fusion
  113.9 0.4 convolution_convert_fusion.1
  114.3 1.8 convolution_convert_fusion
  116.1 0.1 pad_maximum_fusion
  116.2 7.1 %all_to_all.35 = bf16[2,640,512]{2,1,0:T(8,128)(2,1)S(1)} all-to-all(bf16[2,640,512]{2,1,0:T(8,128)(2,1)S(1)} %bitcast.59), channel_id=1, replica_groups=mesh['zl'=8,'core'=2,'y'=4,'zh'=2,'x'=4] {'core'}, dimensions={0} | all-to-all | bytes 2621440 | tf_op jit(solution)/shard_map/all_to_all | solution.py:123
  123.3 1.2 reduce_sum.218
  124.5 3.6 %all-to-all-start.4 = ((bf16[16,40,512]{2,1,0:T(8,128)(2,1)}), bf16[16,40,512]{2,1,0:T(8,128)(2,1)S(1)}, u32[]{:S(2)}, u32[]{:S(2)}) async-start(bf16[16,40,512]{2,1,0:T(8,128)(2,1)} %bitcast.7), calls=%async_computation.4 | async-start | bytes 1310720 | tf_op jit(solution)/shard_map/all_to_all | solution.py:125
  130.1 0.1 maximum_bitcast_fusion
  130.1 10.4 %all-to-all-done.4 = bf16[16,40,512]{2,1,0:T(8,128)(2,1)S(1)} async-done(((bf16[16,40,512]{2,1,0:T(8,128)(2,1)}), bf16[16,40,512]{2,1,0:T(8,128)(2,1)S(1)}, u32[]{:S(2)}, u32[]{:S(2)}) %all-to-all-start.4) | async-done | bytes 655392 | tf_op jit(solution)/shard_map/all_to_all | solution.py:125
  140.5 0.1 reduce_sum.219
  140.6 25.4 %all-gather = bf16[768,512]{1,0:T(8,128)(2,1)S(1)} all-gather(bf16[48,512]{1,0:T(8,128)(2,1)S(1)} %fusion.25), channel_id=2, replica_groups=mesh['zl'=8,'core'=2,'y'=4,'zh'=2,'x'=4] {'zh','zl'}, dimensions={0}, use_global_device_ids=true | all-gather | bytes 835584 | tf_op jit(solution)/shard_map/all_gather | solution.py:127
  166.0 0.2 convert.3
  166.2 0.6 slice_reduce_fusion.5
  166.8 0.1 slice_reduce_fusion
  168.2 0.1 maximum_bitcast_fusion.1
  168.3 0.1 broadcast_in_dim.19
  168.4 13.4 %all_to_all.36 = bf16[16,48,512]{2,1,0:T(8,128)(2,1)S(1)} all-to-all(bf16[16,48,512]{2,1,0:T(8,128)(2,1)S(1)} %broadcast_in_dim.19), channel_id=1, replica_groups=mesh['zl'=8,'core'=2,'y'=4,'zh'=2,'x'=4] {'y','x'}, dimensions={0} | all-to-all | bytes 1572864 | tf_op jit(solution)/shard_map/all_to_all | solution.py:39
  181.8 0.2 broadcast_in_dim.20
  182.0 13.9 %all_to_all.37 = bf16[2,16,48,512]{3,2,1,0:T(8,128)(2,1)S(1)} all-to-all(bf16[2,16,48,512]{3,2,1,0:T(8,128)(2,1)S(1)} %broadcast_in_dim.20), channel_id=1, replica_groups=mesh['zl'=8,'core'=2,'y'=4,'zh'=2,'x'=4] {'core'}, dimensions={0} | all-to-all | bytes 3145728 | tf_op jit(solution)/shard_map/all_to_all | solution.py:39
  195.9 0.5 bitcast_convert_fusion
  196.5 0.6 slice_reduce_fusion.3
  197.1 0.3 slice.127
  197.5 1.3 slice.128
  198.7 1.0 slice.129
  (37 shorter events, 0.3 us)
Async XLA Ops:
  0.6 65.5 %copy-start = (bf16[768,512]{1,0:T(8,128)(2,1)S(1)}, bf16[768,512]{1,0:T(8,128)(2,1)}, u32[]{:S(2)}) copy-start(bf16[768,512]{1,0:T(8,128)(2,1)} %param.14) | copy-start | bytes 2359300
  0.6 11.1 %copy-start.3 = (bf16[16,1024]{1,0:T(8,128)(2,1)S(1)}, bf16[16,1024]{1,0:T(8,128)(2,1)}, u32[]{:S(2)}) copy-start(bf16[16,1024]{1,0:T(8,128)(2,1)} %param.13) | copy-start | bytes 98308
  0.7 11.4 %copy-start.4 = (bf16[16,512]{1,0:T(8,128)(2,1)S(1)}, bf16[16,512]{1,0:T(8,128)(2,1)}, u32[]{:S(2)}) copy-start(bf16[16,512]{1,0:T(8,128)(2,1)} %param.11) | copy-start | bytes 49156
  3.2 60.9 %copy-start.2 = (bf16[512,512]{1,0:T(8,128)(2,1)S(1)}, bf16[512,512]{1,0:T(8,128)(2,1)}, u32[]{:S(2)}) copy-start(bf16[512,512]{1,0:T(8,128)(2,1)} %param.15) | copy-start | bytes 1572868
  4.2 20.6 %all-to-all-start = ((bf16[16,16,1792]{2,1,0:T(8,128)(2,1)}), bf16[16,16,1792]{2,1,0:T(8,128)(2,1)S(1)}, u32[]{:S(2)}, u32[]{:S(2)}) async-start(bf16[16,16,1792]{2,1,0:T(8,128)(2,1)} %broadcast_in_dim.14), calls=%async_computation | async-start | bytes 1835008 | tf_op jit(solution)/shard_map/all_to_all | solution.py:39
  24.8 39.9 %collective-permute-start = (bf16[256,1792]{1,0:T(8,128)(2,1)S(1)}, bf16[256,1792]{1,0:T(8,128)(2,1)S(1)}, u32[]{:S(2)}, u32[]{:S(2)}) collective-permute-start(bf16[256,1792]{1,0:T(8,128)(2,1)S(1)} %bitcast.60), channel_id=1, source_target_pairs={{0,32},{32,0},{1,33},{33,1},{2,34},{34,2},{3,35},{35,3},{4,36},{36... | collective-permute-start | bytes 2752520 | tf_op jit(solution)/shard_map/ppermute | solution.py:43
  64.7 2.0 %copy-start.1 = (bf16[512,1792]{1,0:T(8,128)(2,1)}, bf16[512,1792]{1,0:T(8,128)(2,1)S(1)}, u32[]{:S(2)}) copy-start(bf16[512,1792]{1,0:T(8,128)(2,1)S(1)} %constant_dynamic-update-slice_fusion) | copy-start | bytes 5505028
  70.2 19.1 %all-to-all-start.1 = ((f32[32,12,128]{2,1,0:T(8,128)}), f32[32,12,128]{2,1,0:T(8,128)}, u32[]{:S(2)}, u32[]{:S(2)}) async-start(f32[32,12,128]{2,1,0:T(8,128)} %broadcast_in_dim.16), calls=%async_computation.1 | async-start | bytes 524288 | tf_op jit(solution)/shard_map/all_to_all | solution.py:39
  91.8 18.1 %all-to-all-start.2 = ((f32[16,6,128]{2,1,0:T(8,128)}), f32[16,6,128]{2,1,0:T(8,128)S(1)}, u32[]{:S(2)}, u32[]{:S(2)}) async-start(f32[16,6,128]{2,1,0:T(8,128)} %broadcast_in_dim.18), calls=%async_computation.2 | async-start | bytes 131072 | tf_op jit(solution)/shard_map/all_to_all | solution.py:39
  124.5 16.0 %all-to-all-start.4 = ((bf16[16,40,512]{2,1,0:T(8,128)(2,1)}), bf16[16,40,512]{2,1,0:T(8,128)(2,1)S(1)}, u32[]{:S(2)}, u32[]{:S(2)}) async-start(bf16[16,40,512]{2,1,0:T(8,128)(2,1)} %bitcast.7), calls=%async_computation.4 | async-start | bytes 1310720 | tf_op jit(solution)/shard_map/all_to_all | solution.py:125

commit v2 on v1

--- a/solution.py
+++ b/solution.py
@@ -71,7 +71,6 @@
     pack_txt = jnp.concatenate([normed(teacher_txt), text_feats], 1)
     half_img = spread(pack_img, PLANE)
     half_img = half_img.reshape(-1, pack_img.shape[1])
-    half_img, pack_txt = lax.optimization_barrier((half_img, pack_txt))
     other_img = swap_cores(half_img)
     block_txt = lax.all_gather(pack_txt, RING, axis=0, tiled=True)
     block_img = jnp.concatenate([half_img, other_img], 0)
@@ -94,7 +93,6 @@
     col_stats = jnp.stack([cm, ec.sum(0), es.sum(0)])
     row_stats = jnp.where(core == 0, row_stats, row_stats[:, ::-1])
     row_all = spread(row_stats.reshape(-1, 128), TILE).reshape(-1, 3, rows)
-    row_all, col_stats = lax.optimization_barrier((row_all, col_stats))
     col_all = spread(col_stats.reshape(-1, 128), RING).reshape(-1, 3, cols)
     row_top, row_t, row_s = merge(row_all)
     col_top, col_t, col_s = merge(col_all)
@@ -116,25 +114,29 @@
     rows_first = (((0,), (0,)), ((), ()))
     w_img = lax.dot_general(feats_img, du_img, rows_first, preferred_element_type=F32)
     w_txt = lax.dot_general(feats_txt, du_txt, rows_first, preferred_element_type=F32)
-    part = jnp.concatenate([w_img.astype(BF16), w_txt.astype(BF16)], 0)
 
-    width = part.shape[1]
-    part = part.reshape(2, -1, width)
+    width = w_img.shape[1]
+    peers = lax.axis_size(PLANE)
+    w_img = w_img.astype(BF16).reshape(2, peers, -1, width)
+    w_txt = w_txt.astype(BF16).reshape(2, peers, -1, width)
+    cut = w_img.shape[2]
+    part = jnp.concatenate([w_img, w_txt], 2)
+    chunk = part.shape[2]
     part = lax.all_to_all(part, "core", 0, 0, tiled=True).astype(F32).sum(0).astype(BF16)
-    part = part.reshape(lax.axis_size(PLANE), -1, width)
     part = lax.all_to_all(part, PLANE, 0, 0, tiled=True).astype(F32).sum(0)
-    chunk = part.shape[0]
     part = lax.all_gather(with_loss(part, total), RING).astype(F32)
     chunk_sum = part[:, :chunk].sum(0)
     ring_loss = part[:, chunk, :3].sum()
-    full = spread(with_loss(chunk_sum, ring_loss), PLANE)
-    full = spread(full, "core").astype(F32)
-    full = full.reshape(-1, chunk + 8, width)
-    grads = full[:, :chunk].reshape(-1, width)
+    own = spread(with_loss(chunk_sum, ring_loss), PLANE)
+    other = swap_cores(own)
+    first = jnp.where(core == 0, own, other)
+    second = jnp.where(core == 0, other, own)
+    full = jnp.stack([first, second]).astype(F32)
+    grad_img = full[:, :, :cut].reshape(-1, width)
+    grad_txt = full[:, :, cut:chunk].reshape(-1, width)
     batch_total = image_feats.shape[0] * lax.axis_size(AXES)
-    loss = full[:, chunk, :3].sum() / (2.0 * batch_total)
-    split = image_feats.shape[1]
-    return (loss, grads[:split], grads[split:])
+    loss = full[:, :, chunk, :3].sum() / (2.0 * batch_total)
+    return (loss, grad_img, grad_txt)
 
 
 def solution(mesh):

time: 203 us -> 203 us (level)
  blocking collectives: 93.3 us -> 77.9 us
  starting transfers between devices: 34.4 us -> 46.3 us
  matrix products: 6.69 us -> 8.83 us
    all_to_all x2 -> x1, blocking collectives: 27.4 us -> 13.5 us  [spread(): return lax.all_to_all(copies, axes, 0, 0, tiled=True)]
    ppermute x1 -> x2, starting transfers between devices: 5.89 us -> 17 us  [swap_cores(): return lax.ppermute(block, 'core', [(0, 1), (1, 0)])]
    dot_general x2, matrix products: 1.01 us -> 3.34 us  [project(): u = jnp.dot(feats, weight, preferred_element_type=F32)]
    reduce_sum x2, other arithmetic: 0.19 us -> 2.41 us  [merge(): student = jnp.sum(stats[:, 2], 0)]
  transfers between devices with their start and end apart: 5 -> 6, of which waited for: 4 -> 5; matrix products, arithmetic and copies ran while one was open for 2% -> 3% of each run, Pallas kernels for 0% -> 0%
where the time goes in v2:
time: 203 us; the launch traced here: 202 us
  blocking collectives  77.9 us (38%)
  starting transfers between devices  46.3 us (23%)
  waiting for transfers between devices  41.2 us (20%)
  other arithmetic  15.2 us (7%)
  matrix products  8.83 us (4%)
  local copies, waits for them, and re-layouts  6.39 us (3%)
  between operations  5.96 us (3%)
    all_gather x1, blocking collectives, shards(): block_txt = lax.all_gather(pack_txt, RING, axis=0, tiled=True)  33.5 us
    all_to_all x3, waiting for transfers between devices, spread(): return lax.all_to_all(copies, axes, 0, 0, tiled=True)  29 us
    all_to_all x3, starting transfers between devices, spread(): return lax.all_to_all(copies, axes, 0, 0, tiled=True)  25.7 us
    all_gather x1, blocking collectives, shards(): part = lax.all_gather(with_loss(part, total), RING).astype(F32)  25.4 us
    ppermute x2, starting transfers between devices, swap_cores(): return lax.ppermute(block, 'core', [(0, 1), (1, 0)])  17 us
    all_to_all x1, blocking collectives, spread(): return lax.all_to_all(copies, axes, 0, 0, tiled=True)  13.5 us
    all_to_all x1, waiting for transfers between devices, shards(): part = lax.all_to_all(part, PLANE, 0, 0, tiled=True).astype(F32).sum(0)  10.4 us
    all_to_all x1, blocking collectives, shards(): lax.all_to_all(part, 'core', 0, 0, tiled=True).astype(F32).sum(0)  5.54 us
  transfers between devices with their start and end apart: 6, of which 5 were waited for; matrix products, arithmetic and copies ran while one was open for 3% of the time, Pallas kernels for 0%

profile of v2, /device:TPU:1, one launch (start us, length us, event | category | flops | bytes accessed | tf_op | source)
XLA Modules:
  0.0 201.8 jit_solution(18391404794383063524)
XLA Ops:
  0.6 0.0 copy-start
  0.6 0.0 copy-start.5
  0.7 0.0 copy-start.6
  0.7 0.9 fusion.16
  1.6 0.8 fusion.17
  2.5 0.7 pad_maximum_fusion.4
  3.2 1.0 broadcast_in_dim.12
  4.2 7.6 %all-to-all-start = ((bf16[16,16,1792]{2,1,0:T(8,128)(2,1)}), bf16[16,16,1792]{2,1,0:T(8,128)(2,1)S(1)}, u32[]{:S(2)}, u32[]{:S(2)}) async-start(bf16[16,16,1792]{2,1,0:T(8,128)(2,1)} %broadcast_in_dim.12), calls=%async_computation | async-start | bytes 1835008 | tf_op jit(solution)/shard_map/all_to_all | solution.py:39
  11.8 0.1 fusion.18
  11.9 0.1 fusion.19
  12.0 12.8 %all-to-all-done = bf16[16,16,1792]{2,1,0:T(8,128)(2,1)S(1)} async-done(((bf16[16,16,1792]{2,1,0:T(8,128)(2,1)}), bf16[16,16,1792]{2,1,0:T(8,128)(2,1)S(1)}, u32[]{:S(2)}, u32[]{:S(2)}) %all-to-all-start) | async-done | bytes 917536 | tf_op jit(solution)/shard_map/all_to_all | solution.py:39
  24.7 5.9 %collective-permute-start = (bf16[256,1792]{1,0:T(8,128)(2,1)S(1)}, bf16[256,1792]{1,0:T(8,128)(2,1)S(1)}, u32[]{:S(2)}, u32[]{:S(2)}) collective-permute-start(bf16[256,1792]{1,0:T(8,128)(2,1)S(1)} %bitcast.61), channel_id=1, source_target_pairs={{0,32},{32,0},{1,33},{33,1},{2,34},{34,2},{3,35},{35,3},{4,36},{36... | collective-permute-start | bytes 2752520 | tf_op jit(solution)/shard_map/ppermute | solution.py:43
  30.6 0.0 copy-done.6
  30.7 33.5 %all_gather.9 = bf16[256,1536]{1,0:T(8,128)(2,1)S(1)} all-gather(bf16[16,1536]{1,0:T(8,128)(2,1)S(1)} %pad_maximum_fusion.5), channel_id=1, replica_groups=mesh['zl'=8,'core'=2,'y'=4,'zh'=2,'x'=4] {'zh','zl'}, dimensions={0}, use_global_device_ids=true | all-gather | bytes 835584 | tf_op jit(solution)/shard_map/all_gather | solution.py:75
  64.2 1.7 multiply_reduce_fusion.4
  65.9 0.0 collective-permute-done
  65.9 0.0 copy-start.1
  65.9 1.3 fusion.33
  67.2 0.0 copy-done.3
  67.2 1.3 fusion.6
  68.5 0.0 copy-done
  68.5 1.6 multiply_reduce_fusion.1
  70.2 1.2 exponential_reduce_fusion.1
  71.4 0.1 rev.6
  71.6 0.6 broadcast_in_dim.16
  72.2 6.0 %all-to-all-start.2 = ((f32[16,6,128]{2,1,0:T(8,128)}), f32[16,6,128]{2,1,0:T(8,128)S(1)}, u32[]{:S(2)}, u32[]{:S(2)}) async-start(f32[16,6,128]{2,1,0:T(8,128)} %broadcast_in_dim.16), calls=%async_computation.2 | async-start | bytes 131072 | tf_op jit(solution)/shard_map/all_to_all | solution.py:39
  78.2 11.6 %all-to-all-done.2 = f32[16,6,128]{2,1,0:T(8,128)S(1)} async-done(((f32[16,6,128]{2,1,0:T(8,128)}), f32[16,6,128]{2,1,0:T(8,128)S(1)}, u32[]{:S(2)}, u32[]{:S(2)}) %all-to-all-start.2) | async-done | bytes 49184 | tf_op jit(solution)/shard_map/all_to_all | solution.py:39
  89.8 0.7 broadcast_in_dim.14
  90.6 12.1 %all-to-all-start.1 = ((f32[32,12,128]{2,1,0:T(8,128)}), f32[32,12,128]{2,1,0:T(8,128)S(1)}, u32[]{:S(2)}, u32[]{:S(2)}) async-start(f32[32,12,128]{2,1,0:T(8,128)} %broadcast_in_dim.14), calls=%async_computation.1 | async-start | bytes 524288 | tf_op jit(solution)/shard_map/all_to_all | solution.py:39
  102.7 1.5 reshape.190
  104.2 1.0 slice_reduce_fusion.2
  105.2 1.2 subtract_reduce_fusion.1
  106.4 4.6 %all-to-all-done.1 = f32[32,12,128]{2,1,0:T(8,128)S(1)} async-done(((f32[32,12,128]{2,1,0:T(8,128)}), f32[32,12,128]{2,1,0:T(8,128)S(1)}, u32[]{:S(2)}, u32[]{:S(2)}) %all-to-all-start.1) | async-done | bytes 196640 | tf_op jit(solution)/shard_map/all_to_all | solution.py:39
  111.0 0.8 reshape.189
  111.8 1.4 slice_reduce_fusion.1
  113.2 0.7 subtract_reduce_fusion
  113.9 0.1 rev.7
  114.1 2.3 %fusion.3 = (bf16[512,256]{1,0:T(8,128)(2,1)S(1)}, f32[]{:T(128)}) fusion(f32[512,256]{1,0:T(8,128)} %get-tuple-element.59, f32[512,256]{1,0:T(8,128)} %get-tuple-element.58, f32[256]{0:T(256)} %get-tuple-element.49, f32[512]{0:T(512)S(1)} %exponential_multiply_fusion, f32[256]{0:T(256)} %get-tuple-element.53, f32[256]{0:T(256)S(1)} %get-tuple-element.32, ...), kind=kLoop, calls=%fused_computation.20 | loop fusion | flops 1703935 | bytes 1319940 | tf_op jit(solution)/shard_map/convert_element_type | solution.py:109
  116.4 0.4 multiply_reduce_fusion.3
  116.8 0.4 multiply_reduce_fusion
  117.2 0.0 copy-start.2
  117.2 1.5 convolution_convert_fusion.1
  118.7 0.7 convolution_convert_fusion
  119.4 0.1 pad_maximum_fusion
  119.5 5.5 %all_to_all.30 = bf16[2,16,40,512]{3,2,1,0:T(8,128)(2,1)S(1)} all-to-all(bf16[2,16,40,512]{3,2,1,0:T(8,128)(2,1)S(1)} %pad_maximum_fusion), channel_id=1, replica_groups=mesh['zl'=8,'core'=2,'y'=4,'zh'=2,'x'=4] {'core'}, dimensions={0} | all-to-all | bytes 2621440 | tf_op jit(solution)/shard_map/all_to_all | solution.py:125
  125.0 1.2 reduce_sum.218
  126.3 3.6 %all-to-all-start.4 = ((bf16[16,40,512]{2,1,0:T(8,128)(2,1)}), bf16[16,40,512]{2,1,0:T(8,128)(2,1)S(1)}, u32[]{:S(2)}, u32[]{:S(2)}) async-start(bf16[16,40,512]{2,1,0:T(8,128)(2,1)} %reduce_sum.218), calls=%async_computation.4 | async-start | bytes 1310720 | tf_op jit(solution)/shard_map/all_to_all | solution.py:126
  131.8 0.1 maximum_bitcast_fusion
  131.9 10.4 %all-to-all-done.4 = bf16[16,40,512]{2,1,0:T(8,128)(2,1)S(1)} async-done(((bf16[16,40,512]{2,1,0:T(8,128)(2,1)}), bf16[16,40,512]{2,1,0:T(8,128)(2,1)S(1)}, u32[]{:S(2)}, u32[]{:S(2)}) %all-to-all-start.4) | async-done | bytes 655392 | tf_op jit(solution)/shard_map/all_to_all | solution.py:126
  142.2 0.1 reduce_sum.219
  142.4 25.4 %all-gather = bf16[768,512]{1,0:T(8,128)(2,1)S(1)} all-gather(bf16[48,512]{1,0:T(8,128)(2,1)S(1)} %fusion.24), channel_id=2, replica_groups=mesh['zl'=8,'core'=2,'y'=4,'zh'=2,'x'=4] {'zh','zl'}, dimensions={0}, use_global_device_ids=true | all-gather | bytes 835584 | tf_op jit(solution)/shard_map/all_gather | solution.py:127
  167.8 0.2 convert.2
  168.0 0.6 slice_reduce_fusion.3
  168.6 0.1 slice_reduce_fusion
  170.0 0.1 maximum_bitcast_fusion.1
  170.1 0.1 broadcast_in_dim.17
  170.2 13.5 %all_to_all.31 = bf16[16,48,512]{2,1,0:T(8,128)(2,1)S(1)} all-to-all(bf16[16,48,512]{2,1,0:T(8,128)(2,1)S(1)} %broadcast_in_dim.17), channel_id=1, replica_groups=mesh['zl'=8,'core'=2,'y'=4,'zh'=2,'x'=4] {'y','x'}, dimensions={0} | all-to-all | bytes 1572864 | tf_op jit(solution)/shard_map/all_to_all | solution.py:39
  183.6 11.1 %collective-permute-start.1 = (bf16[16,48,512]{2,1,0:T(8,128)(2,1)S(1)}, bf16[16,48,512]{2,1,0:T(8,128)(2,1)S(1)}, u32[]{:S(2)}, u32[]{:S(2)}) collective-permute-start(bf16[16,48,512]{2,1,0:T(8,128)(2,1)S(1)} %all_to_all.31), channel_id=1, source_target_pairs={{0,32},{32,0},{1,33},{33,1},{2,34},{34,2},{3,35},{35,3},{4,36},{36... | collective-permute-start | bytes 2359304 | tf_op jit(solution)/shard_map/ppermute | solution.py:43
  194.8 1.9 collective-permute-done.1
  196.7 0.1 select_bitcast_fusion.1
  196.8 0.6 convert_reduce_fusion
  197.4 1.1 maximum_convert_fusion.1
  198.5 0.2 maximum_convert_fusion
  198.7 1.3 slice.122
  (37 shorter events, 0.3 us)
Async XLA Ops:
  0.6 67.9 %copy-start = (bf16[768,512]{1,0:T(8,128)(2,1)S(1)}, bf16[768,512]{1,0:T(8,128)(2,1)}, u32[]{:S(2)}) copy-start(bf16[768,512]{1,0:T(8,128)(2,1)} %param.14) | copy-start | bytes 2359300
  0.6 11.1 %copy-start.5 = (bf16[16,1024]{1,0:T(8,128)(2,1)S(1)}, bf16[16,1024]{1,0:T(8,128)(2,1)}, u32[]{:S(2)}) copy-start(bf16[16,1024]{1,0:T(8,128)(2,1)} %param.13) | copy-start | bytes 98308
  0.7 30.0 %copy-start.6 = (bf16[16,512]{1,0:T(8,128)(2,1)S(1)}, bf16[16,512]{1,0:T(8,128)(2,1)}, u32[]{:S(2)}) copy-start(bf16[16,512]{1,0:T(8,128)(2,1)} %param.11) | copy-start | bytes 49156
  4.2 20.6 %all-to-all-start = ((bf16[16,16,1792]{2,1,0:T(8,128)(2,1)}), bf16[16,16,1792]{2,1,0:T(8,128)(2,1)S(1)}, u32[]{:S(2)}, u32[]{:S(2)}) async-start(bf16[16,16,1792]{2,1,0:T(8,128)(2,1)} %broadcast_in_dim.12), calls=%async_computation | async-start | bytes 1835008 | tf_op jit(solution)/shard_map/all_to_all | solution.py:39
  24.7 41.1 %collective-permute-start = (bf16[256,1792]{1,0:T(8,128)(2,1)S(1)}, bf16[256,1792]{1,0:T(8,128)(2,1)S(1)}, u32[]{:S(2)}, u32[]{:S(2)}) collective-permute-start(bf16[256,1792]{1,0:T(8,128)(2,1)S(1)} %bitcast.61), channel_id=1, source_target_pairs={{0,32},{32,0},{1,33},{33,1},{2,34},{34,2},{3,35},{35,3},{4,36},{36... | collective-permute-start | bytes 2752520 | tf_op jit(solution)/shard_map/ppermute | solution.py:43
  64.2 3.0 %copy-start.3 = (bf16[256,1536]{1,0:T(8,128)(2,1)}, bf16[256,1536]{1,0:T(8,128)(2,1)S(1)}, u32[]{:S(2)}) copy-start(bf16[256,1536]{1,0:T(8,128)(2,1)S(1)} %all_gather.9) | copy-start | bytes 2359300
  65.9 1.3 copy-start.1
  72.2 17.6 %all-to-all-start.2 = ((f32[16,6,128]{2,1,0:T(8,128)}), f32[16,6,128]{2,1,0:T(8,128)S(1)}, u32[]{:S(2)}, u32[]{:S(2)}) async-start(f32[16,6,128]{2,1,0:T(8,128)} %broadcast_in_dim.16), calls=%async_computation.2 | async-start | bytes 131072 | tf_op jit(solution)/shard_map/all_to_all | solution.py:39
  89.8 0.7 copy-start.4
  90.6 20.4 %all-to-all-start.1 = ((f32[32,12,128]{2,1,0:T(8,128)}), f32[32,12,128]{2,1,0:T(8,128)S(1)}, u32[]{:S(2)}, u32[]{:S(2)}) async-start(f32[32,12,128]{2,1,0:T(8,128)} %broadcast_in_dim.14), calls=%async_computation.1 | async-start | bytes 524288 | tf_op jit(solution)/shard_map/all_to_all | solution.py:39
  117.2 1.5 copy-start.2
  126.3 16.0 %all-to-all-start.4 = ((bf16[16,40,512]{2,1,0:T(8,128)(2,1)}), bf16[16,40,512]{2,1,0:T(8,128)(2,1)S(1)}, u32[]{:S(2)}, u32[]{:S(2)}) async-start(bf16[16,40,512]{2,1,0:T(8,128)(2,1)} %reduce_sum.218), calls=%async_computation.4 | async-start | bytes 1310720 | tf_op jit(solution)/shard_map/all_to_all | solution.py:126
  183.6 13.0 %collective-permute-start.1 = (bf16[16,48,512]{2,1,0:T(8,128)(2,1)S(1)}, bf16[16,48,512]{2,1,0:T(8,128)(2,1)S(1)}, u32[]{:S(2)}, u32[]{:S(2)}) collective-permute-start(bf16[16,48,512]{2,1,0:T(8,128)(2,1)S(1)} %all_to_all.31), channel_id=1, source_target_pairs={{0,32},{32,0},{1,33},{33,1},{2,34},{34,2},{3,35},{35,3},{4,36},{36... | collective-permute-start | bytes 2359304 | tf_op jit(solution)/shard_map/ppermute | solution.py:43

commit v3 on v2

--- a/solution.py
+++ b/solution.py
@@ -71,8 +71,9 @@
     pack_txt = jnp.concatenate([normed(teacher_txt), text_feats], 1)
     half_img = spread(pack_img, PLANE)
     half_img = half_img.reshape(-1, pack_img.shape[1])
+    block_txt = lax.all_gather(pack_txt, RING, axis=0, tiled=True)
+    half_img, block_txt = lax.optimization_barrier((half_img, block_txt))
     other_img = swap_cores(half_img)
-    block_txt = lax.all_gather(pack_txt, RING, axis=0, tiled=True)
     block_img = jnp.concatenate([half_img, other_img], 0)
     q_img, feats_img = (block_img[:, :dt], block_img[:, dt:])
     q_txt, feats_txt = (block_txt[:, :dt], block_txt[:, dt:])

time: 203 us -> 194 us (0.956)
  waiting for transfers between devices: 41.2 us -> 31.4 us
  other arithmetic: 15.2 us -> 12.7 us
  local copies, waits for them, and re-layouts: 6.39 us -> 8.61 us
    all_to_all x3, waiting for transfers between devices: 29 us -> 19.2 us  [spread(): return lax.all_to_all(copies, axes, 0, 0, tiled=True)]
    ppermute x2, starting transfers between devices: 17 us -> 20 us  [swap_cores(): return lax.ppermute(block, 'core', [(0, 1), (1, 0)])]
    concatenate x0 -> x1, local copies, waits for them, and re-layouts: none -> 2.21 us  [shards(): block_img = jnp.concatenate([half_img, other_img], 0)]
  transfers between devices with their start and end apart: 6 -> 6, of which waited for: 5 -> 4; matrix products, arithmetic and copies ran while one was open for 3% -> 2% of each run, Pallas kernels for 0% -> 0%
where the time goes in v3:
time: 194 us; the launch traced here: 193 us
  blocking collectives  78.3 us (40%)
  starting transfers between devices  47.2 us (24%)
  waiting for transfers between devices  31.4 us (16%)
  other arithmetic  12.7 us (7%)
  matrix products  9.27 us (5%)
  local copies, waits for them, and re-layouts  8.61 us (4%)
  between operations  5.95 us (3%)
    all_gather x1, blocking collectives, shards(): block_txt = lax.all_gather(pack_txt, RING, axis=0, tiled=True)  33.8 us
    all_gather x1, blocking collectives, shards(): part = lax.all_gather(with_loss(part, total), RING).astype(F32)  25.8 us
    all_to_all x3, starting transfers between devices, spread(): return lax.all_to_all(copies, axes, 0, 0, tiled=True)  23.7 us
    ppermute x2, starting transfers between devices, swap_cores(): return lax.ppermute(block, 'core', [(0, 1), (1, 0)])  20 us
    all_to_all x3, waiting for transfers between devices, spread(): return lax.all_to_all(copies, axes, 0, 0, tiled=True)  19.2 us
    all_to_all x1, blocking collectives, spread(): return lax.all_to_all(copies, axes, 0, 0, tiled=True)  13.3 us
    all_to_all x1, waiting for transfers between devices, shards(): part = lax.all_to_all(part, PLANE, 0, 0, tiled=True).astype(F32).sum(0)  10.4 us
    all_to_all x1, blocking collectives, shards(): lax.all_to_all(part, 'core', 0, 0, tiled=True).astype(F32).sum(0)  5.51 us
  transfers between devices with their start and end apart: 6, of which 4 were waited for; matrix products, arithmetic and copies ran while one was open for 2% of the time, Pallas kernels for 0%

profile of v3, /device:TPU:1, one launch (start us, length us, event | category | flops | bytes accessed | tf_op | source)
XLA Modules:
  0.0 193.5 jit_solution(8017531957717240513)
XLA Ops:
  0.6 0.0 copy-start
  0.6 0.0 copy-start.2
  0.7 0.0 copy-start.3
  0.7 0.9 fusion.19
  1.6 0.8 fusion.20
  2.5 0.7 pad_maximum_fusion.1
  3.2 1.0 broadcast_in_dim.12
  4.2 7.6 %all-to-all-start = ((bf16[16,16,1792]{2,1,0:T(8,128)(2,1)}), bf16[16,16,1792]{2,1,0:T(8,128)(2,1)S(1)}, u32[]{:S(2)}, u32[]{:S(2)}) async-start(bf16[16,16,1792]{2,1,0:T(8,128)(2,1)} %broadcast_in_dim.12), calls=%async_computation | async-start | bytes 1835008 | tf_op jit(solution)/shard_map/all_to_all | solution.py:39
  11.8 0.0 copy-done.2
  11.8 0.1 fusion.21
  11.9 0.1 fusion.22
  12.0 0.0 copy-done.3
  12.0 33.8 %all_gather.9 = bf16[256,1536]{1,0:T(8,128)(2,1)S(1)} all-gather(bf16[16,1536]{1,0:T(8,128)(2,1)S(1)} %pad_maximum_fusion.2), channel_id=1, replica_groups=mesh['zl'=8,'core'=2,'y'=4,'zh'=2,'x'=4] {'zh','zl'}, dimensions={0}, use_global_device_ids=true | all-gather | bytes 835584 | tf_op jit(solution)/shard_map/all_gather | solution.py:74
  45.8 0.0 all-to-all-done
  45.8 8.9 %collective-permute-start = (bf16[256,1792]{1,0:T(8,128)(2,1)S(1)}, bf16[256,1792]{1,0:T(8,128)(2,1)}, u32[]{:S(2)}, u32[]{:S(2)}) collective-permute-start(bf16[256,1792]{1,0:T(8,128)(2,1)S(1)} %bitcast.61), channel_id=1, source_target_pairs={{0,32},{32,0},{1,33},{33,1},{2,34},{34,2},{3,35},{35,3},{4,36},{36... | collective-permute-start | bytes 2752520 | tf_op jit(solution)/shard_map/ppermute | solution.py:43
  54.7 1.4 multiply_reduce_fusion.4
  56.1 1.0 constant_dynamic-update-slice_fusion.1
  57.1 0.0 collective-permute-done
  57.1 2.2 %constant_dynamic-update-slice_fusion = bf16[512,1792]{1,0:T(8,128)(2,1)} fusion(bf16[512,1792]{1,0:T(8,128)(2,1)} %constant_dynamic-update-slice_fusion.1, bf16[256,1792]{1,0:T(8,128)(2,1)} %collective-permute-done), kind=kLoop, calls=%fused_computation.63 | loop fusion | bytes 1835008 | tf_op jit(solution)/shard_map/concatenate | solution.py:77
  59.3 1.8 fusion.34
  61.1 0.2 fusion.9
  61.4 0.5 copy-done.1
  61.9 0.0 copy-done
  61.9 1.8 multiply_reduce_fusion.1
  63.7 1.2 exponential_reduce_fusion.1
  64.9 0.1 rev.6
  65.1 0.6 broadcast_in_dim.16
  65.7 6.5 %all-to-all-start.2 = ((f32[16,6,128]{2,1,0:T(8,128)}), f32[16,6,128]{2,1,0:T(8,128)S(1)}, u32[]{:S(2)}, u32[]{:S(2)}) async-start(f32[16,6,128]{2,1,0:T(8,128)} %broadcast_in_dim.16), calls=%async_computation.2 | async-start | bytes 131072 | tf_op jit(solution)/shard_map/all_to_all | solution.py:39
  72.2 11.6 %all-to-all-done.2 = f32[16,6,128]{2,1,0:T(8,128)S(1)} async-done(((f32[16,6,128]{2,1,0:T(8,128)}), f32[16,6,128]{2,1,0:T(8,128)S(1)}, u32[]{:S(2)}, u32[]{:S(2)}) %all-to-all-start.2) | async-done | bytes 49184 | tf_op jit(solution)/shard_map/all_to_all | solution.py:39
  83.8 0.7 broadcast_in_dim.14
  84.6 9.6 %all-to-all-start.1 = ((f32[32,12,128]{2,1,0:T(8,128)}), f32[32,12,128]{2,1,0:T(8,128)S(1)}, u32[]{:S(2)}, u32[]{:S(2)}) async-start(f32[32,12,128]{2,1,0:T(8,128)} %broadcast_in_dim.14), calls=%async_computation.1 | async-start | bytes 524288 | tf_op jit(solution)/shard_map/all_to_all | solution.py:39
  94.2 0.1 slice_reduce_fusion.2
  94.3 0.6 subtract_reduce_fusion.1
  94.9 7.6 %all-to-all-done.1 = f32[32,12,128]{2,1,0:T(8,128)S(1)} async-done(((f32[32,12,128]{2,1,0:T(8,128)}), f32[32,12,128]{2,1,0:T(8,128)S(1)}, u32[]{:S(2)}, u32[]{:S(2)}) %all-to-all-start.1) | async-done | bytes 196640 | tf_op jit(solution)/shard_map/all_to_all | solution.py:39
  102.4 0.8 reshape.189
  103.2 1.4 slice_reduce_fusion.1
  104.7 0.6 subtract_reduce_fusion
  105.4 0.1 rev.7
  105.5 2.3 %fusion.5 = (bf16[512,256]{1,0:T(8,128)(2,1)S(1)}, f32[]{:T(128)}) fusion(f32[512,256]{1,0:T(8,128)} %copy-done.1, f32[512,256]{1,0:T(8,128)} %get-tuple-element.62, f32[256]{0:T(256)S(1)} %get-tuple-element.53, f32[512]{0:T(512)S(1)} %exponential_multiply_fusion, f32[256]{0:T(256)S(1)} %get-tuple-element.57, f32[256]{0:T(256)S(1)} %get-tuple-element.36, ...), kind=kLoop, calls=%fused_computation.20 | loop fusion | flops 1703935 | bytes 1319940 | tf_op jit(solution)/shard_map/convert_element_type | solution.py:110
  107.9 0.4 multiply_reduce_fusion.3
  108.3 0.4 multiply_reduce_fusion
  108.7 0.4 convolution_convert_fusion.1
  109.2 1.8 convolution_convert_fusion
  111.0 0.1 pad_maximum_fusion
  111.1 5.5 %all_to_all.30 = bf16[2,16,40,512]{3,2,1,0:T(8,128)(2,1)S(1)} all-to-all(bf16[2,16,40,512]{3,2,1,0:T(8,128)(2,1)S(1)} %pad_maximum_fusion), channel_id=1, replica_groups=mesh['zl'=8,'core'=2,'y'=4,'zh'=2,'x'=4] {'core'}, dimensions={0} | all-to-all | bytes 2621440 | tf_op jit(solution)/shard_map/all_to_all | solution.py:126
  116.6 1.2 reduce_sum.218
  117.8 3.6 %all-to-all-start.4 = ((bf16[16,40,512]{2,1,0:T(8,128)(2,1)}), bf16[16,40,512]{2,1,0:T(8,128)(2,1)S(1)}, u32[]{:S(2)}, u32[]{:S(2)}) async-start(bf16[16,40,512]{2,1,0:T(8,128)(2,1)} %reduce_sum.218), calls=%async_computation.4 | async-start | bytes 1310720 | tf_op jit(solution)/shard_map/all_to_all | solution.py:127
  123.4 0.1 maximum_bitcast_fusion
  123.4 10.4 %all-to-all-done.4 = bf16[16,40,512]{2,1,0:T(8,128)(2,1)S(1)} async-done(((bf16[16,40,512]{2,1,0:T(8,128)(2,1)}), bf16[16,40,512]{2,1,0:T(8,128)(2,1)S(1)}, u32[]{:S(2)}, u32[]{:S(2)}) %all-to-all-start.4) | async-done | bytes 655392 | tf_op jit(solution)/shard_map/all_to_all | solution.py:127
  133.8 0.1 reduce_sum.219
  133.9 25.8 %all-gather = bf16[768,512]{1,0:T(8,128)(2,1)S(1)} all-gather(bf16[48,512]{1,0:T(8,128)(2,1)S(1)} %fusion.27), channel_id=2, replica_groups=mesh['zl'=8,'core'=2,'y'=4,'zh'=2,'x'=4] {'zh','zl'}, dimensions={0}, use_global_device_ids=true | all-gather | bytes 835584 | tf_op jit(solution)/shard_map/all_gather | solution.py:128
  159.7 0.2 convert.2
  159.9 0.6 slice_reduce_fusion.3
  160.5 0.1 slice_reduce_fusion
  161.9 0.1 maximum_bitcast_fusion.1
  162.0 0.1 broadcast_in_dim.17
  162.1 13.3 %all_to_all.31 = bf16[16,48,512]{2,1,0:T(8,128)(2,1)S(1)} all-to-all(bf16[16,48,512]{2,1,0:T(8,128)(2,1)S(1)} %broadcast_in_dim.17), channel_id=1, replica_groups=mesh['zl'=8,'core'=2,'y'=4,'zh'=2,'x'=4] {'y','x'}, dimensions={0} | all-to-all | bytes 1572864 | tf_op jit(solution)/shard_map/all_to_all | solution.py:39
  175.4 11.1 %collective-permute-start.1 = (bf16[16,48,512]{2,1,0:T(8,128)(2,1)S(1)}, bf16[16,48,512]{2,1,0:T(8,128)(2,1)S(1)}, u32[]{:S(2)}, u32[]{:S(2)}) collective-permute-start(bf16[16,48,512]{2,1,0:T(8,128)(2,1)S(1)} %all_to_all.31), channel_id=1, source_target_pairs={{0,32},{32,0},{1,33},{33,1},{2,34},{34,2},{3,35},{35,3},{4,36},{36... | collective-permute-start | bytes 2359304 | tf_op jit(solution)/shard_map/ppermute | solution.py:43
  186.4 1.9 collective-permute-done.1
  188.3 0.1 select_bitcast_fusion.1
  188.4 0.6 convert_reduce_fusion
  189.1 1.1 maximum_convert_fusion.1
  190.2 0.2 maximum_convert_fusion
  190.4 1.3 slice.122
  (33 shorter events, 0.3 us)
Async XLA Ops:
  0.6 61.3 %copy-start = (bf16[768,512]{1,0:T(8,128)(2,1)S(1)}, bf16[768,512]{1,0:T(8,128)(2,1)}, u32[]{:S(2)}) copy-start(bf16[768,512]{1,0:T(8,128)(2,1)} %param.14) | copy-start | bytes 2359300
  0.6 11.1 %copy-start.2 = (bf16[16,1024]{1,0:T(8,128)(2,1)S(1)}, bf16[16,1024]{1,0:T(8,128)(2,1)}, u32[]{:S(2)}) copy-start(bf16[16,1024]{1,0:T(8,128)(2,1)} %param.13) | copy-start | bytes 98308
  0.7 11.3 %copy-start.3 = (bf16[16,512]{1,0:T(8,128)(2,1)S(1)}, bf16[16,512]{1,0:T(8,128)(2,1)}, u32[]{:S(2)}) copy-start(bf16[16,512]{1,0:T(8,128)(2,1)} %param.11) | copy-start | bytes 49156
  4.2 41.6 %all-to-all-start = ((bf16[16,16,1792]{2,1,0:T(8,128)(2,1)}), bf16[16,16,1792]{2,1,0:T(8,128)(2,1)S(1)}, u32[]{:S(2)}, u32[]{:S(2)}) async-start(bf16[16,16,1792]{2,1,0:T(8,128)(2,1)} %broadcast_in_dim.12), calls=%async_computation | async-start | bytes 1835008 | tf_op jit(solution)/shard_map/all_to_all | solution.py:39
  45.8 11.3 %collective-permute-start = (bf16[256,1792]{1,0:T(8,128)(2,1)S(1)}, bf16[256,1792]{1,0:T(8,128)(2,1)}, u32[]{:S(2)}, u32[]{:S(2)}) collective-permute-start(bf16[256,1792]{1,0:T(8,128)(2,1)S(1)} %bitcast.61), channel_id=1, source_target_pairs={{0,32},{32,0},{1,33},{33,1},{2,34},{34,2},{3,35},{35,3},{4,36},{36... | collective-permute-start | bytes 2752520 | tf_op jit(solution)/shard_map/ppermute | solution.py:43
  61.1 0.8 copy-start.1
  65.7 18.2 %all-to-all-start.2 = ((f32[16,6,128]{2,1,0:T(8,128)}), f32[16,6,128]{2,1,0:T(8,128)S(1)}, u32[]{:S(2)}, u32[]{:S(2)}) async-start(f32[16,6,128]{2,1,0:T(8,128)} %broadcast_in_dim.16), calls=%async_computation.2 | async-start | bytes 131072 | tf_op jit(solution)/shard_map/all_to_all | solution.py:39
  84.6 17.9 %all-to-all-start.1 = ((f32[32,12,128]{2,1,0:T(8,128)}), f32[32,12,128]{2,1,0:T(8,128)S(1)}, u32[]{:S(2)}, u32[]{:S(2)}) async-start(f32[32,12,128]{2,1,0:T(8,128)} %broadcast_in_dim.14), calls=%async_computation.1 | async-start | bytes 524288 | tf_op jit(solution)/shard_map/all_to_all | solution.py:39
  117.8 16.0 %all-to-all-start.4 = ((bf16[16,40,512]{2,1,0:T(8,128)(2,1)}), bf16[16,40,512]{2,1,0:T(8,128)(2,1)S(1)}, u32[]{:S(2)}, u32[]{:S(2)}) async-start(bf16[16,40,512]{2,1,0:T(8,128)(2,1)} %reduce_sum.218), calls=%async_computation.4 | async-start | bytes 1310720 | tf_op jit(solution)/shard_map/all_to_all | solution.py:127
  175.4 13.0 %collective-permute-start.1 = (bf16[16,48,512]{2,1,0:T(8,128)(2,1)S(1)}, bf16[16,48,512]{2,1,0:T(8,128)(2,1)S(1)}, u32[]{:S(2)}, u32[]{:S(2)}) collective-permute-start(bf16[16,48,512]{2,1,0:T(8,128)(2,1)S(1)} %all_to_all.31), channel_id=1, source_target_pairs={{0,32},{32,0},{1,33},{33,1},{2,34},{34,2},{3,35},{35,3},{4,36},{36... | collective-permute-start | bytes 2359304 | tf_op jit(solution)/shard_map/ppermute | solution.py:43

commit v4 on v2

--- a/solution.py
+++ b/solution.py
@@ -8,10 +8,10 @@
 TEACHER_SCALE = 100.0
 STUDENT_SCALE = 50.0
 
-AXES = ("zl", "core", "y", "zh", "x")
-SIZES = (8, 2, 4, 2, 4)
+AXES = ("zm", "zn", "core", "y", "zh", "x")
+SIZES = (2, 4, 2, 4, 2, 4)
 PLANE = ("y", "x")
-RING = ("zh", "zl")
+RING = ("zh", "zm", "zn")
 TILE = ("core", "y", "x")
 
 BF16 = jnp.bfloat16
@@ -69,11 +69,9 @@
     dt = teacher_img.shape[1]
     pack_img = jnp.concatenate([normed(teacher_img), image_feats], 1)
     pack_txt = jnp.concatenate([normed(teacher_txt), text_feats], 1)
-    half_img = spread(pack_img, PLANE)
-    half_img = half_img.reshape(-1, pack_img.shape[1])
-    other_img = swap_cores(half_img)
+    block_img = spread(pack_img, TILE).reshape(-1, pack_img.shape[1])
     block_txt = lax.all_gather(pack_txt, RING, axis=0, tiled=True)
-    block_img = jnp.concatenate([half_img, other_img], 0)
+    block_img, block_txt = lax.optimization_barrier((block_img, block_txt))
     q_img, feats_img = (block_img[:, :dt], block_img[:, dt:])
     q_txt, feats_txt = (block_txt[:, :dt], block_txt[:, dt:])
     e_img, inv_img = project(feats_img, proj_img)
@@ -91,7 +89,6 @@
     es = jnp.exp(sl)
     row_stats = jnp.stack([rm, er.sum(1), es.sum(1)]).reshape(3, 2, -1)
     col_stats = jnp.stack([cm, ec.sum(0), es.sum(0)])
-    row_stats = jnp.where(core == 0, row_stats, row_stats[:, ::-1])
     row_all = spread(row_stats.reshape(-1, 128), TILE).reshape(-1, 3, rows)
     col_all = spread(col_stats.reshape(-1, 128), RING).reshape(-1, 3, cols)
     row_top, row_t, row_s = merge(row_all)
@@ -99,7 +96,7 @@
     row_lse = jnp.sum(jnp.log(row_s) - row_top - jnp.log(row_t))
     col_lse = jnp.sum(jnp.log(col_s) - col_top - jnp.log(col_t))
     mine = jnp.stack([row_top, 1.0 / row_t, 1.0 / row_s]).reshape(3, 2, -1)
-    mine = jnp.where(core == 0, mine, mine[:, ::-1]).reshape(3, rows)
+    mine = mine.reshape(3, rows)
     row_gain = jnp.exp(rm - mine[0]) * mine[1]
     col_gain = jnp.exp(cm - col_top) / col_t
     pt = er * row_gain[:, None] + ec * col_gain[None, :]
@@ -124,7 +121,9 @@
     chunk = part.shape[2]
     part = lax.all_to_all(part, "core", 0, 0, tiled=True).astype(F32).sum(0).astype(BF16)
     part = lax.all_to_all(part, PLANE, 0, 0, tiled=True).astype(F32).sum(0)
-    part = lax.all_gather(with_loss(part, total), RING).astype(F32)
+    part = spread(with_loss(part, total), ("zn",)).astype(F32)
+    mid_loss = part[:, chunk, :3].sum()
+    part = spread(with_loss(part[:, :chunk].sum(0), mid_loss), ("zh", "zm")).astype(F32)
     chunk_sum = part[:, :chunk].sum(0)
     ring_loss = part[:, chunk, :3].sum()
     own = spread(with_loss(chunk_sum, ring_loss), PLANE)
@@ -141,8 +140,8 @@
 
 def solution(mesh):
     fine = Mesh(mesh.devices.reshape(SIZES), AXES)
-    img = P(("zl", "core", "y", "zh", "x"), None)
-    txt = P(("y", "zh", "x", "zl", "core"), None)
+    img = P(("zm", "zn", "core", "y", "zh", "x"), None)
+    txt = P(("y", "zh", "x", "zm", "zn", "core"), None)
     return jax.shard_map(
         shards,
         mesh=fine,

time: 203 us -> 187 us (0.921)
  waiting for transfers between devices: 41.2 us -> 31.3 us
  starting transfers between devices: 46.3 us -> 42.1 us
    all_to_all x1 -> x3, blocking collectives: 13.5 us -> 41.2 us  [spread(): return lax.all_to_all(copies, axes, 0, 0, tiled=True)]
    all_gather x1 -> x0, blocking collectives: 25.4 us -> none  [shards(): part = lax.all_gather(with_loss(part, total), RING).astype(F32)]
    ppermute x2 -> x1, starting transfers between devices: 17 us -> 6.68 us  [swap_cores(): return lax.ppermute(block, 'core', [(0, 1), (1, 0)])]
    all_to_all x3, waiting for transfers between devices: 29 us -> 19.1 us  [spread(): return lax.all_to_all(copies, axes, 0, 0, tiled=True)]
    all_to_all x3, starting transfers between devices: 25.7 us -> 31.9 us  [spread(): return lax.all_to_all(copies, axes, 0, 0, tiled=True)]
  transfers between devices with their start and end apart: 6 -> 5, of which waited for: 5 -> 4; matrix products, arithmetic and copies ran while one was open for 3% -> 1% of each run, Pallas kernels for 0% -> 0%
where the time goes in v4:
time: 187 us; the launch traced here: 186 us
  blocking collectives  79.1 us (42%)
  starting transfers between devices  42.1 us (23%)
  waiting for transfers between devices  31.3 us (17%)
  other arithmetic  13.2 us (7%)
  matrix products  8.42 us (5%)
  between operations  7.2 us (4%)
  local copies, waits for them, and re-layouts  4.97 us (3%)
    all_to_all x3, blocking collectives, spread(): return lax.all_to_all(copies, axes, 0, 0, tiled=True)  41.2 us
    all_gather x1, blocking collectives, shards(): block_txt = lax.all_gather(pack_txt, RING, axis=0, tiled=True)  32.3 us
    all_to_all x3, starting transfers between devices, spread(): return lax.all_to_all(copies, axes, 0, 0, tiled=True)  31.9 us
    all_to_all x3, waiting for transfers between devices, spread(): return lax.all_to_all(copies, axes, 0, 0, tiled=True)  19.1 us
    all_to_all x1, waiting for transfers between devices, shards(): part = lax.all_to_all(part, PLANE, 0, 0, tiled=True).astype(F32).sum(0)  10.4 us
    ppermute x1, starting transfers between devices, swap_cores(): return lax.ppermute(block, 'core', [(0, 1), (1, 0)])  6.68 us
    all_to_all x1, blocking collectives, shards(): lax.all_to_all(part, 'core', 0, 0, tiled=True).astype(F32).sum(0)  5.5 us
  transfers between devices with their start and end apart: 5, of which 4 were waited for; matrix products, arithmetic and copies ran while one was open for 1% of the time, Pallas kernels for 0%

profile of v4, /device:TPU:1, one launch (start us, length us, event | category | flops | bytes accessed | tf_op | source)
XLA Modules:
  0.0 186.3 jit_solution(7815332836455097084)
XLA Ops:
  0.6 0.0 copy-start
  0.6 1.0 fusion.20
  1.6 0.8 fusion.21
  2.4 0.7 pad_maximum_fusion.1
  3.2 1.3 broadcast_in_dim.16
  4.5 0.0 copy-start.3
  4.5 0.0 copy-start.4
  4.5 0.0 copy-start.2
  4.5 11.4 %all-to-all-start = ((bf16[32,16,1792]{2,1,0:T(8,128)(2,1)}), bf16[32,16,1792]{2,1,0:T(8,128)(2,1)}, u32[]{:S(2)}, u32[]{:S(2)}) async-start(bf16[32,16,1792]{2,1,0:T(8,128)(2,1)} %broadcast_in_dim.16), calls=%async_computation | async-start | bytes 3670016 | tf_op jit(solution)/shard_map/all_to_all | solution.py:39
  16.0 0.0 copy-done.3
  16.0 0.1 fusion.22
  16.1 0.1 fusion.23
  16.2 0.0 copy-done.4
  16.2 32.3 %all_gather.3 = bf16[256,1536]{1,0:T(8,128)(2,1)S(1)} all-gather(bf16[16,1536]{1,0:T(8,128)(2,1)S(1)} %pad_maximum_fusion.2), channel_id=1, replica_groups=mesh['zm'=2,'zn'=4,'core'=2,'y'=4,'zh'=2,'x'=4] {'zh','zm','zn'}, dimensions={0}, use_global_device_ids=true | all-gather | bytes 835584 | tf_op jit(solution)/shard_map/all_gather | solution.py:73
  48.6 0.0 all-to-all-done
  48.6 0.0 copy-done.2
  48.6 0.4 multiply_reduce_fusion.4
  49.0 1.8 fusion.36
  50.7 0.0 copy-done
  50.7 0.0 copy-start.1
  50.8 2.0 %multiply_reduce_fusion.1 = (f32[512]{0:T(512)S(1)}, f32[512,512]{0,1:T(8,128)S(1)}) fusion(bf16[768,512]{1,0:T(8,128)(2,1)S(1)} %copy-done, bf16[512,1792]{1,0:T(8,128)(2,1)} %bitcast), kind=kOutput, calls=%fused_computation.9 | convolution fusion | flops 403176960 | bytes 2623488 | tf_op jit(solution)/shard_map/dot_general | solution.py:22
  52.7 0.0 copy-done.1
  52.7 0.2 fusion.9
  53.0 1.2 exponential_reduce_fusion.1
  54.2 0.6 broadcast_in_dim.20
  54.9 7.1 %all-to-all-start.2 = ((f32[16,6,128]{2,1,0:T(8,128)}), f32[16,6,128]{2,1,0:T(8,128)S(1)}, u32[]{:S(2)}, u32[]{:S(2)}) async-start(f32[16,6,128]{2,1,0:T(8,128)} %broadcast_in_dim.20), calls=%async_computation.2 | async-start | bytes 131072 | tf_op jit(solution)/shard_map/all_to_all | solution.py:39
  62.0 11.5 %all-to-all-done.2 = f32[16,6,128]{2,1,0:T(8,128)S(1)} async-done(((f32[16,6,128]{2,1,0:T(8,128)}), f32[16,6,128]{2,1,0:T(8,128)S(1)}, u32[]{:S(2)}, u32[]{:S(2)}) %all-to-all-start.2) | async-done | bytes 49184 | tf_op jit(solution)/shard_map/all_to_all | solution.py:39
  73.5 0.7 broadcast_in_dim.18
  74.2 13.4 %all-to-all-start.1 = ((f32[32,12,128]{2,1,0:T(8,128)}), f32[32,12,128]{2,1,0:T(8,128)S(1)}, u32[]{:S(2)}, u32[]{:S(2)}) async-start(f32[32,12,128]{2,1,0:T(8,128)} %broadcast_in_dim.18), calls=%async_computation.1 | async-start | bytes 524288 | tf_op jit(solution)/shard_map/all_to_all | solution.py:39
  87.6 0.1 slice_reduce_fusion.3
  87.7 0.6 subtract_reduce_fusion.1
  88.3 7.6 %all-to-all-done.1 = f32[32,12,128]{2,1,0:T(8,128)S(1)} async-done(((f32[32,12,128]{2,1,0:T(8,128)}), f32[32,12,128]{2,1,0:T(8,128)S(1)}, u32[]{:S(2)}, u32[]{:S(2)}) %all-to-all-start.1) | async-done | bytes 196640 | tf_op jit(solution)/shard_map/all_to_all | solution.py:39
  95.9 0.8 reshape.171
  96.7 1.4 slice_reduce_fusion.2
  98.1 0.6 subtract_reduce_fusion
  98.8 2.3 %fusion.5 = (bf16[512,256]{1,0:T(8,128)(2,1)S(1)}, f32[]{:T(128)}) fusion(f32[512,256]{1,0:T(8,128)} %copy-done.1, f32[512,256]{1,0:T(8,128)} %get-tuple-element.71, f32[256]{0:T(256)S(1)} %get-tuple-element.65, f32[512]{0:T(512)S(1)} %get-tuple-element.62, f32[256]{0:T(256)S(1)} %get-tuple-element.66, f32[256]{0:T(256)S(1)} %get-tuple-element.46, ...), kind=kLoop, calls=%fused_computation.19 | loop fusion | flops 1703935 | bytes 1319940 | tf_op jit(solution)/shard_map/convert_element_type | solution.py:106
  101.1 0.4 multiply_reduce_fusion.3
  101.5 0.4 multiply_reduce_fusion
  101.9 0.4 convolution_convert_fusion.1
  102.4 1.8 convolution_convert_fusion
  104.2 0.1 pad_maximum_fusion
  104.3 5.5 %all_to_all.40 = bf16[2,16,40,512]{3,2,1,0:T(8,128)(2,1)S(1)} all-to-all(bf16[2,16,40,512]{3,2,1,0:T(8,128)(2,1)S(1)} %pad_maximum_fusion), channel_id=1, replica_groups=mesh['zm'=2,'zn'=4,'core'=2,'y'=4,'zh'=2,'x'=4] {'core'}, dimensions={0} | all-to-all | bytes 2621440 | tf_op jit(solution)/shard_map/all_to_all | solution.py:122
  109.8 1.2 reduce_sum.236
  111.0 3.6 %all-to-all-start.4 = ((bf16[16,40,512]{2,1,0:T(8,128)(2,1)}), bf16[16,40,512]{2,1,0:T(8,128)(2,1)S(1)}, u32[]{:S(2)}, u32[]{:S(2)}) async-start(bf16[16,40,512]{2,1,0:T(8,128)(2,1)} %reduce_sum.236), calls=%async_computation.4 | async-start | bytes 1310720 | tf_op jit(solution)/shard_map/all_to_all | solution.py:123
  116.6 0.1 maximum_bitcast_fusion
  116.6 10.4 %all-to-all-done.4 = bf16[16,40,512]{2,1,0:T(8,128)(2,1)S(1)} async-done(((bf16[16,40,512]{2,1,0:T(8,128)(2,1)}), bf16[16,40,512]{2,1,0:T(8,128)(2,1)S(1)}, u32[]{:S(2)}, u32[]{:S(2)}) %all-to-all-start.4) | async-done | bytes 655392 | tf_op jit(solution)/shard_map/all_to_all | solution.py:123
  127.0 0.1 reduce_sum.237
  127.1 8.0 %all_to_all.41 = bf16[4,48,512]{2,1,0:T(8,128)(2,1)S(1)} all-to-all(bf16[4,48,512]{2,1,0:T(8,128)(2,1)S(1)} %broadcast_in_dim.21), channel_id=1, replica_groups=mesh['zm'=2,'zn'=4,'core'=2,'y'=4,'zh'=2,'x'=4] {'zn'}, dimensions={0} | all-to-all | bytes 393216 | tf_op jit(solution)/shard_map/all_to_all | solution.py:39
  135.2 0.6 slice_reduce_fusion.5
  137.1 0.1 maximum_bitcast_fusion.1
  137.3 19.3 %all_to_all.42 = bf16[4,48,512]{2,1,0:T(8,128)(2,1)S(1)} all-to-all(bf16[4,48,512]{2,1,0:T(8,128)(2,1)S(1)} %broadcast_in_dim.22), channel_id=1, replica_groups=mesh['zm'=2,'zn'=4,'core'=2,'y'=4,'zh'=2,'x'=4] {'zh','zm'}, dimensions={0} | all-to-all | bytes 393216 | tf_op jit(solution)/shard_map/all_to_all | solution.py:39
  156.6 0.6 slice_reduce_fusion.4
  158.5 0.1 maximum_bitcast_fusion.2
  158.6 0.1 broadcast_in_dim.23
  158.7 14.0 %all_to_all.43 = bf16[16,48,512]{2,1,0:T(8,128)(2,1)S(1)} all-to-all(bf16[16,48,512]{2,1,0:T(8,128)(2,1)S(1)} %broadcast_in_dim.23), channel_id=1, replica_groups=mesh['zm'=2,'zn'=4,'core'=2,'y'=4,'zh'=2,'x'=4] {'y','x'}, dimensions={0} | all-to-all | bytes 1572864 | tf_op jit(solution)/shard_map/all_to_all | solution.py:39
  172.6 6.7 %collective-permute-start = (bf16[16,48,512]{2,1,0:T(8,128)(2,1)S(1)}, bf16[16,48,512]{2,1,0:T(8,128)(2,1)S(1)}, u32[]{:S(2)}, u32[]{:S(2)}) collective-permute-start(bf16[16,48,512]{2,1,0:T(8,128)(2,1)S(1)} %all_to_all.43), channel_id=1, source_target_pairs={{0,32},{32,0},{1,33},{33,1},{2,34},{34,2},{3,35},{35,3},{4,36},{36... | collective-permute-start | bytes 2359304 | tf_op jit(solution)/shard_map/ppermute | solution.py:43
  179.3 1.9 %collective-permute-done = bf16[16,48,512]{2,1,0:T(8,128)(2,1)S(1)} collective-permute-done((bf16[16,48,512]{2,1,0:T(8,128)(2,1)S(1)}, bf16[16,48,512]{2,1,0:T(8,128)(2,1)S(1)}, u32[]{:S(2)}, u32[]{:S(2)}) %collective-permute-start) | collective-permute-done | bytes 786464 | tf_op jit(solution)/shard_map/ppermute | solution.py:43
  181.2 0.1 select_bitcast_fusion.1
  181.3 0.6 convert_reduce_fusion
  181.9 1.1 maximum_convert_fusion.1
  183.0 0.2 maximum_convert_fusion
  183.3 1.3 slice.128
  (21 shorter events, 0.3 us)
Async XLA Ops:
  0.6 50.1 %copy-start = (bf16[768,512]{1,0:T(8,128)(2,1)S(1)}, bf16[768,512]{1,0:T(8,128)(2,1)}, u32[]{:S(2)}) copy-start(bf16[768,512]{1,0:T(8,128)(2,1)} %param.16) | copy-start | bytes 2359300
  4.5 11.4 %copy-start.3 = (bf16[16,1024]{1,0:T(8,128)(2,1)S(1)}, bf16[16,1024]{1,0:T(8,128)(2,1)}, u32[]{:S(2)}) copy-start(bf16[16,1024]{1,0:T(8,128)(2,1)} %param.15) | copy-start | bytes 98308
  4.5 11.7 %copy-start.4 = (bf16[16,512]{1,0:T(8,128)(2,1)S(1)}, bf16[16,512]{1,0:T(8,128)(2,1)}, u32[]{:S(2)}) copy-start(bf16[16,512]{1,0:T(8,128)(2,1)} %param.13) | copy-start | bytes 49156
  4.5 44.0 %copy-start.2 = (bf16[512,512]{1,0:T(8,128)(2,1)S(1)}, bf16[512,512]{1,0:T(8,128)(2,1)}, u32[]{:S(2)}) copy-start(bf16[512,512]{1,0:T(8,128)(2,1)} %param.17) | copy-start | bytes 1572868
  4.5 44.0 %all-to-all-start = ((bf16[32,16,1792]{2,1,0:T(8,128)(2,1)}), bf16[32,16,1792]{2,1,0:T(8,128)(2,1)}, u32[]{:S(2)}, u32[]{:S(2)}) async-start(bf16[32,16,1792]{2,1,0:T(8,128)(2,1)} %broadcast_in_dim.16), calls=%async_computation | async-start | bytes 3670016 | tf_op jit(solution)/shard_map/all_to_all | solution.py:39
  50.7 2.0 %copy-start.1 = (f32[512,256]{1,0:T(8,128)}, f32[512,256]{1,0:T(8,128)S(1)}, u32[]{:S(2)}) copy-start(f32[512,256]{1,0:T(8,128)S(1)} %get-tuple-element.72) | copy-start | bytes 1572868
  54.9 18.6 %all-to-all-start.2 = ((f32[16,6,128]{2,1,0:T(8,128)}), f32[16,6,128]{2,1,0:T(8,128)S(1)}, u32[]{:S(2)}, u32[]{:S(2)}) async-start(f32[16,6,128]{2,1,0:T(8,128)} %broadcast_in_dim.20), calls=%async_computation.2 | async-start | bytes 131072 | tf_op jit(solution)/shard_map/all_to_all | solution.py:39
  74.2 21.7 %all-to-all-start.1 = ((f32[32,12,128]{2,1,0:T(8,128)}), f32[32,12,128]{2,1,0:T(8,128)S(1)}, u32[]{:S(2)}, u32[]{:S(2)}) async-start(f32[32,12,128]{2,1,0:T(8,128)} %broadcast_in_dim.18), calls=%async_computation.1 | async-start | bytes 524288 | tf_op jit(solution)/shard_map/all_to_all | solution.py:39
  111.0 16.0 %all-to-all-start.4 = ((bf16[16,40,512]{2,1,0:T(8,128)(2,1)}), bf16[16,40,512]{2,1,0:T(8,128)(2,1)S(1)}, u32[]{:S(2)}, u32[]{:S(2)}) async-start(bf16[16,40,512]{2,1,0:T(8,128)(2,1)} %reduce_sum.236), calls=%async_computation.4 | async-start | bytes 1310720 | tf_op jit(solution)/shard_map/all_to_all | solution.py:123
  172.6 8.6 %collective-permute-start = (bf16[16,48,512]{2,1,0:T(8,128)(2,1)S(1)}, bf16[16,48,512]{2,1,0:T(8,128)(2,1)S(1)}, u32[]{:S(2)}, u32[]{:S(2)}) collective-permute-start(bf16[16,48,512]{2,1,0:T(8,128)(2,1)S(1)} %all_to_all.43), channel_id=1, source_target_pairs={{0,32},{32,0},{1,33},{33,1},{2,34},{34,2},{3,35},{35,3},{4,36},{36... | collective-permute-start | bytes 2359304 | tf_op jit(solution)/shard_map/ppermute | solution.py:43

commit v5 on v0

v5 whole, which is shorter than its diff:
```python
import functools

import jax
import jax.numpy as jnp
from jax import lax
from jax.experimental import pallas as pl
from jax.experimental.pallas import tpu as pltpu
from jax.sharding import Mesh
from jax.sharding import PartitionSpec as P

EPS = 1e-06
TEACHER_SCALE = 100.0
STUDENT_SCALE = 50.0

AXES = ("zm", "zn", "core", "y", "zh", "x")
SIZES = (2, 4, 2, 4, 2, 4)
PLANE = ("y", "x")
NEAR = ("zn",)
FAR = ("zh", "zm")
RING = FAR + NEAR
TILE = ("core", "y", "x")

BF16 = jnp.bfloat16
F32 = jnp.float32
LANES = 128
TALL = 96
CHUNK = 160
BOX = 176

NT = (((1,), (1,)), ((), ()))
TN = (((0,), (0,)), ((), ()))
PARAMS = pltpu.CompilerParams(vmem_limit_bytes=48 * 1024 * 1024)


def call(body, outs, *args, scalars=0):
    vmem = pl.BlockSpec(memory_space=pltpu.VMEM)
    smem = pl.BlockSpec(memory_space=pltpu.SMEM)
    specs = [smem] * scalars + [vmem] * (len(args) - scalars)
    shapes = [jax.ShapeDtypeStruct(s, t) for s, t in outs]
    return pl.pallas_call(
        body,
        out_shape=shapes,
        in_specs=specs,
        out_specs=[vmem] * len(outs),
        compiler_params=PARAMS,
    )(*args)


def dot(a, b, dims=(((1,), (0,)), ((), ()))):
    return lax.dot_general(a, b, dims, preferred_element_type=F32)


def normed(raw):
    x = raw.astype(F32)
    return (x * lax.rsqrt(jnp.sum(x * x, axis=1, keepdims=True) + EPS)).astype(BF16)


def pack_body(teach_img, feats_img, teach_txt, feats_txt, out_img, out_txt):
    width = teach_img.shape[1]
    q = normed(teach_img[...])
    f = feats_img[...]
    for k in range(out_img.shape[0]):
        out_img[k, :, :width] = q
        out_img[k, :, width:] = f
    out_txt[:, :width] = normed(teach_txt[...])
    out_txt[:, width:] = feats_txt[...]


def project(feats, weight):
    u = dot(feats, weight)
    inv = lax.rsqrt(jnp.sum(u * u, axis=1, keepdims=True) + EPS)
    return (u * inv, inv)


def lse(x, axis):
    top = jnp.max(x, axis, keepdims=True)
    return top + jnp.log(jnp.sum(jnp.exp(x - top), axis, keepdims=True))


def tile_body(width, img, txt, w_img, w_txt, row_out, col_out, tl_out, sl_out, e_img, e_txt, inv_img, inv_txt):
    ei, vi = project(img[:, width:], w_img[...])
    et, vt = project(txt[:, width:], w_txt[...])
    e_img[...] = ei
    inv_img[...] = vi
    e_txt[...] = et
    inv_txt[...] = vt
    tl = TEACHER_SCALE * dot(img[:, :width], txt[:, :width], NT)
    sl = STUDENT_SCALE * dot(ei.astype(BF16), et.astype(BF16), NT)
    tl_out[...] = tl
    sl_out[...] = sl
    es = jnp.exp(sl)
    row_t = lse(tl, 1)
    row_s = jnp.log(jnp.sum(es, 1, keepdims=True))
    col_t = lse(tl, 0)
    col_s = jnp.log(jnp.sum(es, 0, keepdims=True))
    rows, cols = tl.shape
    lane = lax.broadcasted_iota(jnp.int32, (rows, LANES), 1)
    turned = jnp.where(lane == 0, row_t, row_s).T
    row_out[0] = jnp.zeros((8, LANES), F32)
    for b in range(rows // LANES):
        row_out[0, 2 * b : 2 * b + 2, :] = turned[0:2, b * LANES : (b + 1) * LANES]
    rep = row_out[0]
    for k in range(1, row_out.shape[0]):
        row_out[k] = rep
    col_out[0] = jnp.zeros((8, LANES), F32)
    for b in range(cols // LANES):
        col_out[0, b : b + 1, :] = col_t[:, b * LANES : (b + 1) * LANES]
        col_out[0, 2 + b : 3 + b, :] = col_s[:, b * LANES : (b + 1) * LANES]
    rep = col_out[0]
    for k in range(1, col_out.shape[0]):
        col_out[k] = rep


def tangent(grad_rows, embeds, inverse):
    return (grad_rows - embeds * jnp.sum(embeds * grad_rows, 1, keepdims=True)) * inverse


def grad_body(
    width, core, row_all, col_all, tl, sl, e_img, e_txt, inv_img, inv_txt, img, txt, keep, send, loss, g, wi, wt
):
    rows, cols = tl.shape
    row_parts, col_parts = (row_all.shape[0], col_all.shape[0])
    row = lse(row_all[...], 0)[0]
    col = lse(col_all[...], 0)[0]
    sub = lax.broadcasted_iota(jnp.int32, (8, LANES), 0)
    row_term = jnp.where(sub % 2 == 1, row, -row)
    col_term = jnp.where(sub < 2, -col, jnp.where(sub < 4, col, 0.0))
    total = jnp.sum(row_term, keepdims=True) / row_parts + jnp.sum(col_term, keepdims=True) / col_parts
    down = row.T
    col_t = jnp.concatenate([col[0:1], col[1:2]], 1)
    col_s = jnp.concatenate([col[2:3], col[3:4]], 1)
    acc = jnp.zeros((LANES, cols), F32)
    for b in range(rows // LANES):
        at = pl.ds(b * LANES, LANES)
        t = tl[at, :]
        s = sl[at, :]
        pt_row = jnp.exp(t - down[:, 2 * b : 2 * b + 1])
        ps_row = jnp.exp(s - down[:, 2 * b + 1 : 2 * b + 2])
        pt_col = jnp.exp(t - col_t)
        ps_col = jnp.exp(s - col_s)
        acc = acc + (pt_row + pt_col) * (t - s)
        g[at, :] = (0.5 * STUDENT_SCALE * ((ps_row - pt_row) + (ps_col - pt_col))).astype(BF16)
    total = total + jnp.sum(acc, keepdims=True)
    loss[...] = jnp.broadcast_to(total, (8, LANES))
    ei = e_img[...]
    et = e_txt[...]
    gb = g[...]
    di = dot(gb, et.astype(BF16))
    dt = dot(gb, ei.astype(BF16), TN)
    wi[...] = dot(img[:, width:], tangent(di, ei, inv_img[...]).astype(BF16), TN).astype(BF16)
    wt[...] = dot(txt[:, width:], tangent(dt, et, inv_txt[...]).astype(BF16), TN).astype(BF16)
    hi, ht = (wi.shape[0] // 2, wt.shape[0] // 2)
    me = core[0]
    for out, who in ((keep, me), (send, 1 - me)):
        a = wi[pl.ds(pl.multiple_of(who * hi, hi), hi), :]
        b = wt[pl.ds(pl.multiple_of(who * ht, ht), ht), :]
        tall, low = (TALL, CHUNK - TALL)
        for p in range(out.shape[0]):
            i, j = divmod(p, 4)
            lanes = slice(j * LANES, (j + 1) * LANES)
            out[p, :tall, :] = a[i * tall : (i + 1) * tall, lanes]
            out[p, tall:, :] = b[i * low : (i + 1) * low, lanes]


def pair_body(a, b, out):
    out[...] = (a[...].astype(F32) + b[...].astype(F32)).astype(BF16)


def thirds(value):
    hi = value.astype(BF16).astype(F32)
    mid = (value - hi).astype(BF16).astype(F32)
    low = value - hi - mid
    lane = lax.broadcasted_iota(jnp.int32, value.shape, 1)
    split = jnp.where(lane == 0, hi, jnp.where(lane == 1, mid, jnp.where(lane == 2, low, 0.0)))
    return split.astype(BF16)


def fold_body(parts, *refs):
    out = refs[-1]
    whole = jnp.sum(parts[:, :CHUNK, :].astype(F32), 0).astype(BF16)
    if len(refs) > 1:
        value = jnp.concatenate([refs[0][...]] * 2, 0)
    else:
        terms = jnp.sum(parts[:, CHUNK:, :].astype(F32), 0)
        value = jnp.broadcast_to(jnp.sum(terms, 1, keepdims=True), (BOX - CHUNK, LANES))
    split = thirds(value)
    for k in range(out.shape[0]):
        out[k, :CHUNK, :] = whole
        out[k, CHUNK:, :] = split


def output_body(scale, core, own, other, loss, grad_img, grad_txt):
    hi, ht = (grad_img.shape[0] // 2, grad_txt.shape[0] // 2)
    me = core[0]
    tall, low = (TALL, CHUNK - TALL)
    sums = []
    for box, who in ((own, me), (other, 1 - me)):
        for p in range(box.shape[0]):
            i, j = divmod(p, 4)
            lanes = slice(j * LANES, (j + 1) * LANES)
            at = pl.multiple_of(who * hi + i * tall, 8)
            grad_img[pl.ds(at, tall), lanes] = box[p, :tall, :].astype(F32)
            at = pl.multiple_of(who * ht + i * low, 8)
            grad_txt[pl.ds(at, low), lanes] = box[p, tall:CHUNK, :].astype(F32)
        terms = jnp.sum(box[:, CHUNK:, :].astype(F32), 0)
        sums.append(jnp.sum(terms, 1, keepdims=True)[:8])
    loss[...] = jnp.broadcast_to((sums[0] + sums[1]) * scale, (8, LANES))


def exchange(copies, axes):
    return lax.all_to_all(copies, axes, 0, 0, tiled=True)


def swap_cores(block):
    return lax.ppermute(block, "core", [(0, 1), (1, 0)])


def shards(image_feats, text_feats, teacher_img, teacher_txt, proj_img, proj_txt):
    core = lax.axis_index("core").reshape(1)
    n_tile, n_ring, n_plane = (lax.axis_size(a) for a in (TILE, RING, PLANE))
    n_near, n_far = (lax.axis_size(a) for a in (NEAR, FAR))
    own, width = teacher_img.shape
    wide_i = width + image_feats.shape[1]
    wide_t = width + text_feats.shape[1]
    rows, cols = (own * n_tile, own * n_ring)
    depth = proj_img.shape[1]

    pack_img, pack_txt = call(
        pack_body,
        [((n_tile, own, wide_i), BF16), ((own, wide_t), BF16)],
        teacher_img,
        image_feats,
        teacher_txt,
        text_feats,
    )
    img = exchange(pack_img, TILE).reshape(rows, wide_i)
    txt = lax.all_gather(pack_txt, RING, axis=0, tiled=True)

    row_part, col_part, *kept = call(
        functools.partial(tile_body, width),
        [
            ((n_tile, 8, LANES), F32),
            ((n_ring, 8, LANES), F32),
            ((rows, cols), F32),
            ((rows, cols), F32),
            ((rows, depth), F32),
            ((cols, depth), F32),
            ((rows, 1), F32),
            ((cols, 1), F32),
        ],
        img,
        txt,
        proj_img,
        proj_txt,
    )
    row_all = exchange(row_part, TILE)
    col_all = exchange(col_part, RING)

    box = (n_plane, CHUNK, LANES)
    vmem = pl.BlockSpec(memory_space=pltpu.VMEM)
    keep, send, total = pl.pallas_call(
        functools.partial(grad_body, width),
        out_shape=[
            jax.ShapeDtypeStruct(box, BF16),
            jax.ShapeDtypeStruct(box, BF16),
            jax.ShapeDtypeStruct((8, LANES), F32),
        ],
        in_specs=[pl.BlockSpec(memory_space=pltpu.SMEM)] + [vmem] * 10,
        out_specs=[vmem] * 3,
        scratch_shapes=[
            pltpu.VMEM((rows, cols), BF16),
            pltpu.VMEM(proj_img.shape, BF16),
            pltpu.VMEM(proj_txt.shape, BF16),
        ],
        compiler_params=PARAMS,
    )(core, row_all, col_all, *kept, img, txt)

    (part,) = call(pair_body, [(box, BF16)], keep, swap_cores(send))
    part = exchange(part, PLANE)
    (part,) = call(fold_body, [((n_near, BOX, LANES), BF16)], part, total)
    part = exchange(part, NEAR)
    (part,) = call(fold_body, [((n_far, BOX, LANES), BF16)], part)
    part = exchange(part, FAR)
    (part,) = call(fold_body, [((n_plane, BOX, LANES), BF16)], part)
    mine = exchange(part, PLANE)
    other = swap_cores(mine)
    batch_total = own * lax.axis_size(AXES)
    loss, grad_img, grad_txt = call(
        functools.partial(output_body, 1.0 / (2.0 * batch_total)),
        [((8, LANES), F32), (proj_img.shape, F32), (proj_txt.shape, F32)],
        core,
        mine,
        other,
        scalars=1,
    )
    return (loss[0, 0], grad_img, grad_txt)


def solution(mesh):
    fine = Mesh(mesh.devices.reshape(SIZES), AXES)
    img = P(("zm", "zn", "core", "y", "zh", "x"), None)
    txt = P(("y", "zh", "x", "zm", "zn", "core"), None)
    return jax.shard_map(
        shards,
        mesh=fine,
        in_specs=(img, txt, img, txt, P(), P()),
        out_specs=(P(), P(), P()),
        check_vma=False,
    )
```

time: 1580 us -> 171 us (0.11)
  waiting for transfers between devices: 736 us -> 15.1 us
  blocking collectives: 792 us -> 108 us
  starting transfers between devices: 0.16 us -> 27.8 us
  between operations: 18.2 us -> 0.73 us
    psum x1 -> x0, waiting for transfers between devices: 369 us -> none  [shards(): lax.psum((local_img, local_txt, local_term), ('img', 'txt'))]
    reduce_scatter x2 -> x0, waiting for transfers between devices: 367 us -> none  [the longest x1 287 us: shards(): d_img = lax.psum_scatter(part_img, 'txt', scatter_dimension=0, tiled=True)]
    psum x4 -> x0, blocking collectives: 361 us -> none  [the longest x1 134 us: tile_terms(): lax.psum((jnp.sum(jnp.exp(tl - rtm[:, None]), 1), jnp.sum(jnp.exp(sl - rs...]
    all_gather x3 -> x1, blocking collectives: 240 us -> 32.8 us  [shards(): txt = lax.all_gather(pack_txt, RING, axis=0, tiled=True)]
    pmax x2 -> x0, blocking collectives: 191 us -> none  [the longest x1 133 us: tile_terms(): rtm, rsm = lax.pmax((tl.max(1), sl.max(1)), 'txt')]
    all_to_all x0 -> x5, blocking collectives: none -> 75.2 us  [exchange(): return lax.all_to_all(copies, axes, 0, 0, tiled=True)]
    all_to_all x0 -> x2, starting transfers between devices: none -> 17.8 us  [exchange(): return lax.all_to_all(copies, axes, 0, 0, tiled=True)]
  transfers between devices with their start and end apart: 4 -> 4, of which waited for: 3 -> 3; matrix products, arithmetic and copies ran while one was open for 1% -> 0% of each run, Pallas kernels for 0% -> 0%
where the time goes in v5:
time: 171 us; the launch traced here: 170 us
  blocking collectives  108 us (63%)
  starting transfers between devices  27.8 us (16%)
  waiting for transfers between devices  15.1 us (9%)
  Pallas kernels  9.93 us (6%)
  local copies, waits for them, and re-layouts  8.99 us (5%)
    all_to_all x5, blocking collectives, exchange(): return lax.all_to_all(copies, axes, 0, 0, tiled=True)  75.2 us
    all_gather x1, blocking collectives, shards(): txt = lax.all_gather(pack_txt, RING, axis=0, tiled=True)  32.8 us
    all_to_all x2, starting transfers between devices, exchange(): return lax.all_to_all(copies, axes, 0, 0, tiled=True)  17.8 us
    all_to_all x2, waiting for transfers between devices, exchange(): return lax.all_to_all(copies, axes, 0, 0, tiled=True)  11.6 us
    ppermute x2, starting transfers between devices, swap_cores(): return lax.ppermute(block, 'core', [(0, 1), (1, 0)])  10 us
    unnamed x26, local copies, waits for them, and re-layouts  8.48 us
    pallas_call x7, Pallas kernels, call(): pl.pallas_call(body, out_shape=shapes, in_specs=specs, out_specs=[vmem] *...  6.73 us
    ppermute x2, waiting for transfers between devices, swap_cores(): return lax.ppermute(block, 'core', [(0, 1), (1, 0)])  3.5 us
  transfers between devices with their start and end apart: 4, of which 3 were waited for; matrix products, arithmetic and copies ran while one was open for 0% of the time, Pallas kernels for 0%

profile of v5, /device:TPU:1, one launch (start us, length us, event | category | flops | bytes accessed | tf_op | source)
XLA Modules:
  0.0 170.5 jit_solution(604907429163977568)
XLA Ops:
  0.6 0.0 copy-start.9
  0.6 0.7 copy-done.9
  1.4 0.0 copy-start.10
  1.4 0.8 copy-done.10
  2.1 0.0 copy-start.11
  2.2 0.7 copy-done.11
  2.9 0.0 copy-start.12
  2.9 0.7 copy-done.12
  3.6 1.4 shard_map.85
  5.0 0.0 copy-start
  5.0 0.0 copy-start.1
  5.0 11.4 %all-to-all-start = ((bf16[32,16,1792]{2,1,0:T(8,128)(2,1)}), bf16[32,16,1792]{2,1,0:T(8,128)(2,1)}, u32[]{:S(2)}, u32[]{:S(2)}) async-start(bf16[32,16,1792]{2,1,0:T(8,128)(2,1)} %get-tuple-element.19), calls=%async_computation | async-start | bytes 3670016 | tf_op jit(solution)/shard_map/all_to_all | solution.py:211
  16.4 32.8 %all_gather.3.txt = bf16[256,1536]{1,0:T(8,128)(2,1)S(1)} all-gather(bf16[16,1536]{1,0:T(8,128)(2,1)S(1)} %get-tuple-element.20), channel_id=1, replica_groups=mesh['zm'=2,'zn'=4,'core'=2,'y'=4,'zh'=2,'x'=4] {'zh','zm','zn'}, dimensions={0}, use_global_device_ids=true | all-gather | bytes 835584 | tf_op jit(solution)/shard_map/all_gather | solution.py:237
  49.2 0.0 all-to-all-done
  49.2 0.0 copy-done
  49.2 0.0 copy-done.1
  49.2 3.1 %shard_map.86 = (f32[32,8,128]{2,1,0:T(8,128)S(1)}, f32[16,8,128]{2,1,0:T(8,128)S(1)}, f32[512,256]{1,0:T(8,128)S(1)}, f32[512,256]{1,0:T(8,128)S(1)}, f32[512,5...) custom-call(bf16[512,1792]{1,0:T(8,128)(2,1)} %bitcast.1.img, ...), custom_call_target="tpu_custom_call" | custom-call | tf_op jit(solution)/shard_map/pallas_call | solution.py:40
  52.4 0.0 copy-start.2
  52.4 0.8 copy-done.2
  53.2 0.0 copy-start.4
  53.2 0.8 copy-done.4
  53.9 0.0 copy-start.6
  53.9 0.8 copy-done.6
  54.7 0.0 copy-start.8
  54.8 19.3 %all_to_all.35.row_all = f32[32,8,128]{2,1,0:T(8,128)S(1)} all-to-all(f32[32,8,128]{2,1,0:T(8,128)S(1)} %get-tuple-element.21), channel_id=1, replica_groups=mesh['zm'=2,'zn'=4,'core'=2,'y'=4,'zh'=2,'x'=4] {'core','y','x'}, dimensions={0} | all-to-all | bytes 262144 | tf_op jit(solution)/shard_map/all_to_all | solution.py:211
  74.0 0.0 copy-done.8
  74.0 6.4 %all-to-all-start.2 = ((f32[16,8,128]{2,1,0:T(8,128)}), f32[16,8,128]{2,1,0:T(8,128)S(1)}, u32[]{:S(2)}, u32[]{:S(2)}) async-start(f32[16,8,128]{2,1,0:T(8,128)} %copy-done.8), calls=%async_computation.2 | async-start | bytes 131072 | tf_op jit(solution)/shard_map/all_to_all | solution.py:211
  80.4 11.6 %all-to-all-done.2.col_all = f32[16,8,128]{2,1,0:T(8,128)S(1)} async-done(((f32[16,8,128]{2,1,0:T(8,128)}), f32[16,8,128]{2,1,0:T(8,128)S(1)}, u32[]{:S(2)}, u32[]{:S(2)}) %all-to-all-start.2) | async-done | bytes 65568 | tf_op jit(solution)/shard_map/all_to_all | solution.py:211
  92.0 0.0 copy-start.3
  92.0 1.0 copy-done.3
  93.0 0.0 copy-start.5
  93.0 1.0 copy-done.5
  94.1 0.0 copy-start.7
  94.1 1.0 copy-done.7
  95.1 3.2 %shard_map.87 = (bf16[16,160,128]{2,1,0:T(8,128)(2,1)S(1)}, bf16[16,160,128]{2,1,0:T(8,128)(2,1)S(1)}, f32[8,128]{1,0:T(8,128)S(1)}) custom-call(s32[1]{0:T(128)} %bitcast.core, f32[32,8,128]{2,1,0:T(8,128)S(1)} %all_to_all.35.row_all, f32[16,8,128]{2,1,0:T(8,128)S(1)} %all-to-all-done.2.col_all, f32[512,256]{1,0:T(8,128)S(1)} %copy-done.3, ...), custom_call_target="tpu_custom_call" | custom-call | tf_op jit(solution)/shard_map/pallas_call | solution.py:261
  98.3 4.1 %collective-permute-start = (bf16[16,160,128]{2,1,0:T(8,128)(2,1)S(1)}, bf16[16,160,128]{2,1,0:T(8,128)(2,1)S(1)}, u32[]{:S(2)}, u32[]{:S(2)}) collective-permute-start(bf16[16,160,128]{2,1,0:T(8,128)(2,1)S(1)} %get-tuple-element.30), channel_id=1, source_target_pairs={{0,32},{32,0},{1,33},{33,1},{2,34},{34,2},{3,35},{35,3},{4,36},{36... | collective-permute-start | bytes 1966088 | tf_op jit(solution)/shard_map/ppermute | solution.py:215
  102.4 1.7 collective-permute-done.b
  104.1 0.2 shard_map.88
  104.3 15.4 %all_to_all.36.parts = bf16[16,160,128]{2,1,0:T(8,128)(2,1)S(1)} all-to-all(bf16[16,160,128]{2,1,0:T(8,128)(2,1)S(1)} %shard_map.88), channel_id=1, replica_groups=mesh['zm'=2,'zn'=4,'core'=2,'y'=4,'zh'=2,'x'=4] {'y','x'}, dimensions={0} | all-to-all | bytes 1310720 | tf_op jit(solution)/shard_map/all_to_all | solution.py:211
  119.6 0.1 shard_map.89
  119.7 8.0 %all_to_all.37.parts = bf16[4,176,128]{2,1,0:T(8,128)(2,1)S(1)} all-to-all(bf16[4,176,128]{2,1,0:T(8,128)(2,1)S(1)} %shard_map.89), channel_id=1, replica_groups=mesh['zm'=2,'zn'=4,'core'=2,'y'=4,'zh'=2,'x'=4] {'zn'}, dimensions={0} | all-to-all | bytes 360448 | tf_op jit(solution)/shard_map/all_to_all | solution.py:211
  127.7 0.1 shard_map.90
  127.8 16.7 %all_to_all.38.parts = bf16[4,176,128]{2,1,0:T(8,128)(2,1)S(1)} all-to-all(bf16[4,176,128]{2,1,0:T(8,128)(2,1)S(1)} %shard_map.90), channel_id=1, replica_groups=mesh['zm'=2,'zn'=4,'core'=2,'y'=4,'zh'=2,'x'=4] {'zh','zm'}, dimensions={0} | all-to-all | bytes 360448 | tf_op jit(solution)/shard_map/all_to_all | solution.py:211
  144.5 0.1 shard_map.91
  144.6 15.9 %all_to_all.39.own = bf16[16,176,128]{2,1,0:T(8,128)(2,1)S(1)} all-to-all(bf16[16,176,128]{2,1,0:T(8,128)(2,1)S(1)} %shard_map.91), channel_id=1, replica_groups=mesh['zm'=2,'zn'=4,'core'=2,'y'=4,'zh'=2,'x'=4] {'y','x'}, dimensions={0} | all-to-all | bytes 1441792 | tf_op jit(solution)/shard_map/all_to_all | solution.py:211
  160.4 6.0 %collective-permute-start.1 = (bf16[16,176,128]{2,1,0:T(8,128)(2,1)S(1)}, bf16[16,176,128]{2,1,0:T(8,128)(2,1)S(1)}, u32[]{:S(2)}, u32[]{:S(2)}) collective-permute-start(bf16[16,176,128]{2,1,0:T(8,128)(2,1)S(1)} %all_to_all.39.own), channel_id=1, source_target_pairs={{0,32},{32,0},{1,33},{33,1},{2,34},{34,2},{3,35},{35,3},{4,36},{36... | collective-permute-start | bytes 2162696 | tf_op jit(solution)/shard_map/ppermute | solution.py:215
  166.4 1.8 %collective-permute-done.1.other = bf16[16,176,128]{2,1,0:T(8,128)(2,1)S(1)} collective-permute-done((bf16[16,176,128]{2,1,0:T(8,128)(2,1)S(1)}, bf16[16,176,128]{2,1,0:T(8,128)(2,1)S(1)}, u32[]{:S(2)}, u32[]{:S(2)}) %collective-permute-start.1) | collective-permute-done | bytes 720928 | tf_op jit(solution)/shard_map/ppermute | solution.py:215
  168.2 1.8 %shard_map.92 = (f32[8,128]{1,0:T(8,128)S(1)}, f32[768,512]{1,0:T(8,128)}, f32[512,512]{1,0:T(8,128)}) custom-call(s32[1]{0:T(128)} %bitcast.core, bf16[16,176,128]{2,1,0:T(8,128)(2,1)S(1)} %all_to_all.39.own, bf16[16,176,128]{2,1,0:T(8,128)(2,1)S(1)} %collective-permute-done.1.other), custom_call_target="tpu_custom_call" | custom-call | tf_op jit(solution)/shard_map/pallas_call | solution.py:40
  170.0 0.5 slice.3
Async XLA Ops:
  0.6 0.8 copy-start.9
  1.4 0.8 copy-start.10
  2.1 0.7 copy-start.11
  2.9 0.7 copy-start.12
  5.0 44.2 %copy-start = (bf16[768,512]{1,0:T(8,128)(2,1)S(1)}, bf16[768,512]{1,0:T(8,128)(2,1)}, u32[]{:S(2)}) copy-start(bf16[768,512]{1,0:T(8,128)(2,1)} %w_img.1) | copy-start | bytes 2359300
  5.0 44.2 %copy-start.1 = (bf16[512,512]{1,0:T(8,128)(2,1)S(1)}, bf16[512,512]{1,0:T(8,128)(2,1)}, u32[]{:S(2)}) copy-start(bf16[512,512]{1,0:T(8,128)(2,1)} %w_txt.1) | copy-start | bytes 1572868
  5.0 44.2 %all-to-all-start = ((bf16[32,16,1792]{2,1,0:T(8,128)(2,1)}), bf16[32,16,1792]{2,1,0:T(8,128)(2,1)}, u32[]{:S(2)}, u32[]{:S(2)}) async-start(bf16[32,16,1792]{2,1,0:T(8,128)(2,1)} %get-tuple-element.19), calls=%async_computation | async-start | bytes 3670016 | tf_op jit(solution)/shard_map/all_to_all | solution.py:211
  52.4 0.8 copy-start.2
  53.2 0.8 copy-start.4
  53.9 0.8 copy-start.6
  54.7 19.3 %copy-start.8 = (f32[16,8,128]{2,1,0:T(8,128)}, f32[16,8,128]{2,1,0:T(8,128)S(1)}, u32[]{:S(2)}) copy-start(f32[16,8,128]{2,1,0:T(8,128)S(1)} %get-tuple-element.22) | copy-start | bytes 196612
  74.0 17.9 %all-to-all-start.2 = ((f32[16,8,128]{2,1,0:T(8,128)}), f32[16,8,128]{2,1,0:T(8,128)S(1)}, u32[]{:S(2)}, u32[]{:S(2)}) async-start(f32[16,8,128]{2,1,0:T(8,128)} %copy-done.8), calls=%async_computation.2 | async-start | bytes 131072 | tf_op jit(solution)/shard_map/all_to_all | solution.py:211
  92.0 1.0 copy-start.3
  93.0 1.0 copy-start.5
  94.1 1.0 copy-start.7
  98.3 5.8 %collective-permute-start = (bf16[16,160,128]{2,1,0:T(8,128)(2,1)S(1)}, bf16[16,160,128]{2,1,0:T(8,128)(2,1)S(1)}, u32[]{:S(2)}, u32[]{:S(2)}) collective-permute-start(bf16[16,160,128]{2,1,0:T(8,128)(2,1)S(1)} %get-tuple-element.30), channel_id=1, source_target_pairs={{0,32},{32,0},{1,33},{33,1},{2,34},{34,2},{3,35},{35,3},{4,36},{36... | collective-permute-start | bytes 1966088 | tf_op jit(solution)/shard_map/ppermute | solution.py:215
  160.4 7.8 %collective-permute-start.1 = (bf16[16,176,128]{2,1,0:T(8,128)(2,1)S(1)}, bf16[16,176,128]{2,1,0:T(8,128)(2,1)S(1)}, u32[]{:S(2)}, u32[]{:S(2)}) collective-permute-start(bf16[16,176,128]{2,1,0:T(8,128)(2,1)S(1)} %all_to_all.39.own), channel_id=1, source_target_pairs={{0,32},{32,0},{1,33},{33,1},{2,34},{34,2},{3,35},{35,3},{4,36},{36... | collective-permute-start | bytes 2162696 | tf_op jit(solution)/shard_map/ppermute | solution.py:215

commit v6 on v5

--- a/solution.py
+++ b/solution.py
@@ -29,10 +29,13 @@
 
 NT = (((1,), (1,)), ((), ()))
 TN = (((0,), (0,)), ((), ()))
-PARAMS = pltpu.CompilerParams(vmem_limit_bytes=48 * 1024 * 1024)
-
-
-def call(body, outs, *args, scalars=0):
+
+
+def room(mib):
+    return pltpu.CompilerParams(vmem_limit_bytes=mib * 1024 * 1024)
+
+
+def call(body, mib, outs, *args, scalars=0):
     vmem = pl.BlockSpec(memory_space=pltpu.VMEM)
     smem = pl.BlockSpec(memory_space=pltpu.SMEM)
     specs = [smem] * scalars + [vmem] * (len(args) - scalars)
@@ -42,8 +45,24 @@
         out_shape=shapes,
         in_specs=specs,
         out_specs=[vmem] * len(outs),
-        compiler_params=PARAMS,
+        compiler_params=room(mib),
     )(*args)
+
+
+def fetch(sources, held, sems):
+    copies = [pltpu.make_async_copy(a, b, sems.at[k]) for k, (a, b) in enumerate(zip(sources, held))]
+    for c in copies:
+        c.start()
+    return copies
+
+
+def pinned(array):
+    return pltpu.with_memory_space_constraint(array, pltpu.HBM)
+
+
+HBM = pl.BlockSpec(memory_space=pltpu.HBM)
+VMEM = pl.BlockSpec(memory_space=pltpu.VMEM)
+SMEM = pl.BlockSpec(memory_space=pltpu.SMEM)
 
 
 def dot(a, b, dims=(((1,), (0,)), ((), ()))):
@@ -55,21 +74,31 @@
     return (x * lax.rsqrt(jnp.sum(x * x, axis=1, keepdims=True) + EPS)).astype(BF16)
 
 
-def pack_body(teach_img, feats_img, teach_txt, feats_txt, out_img, out_txt):
+def pack_body(*refs):
+    ins, (out_img, out_txt), held = refs[:4], refs[4:6], refs[6:10]
+    row_img, row_txt, in_sems, out_sems = refs[10:]
+    copies = fetch(ins, held, in_sems)
+    teach_img, feats_img, teach_txt, feats_txt = held
     width = teach_img.shape[1]
-    q = normed(teach_img[...])
-    f = feats_img[...]
-    for k in range(out_img.shape[0]):
-        out_img[k, :, :width] = q
-        out_img[k, :, width:] = f
-    out_txt[:, :width] = normed(teach_txt[...])
-    out_txt[:, width:] = feats_txt[...]
-
-
-def project(feats, weight):
-    u = dot(feats, weight)
-    inv = lax.rsqrt(jnp.sum(u * u, axis=1, keepdims=True) + EPS)
-    return (u * inv, inv)
+    copies[0].wait()
+    copies[1].wait()
+    row_img[:, :width] = normed(teach_img[...])
+    row_img[:, width:] = feats_img[...]
+    peers = out_img.shape[0]
+    sent = fetch([row_img] * peers, [out_img.at[k] for k in range(peers)], out_sems)
+    copies[2].wait()
+    copies[3].wait()
+    row_txt[:, :width] = normed(teach_txt[...])
+    row_txt[:, width:] = feats_txt[...]
+    last = pltpu.make_async_copy(row_txt, out_txt, in_sems.at[0])
+    last.start()
+    for c in sent:
+        c.wait()
+    last.wait()
+
+
+def scale_of(u):
+    return lax.rsqrt(jnp.sum(u * u, axis=1, keepdims=True) + EPS)
 
 
 def lse(x, axis):
@@ -77,23 +106,37 @@
     return top + jnp.log(jnp.sum(jnp.exp(x - top), axis, keepdims=True))
 
 
-def tile_body(width, img, txt, w_img, w_txt, row_out, col_out, tl_out, sl_out, e_img, e_txt, inv_img, inv_txt):
-    ei, vi = project(img[:, width:], w_img[...])
-    et, vt = project(txt[:, width:], w_txt[...])
-    e_img[...] = ei
-    inv_img[...] = vi
-    e_txt[...] = et
-    inv_txt[...] = vt
-    tl = TEACHER_SCALE * dot(img[:, :width], txt[:, :width], NT)
-    sl = STUDENT_SCALE * dot(ei.astype(BF16), et.astype(BF16), NT)
-    tl_out[...] = tl
-    sl_out[...] = sl
+def tile_body(width, img, txt, *refs):
+    ins, (row_out, col_out), outs = refs[:2], refs[2:4], refs[4:10]
+    w_img, w_txt = refs[10:12]
+    made = refs[12:16]
+    in_sems, out_sems = refs[16:]
+    copies = fetch(ins, (w_img, w_txt), in_sems)
+    tl_own, sl_own, u_img, u_txt = made
+    sources = list(made) + [img.at[:, width:], txt.at[:, width:]]
+    back = [pltpu.make_async_copy(sources[k], outs[k], out_sems.at[k]) for k in range(6)]
+    back[4].start()
+    back[5].start()
+    tl_own[...] = TEACHER_SCALE * dot(img[:, :width], txt[:, :width], NT)
+    back[0].start()
+    copies[0].wait()
+    u_img[...] = dot(img[:, width:], w_img[...])
+    back[2].start()
+    copies[1].wait()
+    u_txt[...] = dot(txt[:, width:], w_txt[...])
+    back[3].start()
+    ui = u_img[...]
+    ut = u_txt[...]
+    ei = (ui * scale_of(ui)).astype(BF16)
+    et = (ut * scale_of(ut)).astype(BF16)
+    sl_own[...] = STUDENT_SCALE * dot(ei, et, NT)
+    back[1].start()
+    tl = tl_own[...]
+    sl = sl_own[...]
     es = jnp.exp(sl)
+    rows, cols = tl.shape
     row_t = lse(tl, 1)
     row_s = jnp.log(jnp.sum(es, 1, keepdims=True))
-    col_t = lse(tl, 0)
-    col_s = jnp.log(jnp.sum(es, 0, keepdims=True))
-    rows, cols = tl.shape
     lane = lax.broadcasted_iota(jnp.int32, (rows, LANES), 1)
     turned = jnp.where(lane == 0, row_t, row_s).T
     row_out[0] = jnp.zeros((8, LANES), F32)
@@ -102,6 +145,8 @@
     rep = row_out[0]
     for k in range(1, row_out.shape[0]):
         row_out[k] = rep
+    col_t = lse(tl, 0)
+    col_s = jnp.log(jnp.sum(es, 0, keepdims=True))
     col_out[0] = jnp.zeros((8, LANES), F32)
     for b in range(cols // LANES):
         col_out[0, b : b + 1, :] = col_t[:, b * LANES : (b + 1) * LANES]
@@ -109,15 +154,18 @@
     rep = col_out[0]
     for k in range(1, col_out.shape[0]):
         col_out[k] = rep
+    for c in back:
+        c.wait()
 
 
 def tangent(grad_rows, embeds, inverse):
     return (grad_rows - embeds * jnp.sum(embeds * grad_rows, 1, keepdims=True)) * inverse
 
 
-def grad_body(
-    width, core, row_all, col_all, tl, sl, e_img, e_txt, inv_img, inv_txt, img, txt, keep, send, loss, g, wi, wt
-):
+def grad_body(core, row_all, col_all, *refs):
+    ins, (keep, send, loss), held, (g, wi, wt, sems) = refs[:6], refs[6:9], refs[9:15], refs[15:]
+    copies = fetch(ins, held, sems)
+    tl, sl, u_img, u_txt, feats_img, feats_txt = held
     rows, cols = tl.shape
     row_parts, col_parts = (row_all.shape[0], col_all.shape[0])
     row = lse(row_all[...], 0)[0]
@@ -130,6 +178,8 @@
     col_t = jnp.concatenate([col[0:1], col[1:2]], 1)
     col_s = jnp.concatenate([col[2:3], col[3:4]], 1)
     acc = jnp.zeros((LANES, cols), F32)
+    copies[0].wait()
+    copies[1].wait()
     for b in range(rows // LANES):
         at = pl.ds(b * LANES, LANES)
         t = tl[at, :]
@@ -142,13 +192,19 @@
         g[at, :] = (0.5 * STUDENT_SCALE * ((ps_row - pt_row) + (ps_col - pt_col))).astype(BF16)
     total = total + jnp.sum(acc, keepdims=True)
     loss[...] = jnp.broadcast_to(total, (8, LANES))
-    ei = e_img[...]
-    et = e_txt[...]
+    for c in copies[2:]:
+        c.wait()
+    ui = u_img[...]
+    ut = u_txt[...]
+    inv_img = scale_of(ui)
+    inv_txt = scale_of(ut)
+    ei = ui * inv_img
+    et = ut * inv_txt
     gb = g[...]
     di = dot(gb, et.astype(BF16))
     dt = dot(gb, ei.astype(BF16), TN)
-    wi[...] = dot(img[:, width:], tangent(di, ei, inv_img[...]).astype(BF16), TN).astype(BF16)
-    wt[...] = dot(txt[:, width:], tangent(dt, et, inv_txt[...]).astype(BF16), TN).astype(BF16)
+    wi[...] = dot(feats_img[...], tangent(di, ei, inv_img).astype(BF16), TN).astype(BF16)
+    wt[...] = dot(feats_txt[...], tangent(dt, et, inv_txt).astype(BF16), TN).astype(BF16)
     hi, ht = (wi.shape[0] // 2, wt.shape[0] // 2)
     me = core[0]
     for out, who in ((keep, me), (send, 1 - me)):
@@ -203,8 +259,8 @@
             at = pl.multiple_of(who * ht + i * low, 8)
             grad_txt[pl.ds(at, low), lanes] = box[p, tall:CHUNK, :].astype(F32)
         terms = jnp.sum(box[:, CHUNK:, :].astype(F32), 0)
-        sums.append(jnp.sum(terms, 1, keepdims=True)[:8])
-    loss[...] = jnp.broadcast_to((sums[0] + sums[1]) * scale, (8, LANES))
+        sums.append(jnp.sum(terms[:1], keepdims=True))
+    loss[...] = (sums[0] + sums[1]) * scale
 
 
 def exchange(copies, axes):
@@ -225,75 +281,83 @@
     rows, cols = (own * n_tile, own * n_ring)
     depth = proj_img.shape[1]
 
-    pack_img, pack_txt = call(
+    raw = (teacher_img, image_feats, teacher_txt, text_feats)
+    pack_img, pack_txt = pl.pallas_call(
         pack_body,
-        [((n_tile, own, wide_i), BF16), ((own, wide_t), BF16)],
-        teacher_img,
-        image_feats,
-        teacher_txt,
-        text_feats,
-    )
+        out_shape=[pltpu.HBM((n_tile, own, wide_i), BF16), pltpu.HBM((own, wide_t), BF16)],
+        in_specs=[HBM] * 4,
+        out_specs=[HBM] * 2,
+        scratch_shapes=[pltpu.VMEM(a.shape, a.dtype) for a in raw]
+        + [
+            pltpu.VMEM((own, wide_i), BF16),
+            pltpu.VMEM((own, wide_t), BF16),
+            pltpu.SemaphoreType.DMA((4,)),
+            pltpu.SemaphoreType.DMA((n_tile,)),
+        ],
+        compiler_params=room(8),
+    )(*[pinned(a) for a in raw])
     img = exchange(pack_img, TILE).reshape(rows, wide_i)
     txt = lax.all_gather(pack_txt, RING, axis=0, tiled=True)
 
-    row_part, col_part, *kept = call(
+    blocks = [(rows, cols), (rows, cols), (rows, depth), (cols, depth)]
+    feats = [(rows, proj_img.shape[0]), (cols, proj_txt.shape[0])]
+    row_part, col_part, *kept = pl.pallas_call(
         functools.partial(tile_body, width),
-        [
-            ((n_tile, 8, LANES), F32),
-            ((n_ring, 8, LANES), F32),
-            ((rows, cols), F32),
-            ((rows, cols), F32),
-            ((rows, depth), F32),
-            ((cols, depth), F32),
-            ((rows, 1), F32),
-            ((cols, 1), F32),
-        ],
-        img,
-        txt,
-        proj_img,
-        proj_txt,
-    )
+        out_shape=[jax.ShapeDtypeStruct((n, 8, LANES), F32) for n in (n_tile, n_ring)]
+        + [pltpu.HBM(b, F32) for b in blocks]
+        + [pltpu.HBM(b, BF16) for b in feats],
+        in_specs=[VMEM] * 2 + [HBM] * 2,
+        out_specs=[VMEM] * 2 + [HBM] * 6,
+        scratch_shapes=[pltpu.VMEM(a.shape, BF16) for a in (proj_img, proj_txt)]
+        + [pltpu.VMEM(b, F32) for b in blocks]
+        + [pltpu.SemaphoreType.DMA((n,)) for n in (2, 6)],
+        compiler_params=room(24),
+    )(img, txt, pinned(proj_img), pinned(proj_txt))
     row_all = exchange(row_part, TILE)
     col_all = exchange(col_part, RING)
 
     box = (n_plane, CHUNK, LANES)
-    vmem = pl.BlockSpec(memory_space=pltpu.VMEM)
     keep, send, total = pl.pallas_call(
-        functools.partial(grad_body, width),
+        grad_body,
         out_shape=[
             jax.ShapeDtypeStruct(box, BF16),
             jax.ShapeDtypeStruct(box, BF16),
             jax.ShapeDtypeStruct((8, LANES), F32),
         ],
-        in_specs=[pl.BlockSpec(memory_space=pltpu.SMEM)] + [vmem] * 10,
-        out_specs=[vmem] * 3,
-        scratch_shapes=[
+        in_specs=[SMEM, VMEM, VMEM] + [HBM] * 6,
+        out_specs=[VMEM] * 3,
+        scratch_shapes=[pltpu.VMEM(b, F32) for b in blocks]
+        + [
+            pltpu.VMEM(feats[0], BF16),
+            pltpu.VMEM(feats[1], BF16),
             pltpu.VMEM((rows, cols), BF16),
             pltpu.VMEM(proj_img.shape, BF16),
             pltpu.VMEM(proj_txt.shape, BF16),
+            pltpu.SemaphoreType.DMA((6,)),
         ],
-        compiler_params=PARAMS,
-    )(core, row_all, col_all, *kept, img, txt)
-
-    (part,) = call(pair_body, [(box, BF16)], keep, swap_cores(send))
+        compiler_params=room(24),
+    )(core, row_all, col_all, *[pinned(k) for k in kept])
+
+    (part,) = call(pair_body, 8, [(box, BF16)], keep, swap_cores(send))
     part = exchange(part, PLANE)
-    (part,) = call(fold_body, [((n_near, BOX, LANES), BF16)], part, total)
+    (part,) = call(fold_body, 8, [((n_near, BOX, LANES), BF16)], part, total)
     part = exchange(part, NEAR)
-    (part,) = call(fold_body, [((n_far, BOX, LANES), BF16)], part)
+    (part,) = call(fold_body, 8, [((n_far, BOX, LANES), BF16)], part)
     part = exchange(part, FAR)
-    (part,) = call(fold_body, [((n_plane, BOX, LANES), BF16)], part)
+    (part,) = call(fold_body, 8, [((n_plane, BOX, LANES), BF16)], part)
     mine = exchange(part, PLANE)
     other = swap_cores(mine)
     batch_total = own * lax.axis_size(AXES)
     loss, grad_img, grad_txt = call(
         functools.partial(output_body, 1.0 / (2.0 * batch_total)),
-        [((8, LANES), F32), (proj_img.shape, F32), (proj_txt.shape, F32)],
+        10,
+        [((1, 1), F32), (proj_img.shape, F32), (proj_txt.shape, F32)],
         core,
         mine,
         other,
         scalars=1,
     )
-    return (loss[0, 0], grad_img, grad_txt)
+    return (loss.reshape(()), grad_img, grad_txt)
 
 
 def solution(mesh):

time: 171 us -> 165 us (0.965)
  local copies, waits for them, and re-layouts: 8.99 us -> 0.01 us
  Pallas kernels: 9.93 us -> 12.9 us
    unnamed x26 -> x2, local copies, waits for them, and re-layouts: 8.48 us -> 0.01 us
    pallas_call x1 -> x3, Pallas kernels: 3.2 us -> 10.7 us  [the longest x1 4.88 us: shards(): pl.pallas_call(functools.partial(tile_body, width), out_shape=[jax.ShapeD...]
    pallas_call x7 -> x5, Pallas kernels: 6.73 us -> 2.2 us  [call(): pl.pallas_call(body, out_shape=shapes, in_specs=specs, out_specs=[vmem] *...]
where the time goes in v6:
time: 165 us; the launch traced here: 164 us
  blocking collectives  108 us (65%)
  starting transfers between devices  27.2 us (16%)
  waiting for transfers between devices  15.1 us (9%)
  Pallas kernels  12.9 us (8%)
    all_to_all x5, blocking collectives, exchange(): return lax.all_to_all(copies, axes, 0, 0, tiled=True)  76 us
    all_gather x1, blocking collectives, shards(): txt = lax.all_gather(pack_txt, RING, axis=0, tiled=True)  32.5 us
    all_to_all x2, starting transfers between devices, exchange(): return lax.all_to_all(copies, axes, 0, 0, tiled=True)  17.2 us
    all_to_all x2, waiting for transfers between devices, exchange(): return lax.all_to_all(copies, axes, 0, 0, tiled=True)  11.6 us
    ppermute x2, starting transfers between devices, swap_cores(): return lax.ppermute(block, 'core', [(0, 1), (1, 0)])  10 us
    pallas_call x1, Pallas kernels, shards(): pl.pallas_call(functools.partial(tile_body, width), out_shape=[jax.ShapeD...  4.88 us
    ppermute x2, waiting for transfers between devices, swap_cores(): return lax.ppermute(block, 'core', [(0, 1), (1, 0)])  3.5 us
    pallas_call x1, Pallas kernels, shards(): pl.pallas_call(grad_body, out_shape=[jax.ShapeDtypeStruct(box, BF16), jax...  3.36 us
  transfers between devices with their start and end apart: 4, of which 3 were waited for; matrix products, arithmetic and copies ran while one was open for 0% of the time, Pallas kernels for 0%

profile of v6, /device:TPU:1, one launch (start us, length us, event | category | flops | bytes accessed | tf_op | source)
XLA Modules:
  0.0 164.4 jit_solution(14562025672249127520)
XLA Ops:
  0.6 2.4 %shard_map.85 = (bf16[32,16,1792]{2,1,0:T(8,128)(2,1)}, bf16[16,1536]{1,0:T(8,128)(2,1)}) custom-call(bf16[16,1024]{1,0:T(8,128)(2,1)} %refs_0_.2, bf16[16,768]{1,0:T(8,128)(2,1)} %refs_1_.2, bf16[16,1024]{1,0:T(8,128)(2,1)} %refs_2_.1, bf16[16,512]{1,0:T(8,128)(2,1)} %refs_3_.1), custom_call_target="tpu_custom_call" | custom-call | tf_op jit(solution)/shard_map/pallas_call | solution.py:285
  3.1 0.0 copy-start
  3.1 10.8 %all-to-all-start = ((bf16[32,16,1792]{2,1,0:T(8,128)(2,1)}), bf16[32,16,1792]{2,1,0:T(8,128)(2,1)S(1)}, u32[]{:S(2)}, u32[]{:S(2)}) async-start(bf16[32,16,1792]{2,1,0:T(8,128)(2,1)} %get-tuple-element.19), calls=%async_computation | async-start | bytes 3670016 | tf_op jit(solution)/shard_map/all_to_all | solution.py:267
  13.9 0.0 copy-done
  13.9 32.5 %all_gather.3.txt = bf16[256,1536]{1,0:T(8,128)(2,1)S(1)} all-gather(bf16[16,1536]{1,0:T(8,128)(2,1)S(1)} %copy-done), channel_id=1, replica_groups=mesh['zm'=2,'zn'=4,'core'=2,'y'=4,'zh'=2,'x'=4] {'zh','zm','zn'}, dimensions={0}, use_global_device_ids=true | all-gather | bytes 835584 | tf_op jit(solution)/shard_map/all_gather | solution.py:300
  46.4 0.0 all-to-all-done
  46.4 4.9 %shard_map.86 = (f32[32,8,128]{2,1,0:T(8,128)S(1)}, f32[16,8,128]{2,1,0:T(8,128)}, f32[512,256]{1,0:T(8,128)}, f32[512,256]{1,0:T(8,128)}, f32[512,512]{1,0:T(8,...) custom-call(bf16[512,1792]{1,0:T(8,128)(2,1)S(1)} %bitcast.3, ...), custom_call_target="tpu_custom_call" | custom-call | tf_op jit(solution)/shard_map/pallas_call | solution.py:304
  51.3 20.1 %all_to_all.35.row_all = f32[32,8,128]{2,1,0:T(8,128)S(1)} all-to-all(f32[32,8,128]{2,1,0:T(8,128)S(1)} %get-tuple-element.21), channel_id=1, replica_groups=mesh['zm'=2,'zn'=4,'core'=2,'y'=4,'zh'=2,'x'=4] {'core','y','x'}, dimensions={0} | all-to-all | bytes 262144 | tf_op jit(solution)/shard_map/all_to_all | solution.py:267
  71.4 6.4 %all-to-all-start.2 = ((f32[16,8,128]{2,1,0:T(8,128)}), f32[16,8,128]{2,1,0:T(8,128)S(1)}, u32[]{:S(2)}, u32[]{:S(2)}) async-start(f32[16,8,128]{2,1,0:T(8,128)} %get-tuple-element.22), calls=%async_computation.2 | async-start | bytes 131072 | tf_op jit(solution)/shard_map/all_to_all | solution.py:267
  77.8 11.6 %all-to-all-done.2.col_all = f32[16,8,128]{2,1,0:T(8,128)S(1)} async-done(((f32[16,8,128]{2,1,0:T(8,128)}), f32[16,8,128]{2,1,0:T(8,128)S(1)}, u32[]{:S(2)}, u32[]{:S(2)}) %all-to-all-start.2) | async-done | bytes 65568 | tf_op jit(solution)/shard_map/all_to_all | solution.py:267
  89.4 3.4 %shard_map.87 = (bf16[16,160,128]{2,1,0:T(8,128)(2,1)S(1)}, bf16[16,160,128]{2,1,0:T(8,128)(2,1)S(1)}, f32[8,128]{1,0:T(8,128)S(1)}) custom-call(s32[1]{0:T(128)} %bitcast.core, f32[32,8,128]{2,1,0:T(8,128)S(1)} %all_to_all.35.row_all, f32[16,8,128]{2,1,0:T(8,128)S(1)} %all-to-all-done.2.col_all, f32[512,256]{1,0:T(8,128)} %get-tuple-element.23.refs_0_, ...), custom_call_target="tpu_custom_call" | custom-call | tf_op jit(solution)/shard_map/pallas_call | solution.py:320
  92.8 4.1 %collective-permute-start = (bf16[16,160,128]{2,1,0:T(8,128)(2,1)S(1)}, bf16[16,160,128]{2,1,0:T(8,128)(2,1)S(1)}, u32[]{:S(2)}, u32[]{:S(2)}) collective-permute-start(bf16[16,160,128]{2,1,0:T(8,128)(2,1)S(1)} %get-tuple-element.30), channel_id=1, source_target_pairs={{0,32},{32,0},{1,33},{33,1},{2,34},{34,2},{3,35},{35,3},{4,36},{36... | collective-permute-start | bytes 1966088 | tf_op jit(solution)/shard_map/ppermute | solution.py:271
  96.8 1.7 %collective-permute-done.b = bf16[16,160,128]{2,1,0:T(8,128)(2,1)S(1)} collective-permute-done((bf16[16,160,128]{2,1,0:T(8,128)(2,1)S(1)}, bf16[16,160,128]{2,1,0:T(8,128)(2,1)S(1)}, u32[]{:S(2)}, u32[]{:S(2)}) %collective-permute-start) | collective-permute-done | bytes 655392 | tf_op jit(solution)/shard_map/ppermute | solution.py:271
  98.5 0.2 shard_map.88
  98.7 15.4 %all_to_all.36.parts = bf16[16,160,128]{2,1,0:T(8,128)(2,1)S(1)} all-to-all(bf16[16,160,128]{2,1,0:T(8,128)(2,1)S(1)} %shard_map.88), channel_id=1, replica_groups=mesh['zm'=2,'zn'=4,'core'=2,'y'=4,'zh'=2,'x'=4] {'y','x'}, dimensions={0} | all-to-all | bytes 1310720 | tf_op jit(solution)/shard_map/all_to_all | solution.py:267
  114.1 0.1 shard_map.89
  114.1 8.0 %all_to_all.37.parts = bf16[4,176,128]{2,1,0:T(8,128)(2,1)S(1)} all-to-all(bf16[4,176,128]{2,1,0:T(8,128)(2,1)S(1)} %shard_map.89), channel_id=1, replica_groups=mesh['zm'=2,'zn'=4,'core'=2,'y'=4,'zh'=2,'x'=4] {'zn'}, dimensions={0} | all-to-all | bytes 360448 | tf_op jit(solution)/shard_map/all_to_all | solution.py:267
  122.1 0.1 shard_map.90
  122.2 16.7 %all_to_all.38.parts = bf16[4,176,128]{2,1,0:T(8,128)(2,1)S(1)} all-to-all(bf16[4,176,128]{2,1,0:T(8,128)(2,1)S(1)} %shard_map.90), channel_id=1, replica_groups=mesh['zm'=2,'zn'=4,'core'=2,'y'=4,'zh'=2,'x'=4] {'zh','zm'}, dimensions={0} | all-to-all | bytes 360448 | tf_op jit(solution)/shard_map/all_to_all | solution.py:267
  138.9 0.1 shard_map.91
  139.0 15.9 %all_to_all.39.own = bf16[16,176,128]{2,1,0:T(8,128)(2,1)S(1)} all-to-all(bf16[16,176,128]{2,1,0:T(8,128)(2,1)S(1)} %shard_map.91), channel_id=1, replica_groups=mesh['zm'=2,'zn'=4,'core'=2,'y'=4,'zh'=2,'x'=4] {'y','x'}, dimensions={0} | all-to-all | bytes 1441792 | tf_op jit(solution)/shard_map/all_to_all | solution.py:267
  154.9 6.0 %collective-permute-start.1 = (bf16[16,176,128]{2,1,0:T(8,128)(2,1)S(1)}, bf16[16,176,128]{2,1,0:T(8,128)(2,1)S(1)}, u32[]{:S(2)}, u32[]{:S(2)}) collective-permute-start(bf16[16,176,128]{2,1,0:T(8,128)(2,1)S(1)} %all_to_all.39.own), channel_id=1, source_target_pairs={{0,32},{32,0},{1,33},{33,1},{2,34},{34,2},{3,35},{35,3},{4,36},{36... | collective-permute-start | bytes 2162696 | tf_op jit(solution)/shard_map/ppermute | solution.py:271
  160.8 1.8 %collective-permute-done.1.other = bf16[16,176,128]{2,1,0:T(8,128)(2,1)S(1)} collective-permute-done((bf16[16,176,128]{2,1,0:T(8,128)(2,1)S(1)}, bf16[16,176,128]{2,1,0:T(8,128)(2,1)S(1)}, u32[]{:S(2)}, u32[]{:S(2)}) %collective-permute-start.1) | collective-permute-done | bytes 720928 | tf_op jit(solution)/shard_map/ppermute | solution.py:271
  162.6 1.8 %shard_map.92 = (f32[1,1]{1,0:T(1,128)}, f32[768,512]{1,0:T(8,128)}, f32[512,512]{1,0:T(8,128)}) custom-call(s32[1]{0:T(128)} %bitcast.core, bf16[16,176,128]{2,1,0:T(8,128)(2,1)S(1)} %all_to_all.39.own, bf16[16,176,128]{2,1,0:T(8,128)(2,1)S(1)} %collective-permute-done.1.other), custom_call_target="tpu_custom_call" | custom-call | tf_op jit(solution)/shard_map/pallas_call | solution.py:43
Async XLA Ops:
  3.1 10.8 %copy-start = (bf16[16,1536]{1,0:T(8,128)(2,1)S(1)}, bf16[16,1536]{1,0:T(8,128)(2,1)}, u32[]{:S(2)}) copy-start(bf16[16,1536]{1,0:T(8,128)(2,1)} %get-tuple-element.20) | copy-start | bytes 147460
  3.1 43.3 %all-to-all-start = ((bf16[32,16,1792]{2,1,0:T(8,128)(2,1)}), bf16[32,16,1792]{2,1,0:T(8,128)(2,1)S(1)}, u32[]{:S(2)}, u32[]{:S(2)}) async-start(bf16[32,16,1792]{2,1,0:T(8,128)(2,1)} %get-tuple-element.19), calls=%async_computation | async-start | bytes 3670016 | tf_op jit(solution)/shard_map/all_to_all | solution.py:267
  71.4 18.0 %all-to-all-start.2 = ((f32[16,8,128]{2,1,0:T(8,128)}), f32[16,8,128]{2,1,0:T(8,128)S(1)}, u32[]{:S(2)}, u32[]{:S(2)}) async-start(f32[16,8,128]{2,1,0:T(8,128)} %get-tuple-element.22), calls=%async_computation.2 | async-start | bytes 131072 | tf_op jit(solution)/shard_map/all_to_all | solution.py:267
  92.8 5.8 %collective-permute-start = (bf16[16,160,128]{2,1,0:T(8,128)(2,1)S(1)}, bf16[16,160,128]{2,1,0:T(8,128)(2,1)S(1)}, u32[]{:S(2)}, u32[]{:S(2)}) collective-permute-start(bf16[16,160,128]{2,1,0:T(8,128)(2,1)S(1)} %get-tuple-element.30), channel_id=1, source_target_pairs={{0,32},{32,0},{1,33},{33,1},{2,34},{34,2},{3,35},{35,3},{4,36},{36... | collective-permute-start | bytes 1966088 | tf_op jit(solution)/shard_map/ppermute | solution.py:271
  154.9 7.8 %collective-permute-start.1 = (bf16[16,176,128]{2,1,0:T(8,128)(2,1)S(1)}, bf16[16,176,128]{2,1,0:T(8,128)(2,1)S(1)}, u32[]{:S(2)}, u32[]{:S(2)}) collective-permute-start(bf16[16,176,128]{2,1,0:T(8,128)(2,1)S(1)} %all_to_all.39.own), channel_id=1, source_target_pairs={{0,32},{32,0},{1,33},{33,1},{2,34},{34,2},{3,35},{35,3},{4,36},{36... | collective-permute-start | bytes 2162696 | tf_op jit(solution)/shard_map/ppermute | solution.py:271

commit v7 on v6

--- a/solution.py
+++ b/solution.py
@@ -106,12 +106,10 @@
     return top + jnp.log(jnp.sum(jnp.exp(x - top), axis, keepdims=True))
 
 
-def tile_body(width, img, txt, *refs):
-    ins, (row_out, col_out), outs = refs[:2], refs[2:4], refs[4:10]
-    w_img, w_txt = refs[10:12]
-    made = refs[12:16]
-    in_sems, out_sems = refs[16:]
-    copies = fetch(ins, (w_img, w_txt), in_sems)
+def tile_body(width, img, txt, w_img, w_txt_in, *refs):
+    (row_out, col_out), outs, w_txt, made = refs[:2], refs[2:8], refs[8], refs[9:13]
+    in_sems, out_sems = refs[13:]
+    copies = fetch([w_txt_in], [w_txt], in_sems)
     tl_own, sl_own, u_img, u_txt = made
     sources = list(made) + [img.at[:, width:], txt.at[:, width:]]
     back = [pltpu.make_async_copy(sources[k], outs[k], out_sems.at[k]) for k in range(6)]
@@ -119,10 +117,9 @@
     back[5].start()
     tl_own[...] = TEACHER_SCALE * dot(img[:, :width], txt[:, :width], NT)
     back[0].start()
-    copies[0].wait()
     u_img[...] = dot(img[:, width:], w_img[...])
     back[2].start()
-    copies[1].wait()
+    copies[0].wait()
     u_txt[...] = dot(txt[:, width:], w_txt[...])
     back[3].start()
     ui = u_img[...]
@@ -296,6 +293,7 @@
         ],
         compiler_params=room(8),
     )(*[pinned(a) for a in raw])
+    pack_img, core = lax.optimization_barrier((pack_img, core))
     img = exchange(pack_img, TILE).reshape(rows, wide_i)
     txt = lax.all_gather(pack_txt, RING, axis=0, tiled=True)
 
@@ -306,14 +304,15 @@
         out_shape=[jax.ShapeDtypeStruct((n, 8, LANES), F32) for n in (n_tile, n_ring)]
         + [pltpu.HBM(b, F32) for b in blocks]
         + [pltpu.HBM(b, BF16) for b in feats],
-        in_specs=[VMEM] * 2 + [HBM] * 2,
+        in_specs=[VMEM] * 3 + [HBM],
         out_specs=[VMEM] * 2 + [HBM] * 6,
-        scratch_shapes=[pltpu.VMEM(a.shape, BF16) for a in (proj_img, proj_txt)]
+        scratch_shapes=[pltpu.VMEM(proj_txt.shape, BF16)]
         + [pltpu.VMEM(b, F32) for b in blocks]
-        + [pltpu.SemaphoreType.DMA((n,)) for n in (2, 6)],
+        + [pltpu.SemaphoreType.DMA((n,)) for n in (1, 6)],
         compiler_params=room(24),
-    )(img, txt, pinned(proj_img), pinned(proj_txt))
+    )(img, txt, proj_img, pinned(proj_txt))
     row_all = exchange(row_part, TILE)
+    col_part, row_all = lax.optimization_barrier((col_part, row_all))
     col_all = exchange(col_part, RING)
 
     box = (n_plane, CHUNK, LANES)
@@ -342,8 +341,8 @@
     part = exchange(part, PLANE)
     (part,) = call(fold_body, 8, [((n_near, BOX, LANES), BF16)], part, total)
     part = exchange(part, NEAR)
-    (part,) = call(fold_body, 8, [((n_far, BOX, LANES), BF16)], part)
-    part = exchange(part, FAR)
+    (part,) = call(fold_body, 8, [((1, BOX, LANES), BF16)], part)
+    part = lax.all_gather(part, FAR, axis=0, tiled=True)
     (part,) = call(fold_body, 8, [((n_plane, BOX, LANES), BF16)], part)
     mine = exchange(part, PLANE)
     other = swap_cores(mine)

time: 165 us -> 162 us (0.982)
  blocking collectives: 108 us -> 124 us
  waiting for transfers between devices: 15.1 us -> 3.5 us
  starting transfers between devices: 27.2 us -> 22.6 us
  Pallas kernels: 12.9 us -> 10.7 us
    all_gather x0 -> x1, blocking collectives: none -> 16.9 us  [shards(): part = lax.all_gather(part, FAR, axis=0, tiled=True)]
    all_to_all x2 -> x1, waiting for transfers between devices: 11.6 us -> 0.01 us  [exchange(): return lax.all_to_all(copies, axes, 0, 0, tiled=True)]
    all_to_all x2 -> x1, starting transfers between devices: 17.2 us -> 10.8 us  [exchange(): return lax.all_to_all(copies, axes, 0, 0, tiled=True)]
    pallas_call x1, Pallas kernels: 4.88 us -> 2.71 us  [shards(): pl.pallas_call(functools.partial(tile_body, width), out_shape=[jax.ShapeD...]
    ppermute x2, starting transfers between devices: 10 us -> 11.9 us  [swap_cores(): return lax.ppermute(block, 'core', [(0, 1), (1, 0)])]
  transfers between devices with their start and end apart: 4 -> 3, of which waited for: 3 -> 2; matrix products, arithmetic and copies ran while one was open for 0% -> 0% of each run, Pallas kernels for 0% -> 0%
where the time goes in v7:
time: 162 us
  blocking collectives  124 us (77%)
  starting transfers between devices  22.6 us (14%)
  Pallas kernels  10.7 us (7%)
  waiting for transfers between devices  3.5 us (2%)
    all_to_all x5, blocking collectives, exchange(): return lax.all_to_all(copies, axes, 0, 0, tiled=True)  74.6 us
    all_gather x1, blocking collectives, shards(): txt = lax.all_gather(pack_txt, RING, axis=0, tiled=True)  32.5 us
    all_gather x1, blocking collectives, shards(): part = lax.all_gather(part, FAR, axis=0, tiled=True)  16.9 us
    ppermute x2, starting transfers between devices, swap_cores(): return lax.ppermute(block, 'core', [(0, 1), (1, 0)])  11.9 us
    all_to_all x1, starting transfers between devices, exchange(): return lax.all_to_all(copies, axes, 0, 0, tiled=True)  10.8 us
    ppermute x2, waiting for transfers between devices, swap_cores(): return lax.ppermute(block, 'core', [(0, 1), (1, 0)])  3.5 us
    pallas_call x1, Pallas kernels, shards(): pl.pallas_call(grad_body, out_shape=[jax.ShapeDtypeStruct(box, BF16), jax...  3.36 us
  transfers between devices with their start and end apart: 3, of which 2 were waited for; matrix products, arithmetic and copies ran while one was open for 0% of the time, Pallas kernels for 0%

profile of v7, /device:TPU:1, one launch (start us, length us, event | category | flops | bytes accessed | tf_op | source)
XLA Modules:
  0.0 161.6 jit_solution(8947734392554622351)
XLA Ops:
  0.6 2.4 %shard_map.85 = (bf16[32,16,1792]{2,1,0:T(8,128)(2,1)}, bf16[16,1536]{1,0:T(8,128)(2,1)}) custom-call(bf16[16,1024]{1,0:T(8,128)(2,1)} %refs_0_.1, bf16[16,768]{1,0:T(8,128)(2,1)} %refs_1_.1, bf16[16,1024]{1,0:T(8,128)(2,1)} %refs_2_.1, bf16[16,512]{1,0:T(8,128)(2,1)} %refs_3_.1), custom_call_target="tpu_custom_call" | custom-call | tf_op jit(solution)/shard_map/pallas_call | solution.py:282
  3.1 0.0 copy-start.1
  3.1 0.0 copy-start
  3.1 10.8 %all-to-all-start = ((bf16[32,16,1792]{2,1,0:T(8,128)(2,1)}), bf16[32,16,1792]{2,1,0:T(8,128)(2,1)S(1)}, u32[]{:S(2)}, u32[]{:S(2)}) async-start(bf16[32,16,1792]{2,1,0:T(8,128)(2,1)} %get-tuple-element.25), calls=%async_computation | async-start | bytes 3670016 | tf_op jit(solution)/shard_map/all_to_all | solution.py:264
  13.9 0.0 copy-done.1
  13.9 32.5 %all_gather.6.txt = bf16[256,1536]{1,0:T(8,128)(2,1)S(1)} all-gather(bf16[16,1536]{1,0:T(8,128)(2,1)S(1)} %copy-done.1), channel_id=1, replica_groups=mesh['zm'=2,'zn'=4,'core'=2,'y'=4,'zh'=2,'x'=4] {'zh','zm','zn'}, dimensions={0}, use_global_device_ids=true | all-gather | bytes 835584 | tf_op jit(solution)/shard_map/all_gather | solution.py:298
  46.4 0.0 all-to-all-done
  46.4 0.0 copy-done
  46.4 2.7 %shard_map.86 = (f32[32,8,128]{2,1,0:T(8,128)S(1)}, f32[16,8,128]{2,1,0:T(8,128)S(1)}, f32[512,256]{1,0:T(8,128)}, f32[512,256]{1,0:T(8,128)}, f32[512,512]{1,0:...) custom-call(bf16[512,1792]{1,0:T(8,128)(2,1)S(1)} %bitcast.3, ...), custom_call_target="tpu_custom_call" | custom-call | tf_op jit(solution)/shard_map/pallas_call | solution.py:302
  49.1 20.1 %all_to_all.30.row_all = f32[32,8,128]{2,1,0:T(8,128)S(1)} all-to-all(f32[32,8,128]{2,1,0:T(8,128)S(1)} %get-tuple-element.28), channel_id=1, replica_groups=mesh['zm'=2,'zn'=4,'core'=2,'y'=4,'zh'=2,'x'=4] {'core','y','x'}, dimensions={0} | all-to-all | bytes 262144 | tf_op jit(solution)/shard_map/all_to_all | solution.py:264
  69.2 17.8 %all_to_all.31.col_all = f32[16,8,128]{2,1,0:T(8,128)S(1)} all-to-all(f32[16,8,128]{2,1,0:T(8,128)S(1)} %get-tuple-element.30), channel_id=1, replica_groups=mesh['zm'=2,'zn'=4,'core'=2,'y'=4,'zh'=2,'x'=4] {'zh','zm','zn'}, dimensions={0} | all-to-all | bytes 131072 | tf_op jit(solution)/shard_map/all_to_all | solution.py:264
  87.0 3.4 %shard_map.87 = (bf16[16,160,128]{2,1,0:T(8,128)(2,1)S(1)}, bf16[16,160,128]{2,1,0:T(8,128)(2,1)S(1)}, f32[8,128]{1,0:T(8,128)S(1)}) custom-call(s32[1]{0:T(128)} %bitcast.core, f32[32,8,128]{2,1,0:T(8,128)S(1)} %all_to_all.30.row_all, f32[16,8,128]{2,1,0:T(8,128)S(1)} %all_to_all.31.col_all, f32[512,256]{1,0:T(8,128)} %get-tuple-element.31.refs_0_, ...), custom_call_target="tpu_custom_call" | custom-call | tf_op jit(solution)/shard_map/pallas_call | solution.py:319
  90.4 4.1 %collective-permute-start = (bf16[16,160,128]{2,1,0:T(8,128)(2,1)S(1)}, bf16[16,160,128]{2,1,0:T(8,128)(2,1)S(1)}, u32[]{:S(2)}, u32[]{:S(2)}) collective-permute-start(bf16[16,160,128]{2,1,0:T(8,128)(2,1)S(1)} %get-tuple-element.38), channel_id=1, source_target_pairs={{0,32},{32,0},{1,33},{33,1},{2,34},{34,2},{3,35},{35,3},{4,36},{36... | collective-permute-start | bytes 1966088 | tf_op jit(solution)/shard_map/ppermute | solution.py:268
  94.5 1.7 %collective-permute-done.b = bf16[16,160,128]{2,1,0:T(8,128)(2,1)S(1)} collective-permute-done((bf16[16,160,128]{2,1,0:T(8,128)(2,1)S(1)}, bf16[16,160,128]{2,1,0:T(8,128)(2,1)S(1)}, u32[]{:S(2)}, u32[]{:S(2)}) %collective-permute-start) | collective-permute-done | bytes 655392 | tf_op jit(solution)/shard_map/ppermute | solution.py:268
  96.2 0.2 shard_map.88
  96.3 15.3 %all_to_all.32.parts = bf16[16,160,128]{2,1,0:T(8,128)(2,1)S(1)} all-to-all(bf16[16,160,128]{2,1,0:T(8,128)(2,1)S(1)} %shard_map.88), channel_id=1, replica_groups=mesh['zm'=2,'zn'=4,'core'=2,'y'=4,'zh'=2,'x'=4] {'y','x'}, dimensions={0} | all-to-all | bytes 1310720 | tf_op jit(solution)/shard_map/all_to_all | solution.py:264
  111.7 0.1 shard_map.89
  111.8 8.0 %all_to_all.33.parts = bf16[4,176,128]{2,1,0:T(8,128)(2,1)S(1)} all-to-all(bf16[4,176,128]{2,1,0:T(8,128)(2,1)S(1)} %shard_map.89), channel_id=1, replica_groups=mesh['zm'=2,'zn'=4,'core'=2,'y'=4,'zh'=2,'x'=4] {'zn'}, dimensions={0} | all-to-all | bytes 360448 | tf_op jit(solution)/shard_map/all_to_all | solution.py:264
  119.7 0.1 shard_map.90
  119.8 16.9 %all_gather.7.parts = bf16[4,176,128]{2,1,0:T(8,128)(2,1)S(1)} all-gather(bf16[1,176,128]{2,1,0:T(8,128)(2,1)S(1)} %shard_map.90), channel_id=1, replica_groups=mesh['zm'=2,'zn'=4,'core'=2,'y'=4,'zh'=2,'x'=4] {'zh','zm'}, dimensions={0}, use_global_device_ids=true | all-gather | bytes 225280 | tf_op jit(solution)/shard_map/all_gather | solution.py:345
  136.8 0.1 shard_map.91
  136.8 13.3 %all_to_all.34.own = bf16[16,176,128]{2,1,0:T(8,128)(2,1)S(1)} all-to-all(bf16[16,176,128]{2,1,0:T(8,128)(2,1)S(1)} %shard_map.91), channel_id=1, replica_groups=mesh['zm'=2,'zn'=4,'core'=2,'y'=4,'zh'=2,'x'=4] {'y','x'}, dimensions={0} | all-to-all | bytes 1441792 | tf_op jit(solution)/shard_map/all_to_all | solution.py:264
  150.2 7.8 %collective-permute-start.1 = (bf16[16,176,128]{2,1,0:T(8,128)(2,1)S(1)}, bf16[16,176,128]{2,1,0:T(8,128)(2,1)S(1)}, u32[]{:S(2)}, u32[]{:S(2)}) collective-permute-start(bf16[16,176,128]{2,1,0:T(8,128)(2,1)S(1)} %all_to_all.34.own), channel_id=1, source_target_pairs={{0,32},{32,0},{1,33},{33,1},{2,34},{34,2},{3,35},{35,3},{4,36},{36... | collective-permute-start | bytes 2162696 | tf_op jit(solution)/shard_map/ppermute | solution.py:268
  158.0 1.8 %collective-permute-done.1.other = bf16[16,176,128]{2,1,0:T(8,128)(2,1)S(1)} collective-permute-done((bf16[16,176,128]{2,1,0:T(8,128)(2,1)S(1)}, bf16[16,176,128]{2,1,0:T(8,128)(2,1)S(1)}, u32[]{:S(2)}, u32[]{:S(2)}) %collective-permute-start.1) | collective-permute-done | bytes 720928 | tf_op jit(solution)/shard_map/ppermute | solution.py:268
  159.8 1.8 %shard_map.92 = (f32[1,1]{1,0:T(1,128)}, f32[768,512]{1,0:T(8,128)}, f32[512,512]{1,0:T(8,128)}) custom-call(s32[1]{0:T(128)} %bitcast.core, bf16[16,176,128]{2,1,0:T(8,128)(2,1)S(1)} %all_to_all.34.own, bf16[16,176,128]{2,1,0:T(8,128)(2,1)S(1)} %collective-permute-done.1.other), custom_call_target="tpu_custom_call" | custom-call | tf_op jit(solution)/shard_map/pallas_call | solution.py:43
Async XLA Ops:
  3.1 10.8 %copy-start.1 = (bf16[16,1536]{1,0:T(8,128)(2,1)S(1)}, bf16[16,1536]{1,0:T(8,128)(2,1)}, u32[]{:S(2)}) copy-start(bf16[16,1536]{1,0:T(8,128)(2,1)} %get-tuple-element.26) | copy-start | bytes 147460
  3.1 43.3 %copy-start = (bf16[768,512]{1,0:T(8,128)(2,1)S(1)}, bf16[768,512]{1,0:T(8,128)(2,1)}, u32[]{:S(2)}) copy-start(bf16[768,512]{1,0:T(8,128)(2,1)} %w_img.1) | copy-start | bytes 2359300
  3.1 43.3 %all-to-all-start = ((bf16[32,16,1792]{2,1,0:T(8,128)(2,1)}), bf16[32,16,1792]{2,1,0:T(8,128)(2,1)S(1)}, u32[]{:S(2)}, u32[]{:S(2)}) async-start(bf16[32,16,1792]{2,1,0:T(8,128)(2,1)} %get-tuple-element.25), calls=%async_computation | async-start | bytes 3670016 | tf_op jit(solution)/shard_map/all_to_all | solution.py:264
  90.4 5.8 %collective-permute-start = (bf16[16,160,128]{2,1,0:T(8,128)(2,1)S(1)}, bf16[16,160,128]{2,1,0:T(8,128)(2,1)S(1)}, u32[]{:S(2)}, u32[]{:S(2)}) collective-permute-start(bf16[16,160,128]{2,1,0:T(8,128)(2,1)S(1)} %get-tuple-element.38), channel_id=1, source_target_pairs={{0,32},{32,0},{1,33},{33,1},{2,34},{34,2},{3,35},{35,3},{4,36},{36... | collective-permute-start | bytes 1966088 | tf_op jit(solution)/shard_map/ppermute | solution.py:268
  150.2 9.6 %collective-permute-start.1 = (bf16[16,176,128]{2,1,0:T(8,128)(2,1)S(1)}, bf16[16,176,128]{2,1,0:T(8,128)(2,1)S(1)}, u32[]{:S(2)}, u32[]{:S(2)}) collective-permute-start(bf16[16,176,128]{2,1,0:T(8,128)(2,1)S(1)} %all_to_all.34.own), channel_id=1, source_target_pairs={{0,32},{32,0},{1,33},{33,1},{2,34},{34,2},{3,35},{35,3},{4,36},{36... | collective-permute-start | bytes 2162696 | tf_op jit(solution)/shard_map/ppermute | solution.py:268

commit v8 on v7

--- a/solution.py
+++ b/solution.py
@@ -107,29 +107,27 @@
 
 
 def tile_body(width, img, txt, w_img, w_txt_in, *refs):
-    (row_out, col_out), outs, w_txt, made = refs[:2], refs[2:8], refs[8], refs[9:13]
-    in_sems, out_sems = refs[13:]
+    (row_out, col_out), outs, w_txt, made = refs[:2], refs[2:7], refs[7], refs[8:11]
+    in_sems, out_sems = refs[11:]
     copies = fetch([w_txt_in], [w_txt], in_sems)
-    tl_own, sl_own, u_img, u_txt = made
+    tl_own, u_img, u_txt = made
     sources = list(made) + [img.at[:, width:], txt.at[:, width:]]
-    back = [pltpu.make_async_copy(sources[k], outs[k], out_sems.at[k]) for k in range(6)]
-    back[4].start()
-    back[5].start()
+    back = [pltpu.make_async_copy(sources[k], outs[k], out_sems.at[k]) for k in range(5)]
+    for c in back[3:]:
+        c.start()
     tl_own[...] = TEACHER_SCALE * dot(img[:, :width], txt[:, :width], NT)
     back[0].start()
     u_img[...] = dot(img[:, width:], w_img[...])
-    back[2].start()
+    back[1].start()
     copies[0].wait()
     u_txt[...] = dot(txt[:, width:], w_txt[...])
-    back[3].start()
+    back[2].start()
     ui = u_img[...]
     ut = u_txt[...]
     ei = (ui * scale_of(ui)).astype(BF16)
     et = (ut * scale_of(ut)).astype(BF16)
-    sl_own[...] = STUDENT_SCALE * dot(ei, et, NT)
-    back[1].start()
+    sl = STUDENT_SCALE * dot(ei, et, NT)
     tl = tl_own[...]
-    sl = sl_own[...]
     es = jnp.exp(sl)
     rows, cols = tl.shape
     row_t = lse(tl, 1)
@@ -160,9 +158,9 @@
 
 
 def grad_body(core, row_all, col_all, *refs):
-    ins, (keep, send, loss), held, (g, wi, wt, sems) = refs[:6], refs[6:9], refs[9:15], refs[15:]
+    ins, (keep, send, loss), held, (g, wi, wt, sems) = refs[:5], refs[5:8], refs[8:13], refs[13:]
     copies = fetch(ins, held, sems)
-    tl, sl, u_img, u_txt, feats_img, feats_txt = held
+    tl, u_img, u_txt, feats_img, feats_txt = held
     rows, cols = tl.shape
     row_parts, col_parts = (row_all.shape[0], col_all.shape[0])
     row = lse(row_all[...], 0)[0]
@@ -175,12 +173,19 @@
     col_t = jnp.concatenate([col[0:1], col[1:2]], 1)
     col_s = jnp.concatenate([col[2:3], col[3:4]], 1)
     acc = jnp.zeros((LANES, cols), F32)
-    copies[0].wait()
-    copies[1].wait()
+    for c in copies:
+        c.wait()
+    ui = u_img[...]
+    ut = u_txt[...]
+    inv_img = scale_of(ui)
+    inv_txt = scale_of(ut)
+    ei = ui * inv_img
+    et = ut * inv_txt
+    sl = STUDENT_SCALE * dot(ei.astype(BF16), et.astype(BF16), NT)
     for b in range(rows // LANES):
         at = pl.ds(b * LANES, LANES)
         t = tl[at, :]
-        s = sl[at, :]
+        s = sl[b * LANES : (b + 1) * LANES]
         pt_row = jnp.exp(t - down[:, 2 * b : 2 * b + 1])
         ps_row = jnp.exp(s - down[:, 2 * b + 1 : 2 * b + 2])
         pt_col = jnp.exp(t - col_t)
@@ -189,14 +194,6 @@
         g[at, :] = (0.5 * STUDENT_SCALE * ((ps_row - pt_row) + (ps_col - pt_col))).astype(BF16)
     total = total + jnp.sum(acc, keepdims=True)
     loss[...] = jnp.broadcast_to(total, (8, LANES))
-    for c in copies[2:]:
-        c.wait()
-    ui = u_img[...]
-    ut = u_txt[...]
-    inv_img = scale_of(ui)
-    inv_txt = scale_of(ut)
-    ei = ui * inv_img
-    et = ut * inv_txt
     gb = g[...]
     di = dot(gb, et.astype(BF16))
     dt = dot(gb, ei.astype(BF16), TN)
@@ -297,7 +294,7 @@
     img = exchange(pack_img, TILE).reshape(rows, wide_i)
     txt = lax.all_gather(pack_txt, RING, axis=0, tiled=True)
 
-    blocks = [(rows, cols), (rows, cols), (rows, depth), (cols, depth)]
+    blocks = [(rows, cols), (rows, depth), (cols, depth)]
     feats = [(rows, proj_img.shape[0]), (cols, proj_txt.shape[0])]
     row_part, col_part, *kept = pl.pallas_call(
         functools.partial(tile_body, width),
@@ -305,10 +302,10 @@
         + [pltpu.HBM(b, F32) for b in blocks]
         + [pltpu.HBM(b, BF16) for b in feats],
         in_specs=[VMEM] * 3 + [HBM],
-        out_specs=[VMEM] * 2 + [HBM] * 6,
+        out_specs=[VMEM] * 2 + [HBM] * 5,
         scratch_shapes=[pltpu.VMEM(proj_txt.shape, BF16)]
         + [pltpu.VMEM(b, F32) for b in blocks]
-        + [pltpu.SemaphoreType.DMA((n,)) for n in (1, 6)],
+        + [pltpu.SemaphoreType.DMA((n,)) for n in (1, 5)],
         compiler_params=room(24),
     )(img, txt, proj_img, pinned(proj_txt))
     row_all = exchange(row_part, TILE)
@@ -323,7 +320,7 @@
             jax.ShapeDtypeStruct(box, BF16),
             jax.ShapeDtypeStruct((8, LANES), F32),
         ],
-        in_specs=[SMEM, VMEM, VMEM] + [HBM] * 6,
+        in_specs=[SMEM, VMEM, VMEM] + [HBM] * 5,
         out_specs=[VMEM] * 3,
         scratch_shapes=[pltpu.VMEM(b, F32) for b in blocks]
         + [
@@ -332,7 +329,7 @@
             pltpu.VMEM((rows, cols), BF16),
             pltpu.VMEM(proj_img.shape, BF16),
             pltpu.VMEM(proj_txt.shape, BF16),
-            pltpu.SemaphoreType.DMA((6,)),
+            pltpu.SemaphoreType.DMA((5,)),
         ],
         compiler_params=room(24),
     )(core, row_all, col_all, *[pinned(k) for k in kept])

time: 162 us -> 162 us (level)
  no operation moved by 1% of the time
where the time goes in v8:
time: 162 us
  blocking collectives  124 us (77%)
  starting transfers between devices  22.7 us (14%)
  Pallas kernels  11 us (7%)
  waiting for transfers between devices  3.5 us (2%)
    all_to_all x5, blocking collectives, exchange(): return lax.all_to_all(copies, axes, 0, 0, tiled=True)  74.6 us
    all_gather x1, blocking collectives, shards(): txt = lax.all_gather(pack_txt, RING, axis=0, tiled=True)  32.5 us
    all_gather x1, blocking collectives, shards(): part = lax.all_gather(part, FAR, axis=0, tiled=True)  16.9 us
    ppermute x2, starting transfers between devices, swap_cores(): return lax.ppermute(block, 'core', [(0, 1), (1, 0)])  11.9 us
    all_to_all x1, starting transfers between devices, exchange(): return lax.all_to_all(copies, axes, 0, 0, tiled=True)  10.8 us
    pallas_call x1, Pallas kernels, shards(): pl.pallas_call(grad_body, out_shape=[jax.ShapeDtypeStruct(box, BF16), jax...  3.78 us
    ppermute x2, waiting for transfers between devices, swap_cores(): return lax.ppermute(block, 'core', [(0, 1), (1, 0)])  3.5 us
  transfers between devices with their start and end apart: 3, of which 2 were waited for; matrix products, arithmetic and copies ran while one was open for 0% of the time, Pallas kernels for 0%

profile of v8, /device:TPU:1, one launch (start us, length us, event | category | flops | bytes accessed | tf_op | source)
XLA Modules:
  0.0 161.9 jit_solution(10347634889518945625)
XLA Ops:
  0.6 2.4 %shard_map.85 = (bf16[32,16,1792]{2,1,0:T(8,128)(2,1)}, bf16[16,1536]{1,0:T(8,128)(2,1)}) custom-call(bf16[16,1024]{1,0:T(8,128)(2,1)} %refs_0_.1, bf16[16,768]{1,0:T(8,128)(2,1)} %refs_1_.1, bf16[16,1024]{1,0:T(8,128)(2,1)} %refs_2_.1, bf16[16,512]{1,0:T(8,128)(2,1)} %refs_3_.1), custom_call_target="tpu_custom_call" | custom-call | tf_op jit(solution)/shard_map/pallas_call | solution.py:279
  3.1 0.0 copy-start.1
  3.1 0.0 copy-start
  3.1 10.8 %all-to-all-start = ((bf16[32,16,1792]{2,1,0:T(8,128)(2,1)}), bf16[32,16,1792]{2,1,0:T(8,128)(2,1)S(1)}, u32[]{:S(2)}, u32[]{:S(2)}) async-start(bf16[32,16,1792]{2,1,0:T(8,128)(2,1)} %get-tuple-element.24), calls=%async_computation | async-start | bytes 3670016 | tf_op jit(solution)/shard_map/all_to_all | solution.py:261
  13.9 0.0 copy-done.1
  13.9 32.5 %all_gather.6.txt = bf16[256,1536]{1,0:T(8,128)(2,1)S(1)} all-gather(bf16[16,1536]{1,0:T(8,128)(2,1)S(1)} %copy-done.1), channel_id=1, replica_groups=mesh['zm'=2,'zn'=4,'core'=2,'y'=4,'zh'=2,'x'=4] {'zh','zm','zn'}, dimensions={0}, use_global_device_ids=true | all-gather | bytes 835584 | tf_op jit(solution)/shard_map/all_gather | solution.py:295
  46.4 0.0 all-to-all-done
  46.4 0.0 copy-done
  46.4 2.6 %shard_map.86 = (f32[32,8,128]{2,1,0:T(8,128)S(1)}, f32[16,8,128]{2,1,0:T(8,128)S(1)}, f32[512,256]{1,0:T(8,128)}, f32[512,512]{1,0:T(8,128)}, f32[256,512]{1,0:...) custom-call(bf16[512,1792]{1,0:T(8,128)(2,1)S(1)} %bitcast.3, bf16[256,1536]{1,0:T(8,128)(2,1)S(1)} %all_gather.6.txt, ...), custom_call_target="tpu_custom_call" | custom-call | tf_op jit(solution)/shard_map/pallas_call | solution.py:299
  49.0 20.1 %all_to_all.30.row_all = f32[32,8,128]{2,1,0:T(8,128)S(1)} all-to-all(f32[32,8,128]{2,1,0:T(8,128)S(1)} %get-tuple-element.27), channel_id=1, replica_groups=mesh['zm'=2,'zn'=4,'core'=2,'y'=4,'zh'=2,'x'=4] {'core','y','x'}, dimensions={0} | all-to-all | bytes 262144 | tf_op jit(solution)/shard_map/all_to_all | solution.py:261
  69.1 17.8 %all_to_all.31.col_all = f32[16,8,128]{2,1,0:T(8,128)S(1)} all-to-all(f32[16,8,128]{2,1,0:T(8,128)S(1)} %get-tuple-element.29), channel_id=1, replica_groups=mesh['zm'=2,'zn'=4,'core'=2,'y'=4,'zh'=2,'x'=4] {'zh','zm','zn'}, dimensions={0} | all-to-all | bytes 131072 | tf_op jit(solution)/shard_map/all_to_all | solution.py:261
  86.9 3.8 %shard_map.87 = (bf16[16,160,128]{2,1,0:T(8,128)(2,1)S(1)}, bf16[16,160,128]{2,1,0:T(8,128)(2,1)S(1)}, f32[8,128]{1,0:T(8,128)S(1)}) custom-call(s32[1]{0:T(128)} %bitcast.core, f32[32,8,128]{2,1,0:T(8,128)S(1)} %all_to_all.30.row_all, f32[16,8,128]{2,1,0:T(8,128)S(1)} %all_to_all.31.col_all, f32[512,256]{1,0:T(8,128)} %get-tuple-element.30.refs_0_, ...), custom_call_target="tpu_custom_call" | custom-call | tf_op jit(solution)/shard_map/pallas_call | solution.py:316
  90.7 4.1 %collective-permute-start = (bf16[16,160,128]{2,1,0:T(8,128)(2,1)S(1)}, bf16[16,160,128]{2,1,0:T(8,128)(2,1)S(1)}, u32[]{:S(2)}, u32[]{:S(2)}) collective-permute-start(bf16[16,160,128]{2,1,0:T(8,128)(2,1)S(1)} %get-tuple-element.36), channel_id=1, source_target_pairs={{0,32},{32,0},{1,33},{33,1},{2,34},{34,2},{3,35},{35,3},{4,36},{36... | collective-permute-start | bytes 1966088 | tf_op jit(solution)/shard_map/ppermute | solution.py:265
  94.8 1.7 %collective-permute-done.b = bf16[16,160,128]{2,1,0:T(8,128)(2,1)S(1)} collective-permute-done((bf16[16,160,128]{2,1,0:T(8,128)(2,1)S(1)}, bf16[16,160,128]{2,1,0:T(8,128)(2,1)S(1)}, u32[]{:S(2)}, u32[]{:S(2)}) %collective-permute-start) | collective-permute-done | bytes 655392 | tf_op jit(solution)/shard_map/ppermute | solution.py:265
  96.5 0.2 shard_map.88
  96.6 15.4 %all_to_all.32.parts = bf16[16,160,128]{2,1,0:T(8,128)(2,1)S(1)} all-to-all(bf16[16,160,128]{2,1,0:T(8,128)(2,1)S(1)} %shard_map.88), channel_id=1, replica_groups=mesh['zm'=2,'zn'=4,'core'=2,'y'=4,'zh'=2,'x'=4] {'y','x'}, dimensions={0} | all-to-all | bytes 1310720 | tf_op jit(solution)/shard_map/all_to_all | solution.py:261
  112.0 0.1 shard_map.89
  112.1 8.0 %all_to_all.33.parts = bf16[4,176,128]{2,1,0:T(8,128)(2,1)S(1)} all-to-all(bf16[4,176,128]{2,1,0:T(8,128)(2,1)S(1)} %shard_map.89), channel_id=1, replica_groups=mesh['zm'=2,'zn'=4,'core'=2,'y'=4,'zh'=2,'x'=4] {'zn'}, dimensions={0} | all-to-all | bytes 360448 | tf_op jit(solution)/shard_map/all_to_all | solution.py:261
  120.1 0.1 shard_map.90
  120.1 16.9 %all_gather.7.parts = bf16[4,176,128]{2,1,0:T(8,128)(2,1)S(1)} all-gather(bf16[1,176,128]{2,1,0:T(8,128)(2,1)S(1)} %shard_map.90), channel_id=1, replica_groups=mesh['zm'=2,'zn'=4,'core'=2,'y'=4,'zh'=2,'x'=4] {'zh','zm'}, dimensions={0}, use_global_device_ids=true | all-gather | bytes 225280 | tf_op jit(solution)/shard_map/all_gather | solution.py:342
  137.1 0.1 shard_map.91
  137.2 13.3 %all_to_all.34.own = bf16[16,176,128]{2,1,0:T(8,128)(2,1)S(1)} all-to-all(bf16[16,176,128]{2,1,0:T(8,128)(2,1)S(1)} %shard_map.91), channel_id=1, replica_groups=mesh['zm'=2,'zn'=4,'core'=2,'y'=4,'zh'=2,'x'=4] {'y','x'}, dimensions={0} | all-to-all | bytes 1441792 | tf_op jit(solution)/shard_map/all_to_all | solution.py:261
  150.5 7.8 %collective-permute-start.1 = (bf16[16,176,128]{2,1,0:T(8,128)(2,1)S(1)}, bf16[16,176,128]{2,1,0:T(8,128)(2,1)S(1)}, u32[]{:S(2)}, u32[]{:S(2)}) collective-permute-start(bf16[16,176,128]{2,1,0:T(8,128)(2,1)S(1)} %all_to_all.34.own), channel_id=1, source_target_pairs={{0,32},{32,0},{1,33},{33,1},{2,34},{34,2},{3,35},{35,3},{4,36},{36... | collective-permute-start | bytes 2162696 | tf_op jit(solution)/shard_map/ppermute | solution.py:265
  158.3 1.8 %collective-permute-done.1.other = bf16[16,176,128]{2,1,0:T(8,128)(2,1)S(1)} collective-permute-done((bf16[16,176,128]{2,1,0:T(8,128)(2,1)S(1)}, bf16[16,176,128]{2,1,0:T(8,128)(2,1)S(1)}, u32[]{:S(2)}, u32[]{:S(2)}) %collective-permute-start.1) | collective-permute-done | bytes 720928 | tf_op jit(solution)/shard_map/ppermute | solution.py:265
  160.1 1.8 %shard_map.92 = (f32[1,1]{1,0:T(1,128)}, f32[768,512]{1,0:T(8,128)}, f32[512,512]{1,0:T(8,128)}) custom-call(s32[1]{0:T(128)} %bitcast.core, bf16[16,176,128]{2,1,0:T(8,128)(2,1)S(1)} %all_to_all.34.own, bf16[16,176,128]{2,1,0:T(8,128)(2,1)S(1)} %collective-permute-done.1.other), custom_call_target="tpu_custom_call" | custom-call | tf_op jit(solution)/shard_map/pallas_call | solution.py:43
Async XLA Ops:
  3.1 10.8 %copy-start.1 = (bf16[16,1536]{1,0:T(8,128)(2,1)S(1)}, bf16[16,1536]{1,0:T(8,128)(2,1)}, u32[]{:S(2)}) copy-start(bf16[16,1536]{1,0:T(8,128)(2,1)} %get-tuple-element.25) | copy-start | bytes 147460
  3.1 43.3 %copy-start = (bf16[768,512]{1,0:T(8,128)(2,1)S(1)}, bf16[768,512]{1,0:T(8,128)(2,1)}, u32[]{:S(2)}) copy-start(bf16[768,512]{1,0:T(8,128)(2,1)} %w_img.1) | copy-start | bytes 2359300
  3.1 43.3 %all-to-all-start = ((bf16[32,16,1792]{2,1,0:T(8,128)(2,1)}), bf16[32,16,1792]{2,1,0:T(8,128)(2,1)S(1)}, u32[]{:S(2)}, u32[]{:S(2)}) async-start(bf16[32,16,1792]{2,1,0:T(8,128)(2,1)} %get-tuple-element.24), calls=%async_computation | async-start | bytes 3670016 | tf_op jit(solution)/shard_map/all_to_all | solution.py:261
  90.7 5.8 %collective-permute-start = (bf16[16,160,128]{2,1,0:T(8,128)(2,1)S(1)}, bf16[16,160,128]{2,1,0:T(8,128)(2,1)S(1)}, u32[]{:S(2)}, u32[]{:S(2)}) collective-permute-start(bf16[16,160,128]{2,1,0:T(8,128)(2,1)S(1)} %get-tuple-element.36), channel_id=1, source_target_pairs={{0,32},{32,0},{1,33},{33,1},{2,34},{34,2},{3,35},{35,3},{4,36},{36... | collective-permute-start | bytes 1966088 | tf_op jit(solution)/shard_map/ppermute | solution.py:265
  150.5 9.6 %collective-permute-start.1 = (bf16[16,176,128]{2,1,0:T(8,128)(2,1)S(1)}, bf16[16,176,128]{2,1,0:T(8,128)(2,1)S(1)}, u32[]{:S(2)}, u32[]{:S(2)}) collective-permute-start(bf16[16,176,128]{2,1,0:T(8,128)(2,1)S(1)} %all_to_all.34.own), channel_id=1, source_target_pairs={{0,32},{32,0},{1,33},{33,1},{2,34},{34,2},{3,35},{35,3},{4,36},{36... | collective-permute-start | bytes 2162696 | tf_op jit(solution)/shard_map/ppermute | solution.py:265

commit v9 on v7

--- a/solution.py
+++ b/solution.py
@@ -18,7 +18,7 @@
 NEAR = ("zn",)
 FAR = ("zh", "zm")
 RING = FAR + NEAR
-TILE = ("core", "y", "x")
+TILE = ("y", "x", "core")
 
 BF16 = jnp.bfloat16
 F32 = jnp.float32

time: 162 us -> 162 us (level)
  no operation moved by 1% of the time
where the time goes in v9:
time: 162 us; the launch traced here: 161 us
  blocking collectives  124 us (77%)
  starting transfers between devices  22.5 us (14%)
  Pallas kernels  10.7 us (7%)
  waiting for transfers between devices  3.5 us (2%)
    all_to_all x5, blocking collectives, exchange(): return lax.all_to_all(copies, axes, 0, 0, tiled=True)  74.4 us
    all_gather x1, blocking collectives, shards(): txt = lax.all_gather(pack_txt, RING, axis=0, tiled=True)  32.7 us
    all_gather x1, blocking collectives, shards(): part = lax.all_gather(part, FAR, axis=0, tiled=True)  16.9 us
    ppermute x2, starting transfers between devices, swap_cores(): return lax.ppermute(block, 'core', [(0, 1), (1, 0)])  11.8 us
    all_to_all x1, starting transfers between devices, exchange(): return lax.all_to_all(copies, axes, 0, 0, tiled=True)  10.7 us
    ppermute x2, waiting for transfers between devices, swap_cores(): return lax.ppermute(block, 'core', [(0, 1), (1, 0)])  3.5 us
    pallas_call x1, Pallas kernels, shards(): pl.pallas_call(grad_body, out_shape=[jax.ShapeDtypeStruct(box, BF16), jax...  3.36 us
  transfers between devices with their start and end apart: 3, of which 2 were waited for; matrix products, arithmetic and copies ran while one was open for 0% of the time, Pallas kernels for 0%

profile of v9, /device:TPU:1, one launch (start us, length us, event | category | flops | bytes accessed | tf_op | source)
XLA Modules:
  0.0 161.5 jit_solution(5267034312150010857)
XLA Ops:
  0.6 2.4 %shard_map.85 = (bf16[32,16,1792]{2,1,0:T(8,128)(2,1)}, bf16[16,1536]{1,0:T(8,128)(2,1)}) custom-call(bf16[16,1024]{1,0:T(8,128)(2,1)} %refs_0_.1, bf16[16,768]{1,0:T(8,128)(2,1)} %refs_1_.1, bf16[16,1024]{1,0:T(8,128)(2,1)} %refs_2_.1, bf16[16,512]{1,0:T(8,128)(2,1)} %refs_3_.1), custom_call_target="tpu_custom_call" | custom-call | tf_op jit(solution)/shard_map/pallas_call | solution.py:282
  3.1 0.0 copy-start.1
  3.1 0.0 copy-start
  3.1 10.7 %all-to-all-start = ((bf16[32,16,1792]{2,1,0:T(8,128)(2,1)}), bf16[32,16,1792]{2,1,0:T(8,128)(2,1)S(1)}, u32[]{:S(2)}, u32[]{:S(2)}) async-start(bf16[32,16,1792]{2,1,0:T(8,128)(2,1)} %get-tuple-element.25), calls=%async_computation | async-start | bytes 3670016 | tf_op jit(solution)/shard_map/all_to_all | solution.py:264
  13.8 0.0 copy-done.1
  13.8 32.7 %all_gather.6.txt = bf16[256,1536]{1,0:T(8,128)(2,1)S(1)} all-gather(bf16[16,1536]{1,0:T(8,128)(2,1)S(1)} %copy-done.1), channel_id=1, replica_groups=mesh['zm'=2,'zn'=4,'core'=2,'y'=4,'zh'=2,'x'=4] {'zh','zm','zn'}, dimensions={0}, use_global_device_ids=true | all-gather | bytes 835584 | tf_op jit(solution)/shard_map/all_gather | solution.py:298
  46.5 0.0 all-to-all-done
  46.5 0.0 copy-done
  46.5 2.7 %shard_map.86 = (f32[32,8,128]{2,1,0:T(8,128)S(1)}, f32[16,8,128]{2,1,0:T(8,128)S(1)}, f32[512,256]{1,0:T(8,128)}, f32[512,256]{1,0:T(8,128)}, f32[512,512]{1,0:...) custom-call(bf16[512,1792]{1,0:T(8,128)(2,1)S(1)} %bitcast.3, ...), custom_call_target="tpu_custom_call" | custom-call | tf_op jit(solution)/shard_map/pallas_call | solution.py:302
  49.2 20.2 %all_to_all.30.row_all = f32[32,8,128]{2,1,0:T(8,128)S(1)} all-to-all(f32[32,8,128]{2,1,0:T(8,128)S(1)} %get-tuple-element.28), channel_id=1, replica_groups=mesh['zm'=2,'zn'=4,'core'=2,'y'=4,'zh'=2,'x'=4] {'y','x','core'}, dimensions={0} | all-to-all | bytes 262144 | tf_op jit(solution)/shard_map/all_to_all | solution.py:264
  69.5 17.7 %all_to_all.31.col_all = f32[16,8,128]{2,1,0:T(8,128)S(1)} all-to-all(f32[16,8,128]{2,1,0:T(8,128)S(1)} %get-tuple-element.30), channel_id=1, replica_groups=mesh['zm'=2,'zn'=4,'core'=2,'y'=4,'zh'=2,'x'=4] {'zh','zm','zn'}, dimensions={0} | all-to-all | bytes 131072 | tf_op jit(solution)/shard_map/all_to_all | solution.py:264
  87.1 3.4 %shard_map.87 = (bf16[16,160,128]{2,1,0:T(8,128)(2,1)S(1)}, bf16[16,160,128]{2,1,0:T(8,128)(2,1)S(1)}, f32[8,128]{1,0:T(8,128)S(1)}) custom-call(s32[1]{0:T(128)} %bitcast.core, f32[32,8,128]{2,1,0:T(8,128)S(1)} %all_to_all.30.row_all, f32[16,8,128]{2,1,0:T(8,128)S(1)} %all_to_all.31.col_all, f32[512,256]{1,0:T(8,128)} %get-tuple-element.31.refs_0_, ...), custom_call_target="tpu_custom_call" | custom-call | tf_op jit(solution)/shard_map/pallas_call | solution.py:319
  90.5 4.0 %collective-permute-start = (bf16[16,160,128]{2,1,0:T(8,128)(2,1)S(1)}, bf16[16,160,128]{2,1,0:T(8,128)(2,1)S(1)}, u32[]{:S(2)}, u32[]{:S(2)}) collective-permute-start(bf16[16,160,128]{2,1,0:T(8,128)(2,1)S(1)} %get-tuple-element.38), channel_id=1, source_target_pairs={{0,32},{32,0},{1,33},{33,1},{2,34},{34,2},{3,35},{35,3},{4,36},{36... | collective-permute-start | bytes 1966088 | tf_op jit(solution)/shard_map/ppermute | solution.py:268
  94.5 1.7 %collective-permute-done.b = bf16[16,160,128]{2,1,0:T(8,128)(2,1)S(1)} collective-permute-done((bf16[16,160,128]{2,1,0:T(8,128)(2,1)S(1)}, bf16[16,160,128]{2,1,0:T(8,128)(2,1)S(1)}, u32[]{:S(2)}, u32[]{:S(2)}) %collective-permute-start) | collective-permute-done | bytes 655392 | tf_op jit(solution)/shard_map/ppermute | solution.py:268
  96.2 0.2 shard_map.88
  96.4 15.2 %all_to_all.32.parts = bf16[16,160,128]{2,1,0:T(8,128)(2,1)S(1)} all-to-all(bf16[16,160,128]{2,1,0:T(8,128)(2,1)S(1)} %shard_map.88), channel_id=1, replica_groups=mesh['zm'=2,'zn'=4,'core'=2,'y'=4,'zh'=2,'x'=4] {'y','x'}, dimensions={0} | all-to-all | bytes 1310720 | tf_op jit(solution)/shard_map/all_to_all | solution.py:264
  111.6 0.1 shard_map.89
  111.7 8.0 %all_to_all.33.parts = bf16[4,176,128]{2,1,0:T(8,128)(2,1)S(1)} all-to-all(bf16[4,176,128]{2,1,0:T(8,128)(2,1)S(1)} %shard_map.89), channel_id=1, replica_groups=mesh['zm'=2,'zn'=4,'core'=2,'y'=4,'zh'=2,'x'=4] {'zn'}, dimensions={0} | all-to-all | bytes 360448 | tf_op jit(solution)/shard_map/all_to_all | solution.py:264
  119.7 0.1 shard_map.90
  119.7 16.9 %all_gather.7.parts = bf16[4,176,128]{2,1,0:T(8,128)(2,1)S(1)} all-gather(bf16[1,176,128]{2,1,0:T(8,128)(2,1)S(1)} %shard_map.90), channel_id=1, replica_groups=mesh['zm'=2,'zn'=4,'core'=2,'y'=4,'zh'=2,'x'=4] {'zh','zm'}, dimensions={0}, use_global_device_ids=true | all-gather | bytes 225280 | tf_op jit(solution)/shard_map/all_gather | solution.py:345
  136.7 0.1 shard_map.91
  136.8 13.3 %all_to_all.34.own = bf16[16,176,128]{2,1,0:T(8,128)(2,1)S(1)} all-to-all(bf16[16,176,128]{2,1,0:T(8,128)(2,1)S(1)} %shard_map.91), channel_id=1, replica_groups=mesh['zm'=2,'zn'=4,'core'=2,'y'=4,'zh'=2,'x'=4] {'y','x'}, dimensions={0} | all-to-all | bytes 1441792 | tf_op jit(solution)/shard_map/all_to_all | solution.py:264
  150.1 7.8 %collective-permute-start.1 = (bf16[16,176,128]{2,1,0:T(8,128)(2,1)S(1)}, bf16[16,176,128]{2,1,0:T(8,128)(2,1)S(1)}, u32[]{:S(2)}, u32[]{:S(2)}) collective-permute-start(bf16[16,176,128]{2,1,0:T(8,128)(2,1)S(1)} %all_to_all.34.own), channel_id=1, source_target_pairs={{0,32},{32,0},{1,33},{33,1},{2,34},{34,2},{3,35},{35,3},{4,36},{36... | collective-permute-start | bytes 2162696 | tf_op jit(solution)/shard_map/ppermute | solution.py:268
  157.9 1.8 %collective-permute-done.1.other = bf16[16,176,128]{2,1,0:T(8,128)(2,1)S(1)} collective-permute-done((bf16[16,176,128]{2,1,0:T(8,128)(2,1)S(1)}, bf16[16,176,128]{2,1,0:T(8,128)(2,1)S(1)}, u32[]{:S(2)}, u32[]{:S(2)}) %collective-permute-start.1) | collective-permute-done | bytes 720928 | tf_op jit(solution)/shard_map/ppermute | solution.py:268
  159.7 1.8 %shard_map.92 = (f32[1,1]{1,0:T(1,128)}, f32[768,512]{1,0:T(8,128)}, f32[512,512]{1,0:T(8,128)}) custom-call(s32[1]{0:T(128)} %bitcast.core, bf16[16,176,128]{2,1,0:T(8,128)(2,1)S(1)} %all_to_all.34.own, bf16[16,176,128]{2,1,0:T(8,128)(2,1)S(1)} %collective-permute-done.1.other), custom_call_target="tpu_custom_call" | custom-call | tf_op jit(solution)/shard_map/pallas_call | solution.py:43
Async XLA Ops:
  3.1 10.7 %copy-start.1 = (bf16[16,1536]{1,0:T(8,128)(2,1)S(1)}, bf16[16,1536]{1,0:T(8,128)(2,1)}, u32[]{:S(2)}) copy-start(bf16[16,1536]{1,0:T(8,128)(2,1)} %get-tuple-element.26) | copy-start | bytes 147460
  3.1 43.4 %copy-start = (bf16[768,512]{1,0:T(8,128)(2,1)S(1)}, bf16[768,512]{1,0:T(8,128)(2,1)}, u32[]{:S(2)}) copy-start(bf16[768,512]{1,0:T(8,128)(2,1)} %w_img.1) | copy-start | bytes 2359300
  3.1 43.4 %all-to-all-start = ((bf16[32,16,1792]{2,1,0:T(8,128)(2,1)}), bf16[32,16,1792]{2,1,0:T(8,128)(2,1)S(1)}, u32[]{:S(2)}, u32[]{:S(2)}) async-start(bf16[32,16,1792]{2,1,0:T(8,128)(2,1)} %get-tuple-element.25), calls=%async_computation | async-start | bytes 3670016 | tf_op jit(solution)/shard_map/all_to_all | solution.py:264
  90.5 5.7 %collective-permute-start = (bf16[16,160,128]{2,1,0:T(8,128)(2,1)S(1)}, bf16[16,160,128]{2,1,0:T(8,128)(2,1)S(1)}, u32[]{:S(2)}, u32[]{:S(2)}) collective-permute-start(bf16[16,160,128]{2,1,0:T(8,128)(2,1)S(1)} %get-tuple-element.38), channel_id=1, source_target_pairs={{0,32},{32,0},{1,33},{33,1},{2,34},{34,2},{3,35},{35,3},{4,36},{36... | collective-permute-start | bytes 1966088 | tf_op jit(solution)/shard_map/ppermute | solution.py:268
  150.1 9.6 %collective-permute-start.1 = (bf16[16,176,128]{2,1,0:T(8,128)(2,1)S(1)}, bf16[16,176,128]{2,1,0:T(8,128)(2,1)S(1)}, u32[]{:S(2)}, u32[]{:S(2)}) collective-permute-start(bf16[16,176,128]{2,1,0:T(8,128)(2,1)S(1)} %all_to_all.34.own), channel_id=1, source_target_pairs={{0,32},{32,0},{1,33},{33,1},{2,34},{34,2},{3,35},{35,3},{4,36},{36... | collective-permute-start | bytes 2162696 | tf_op jit(solution)/shard_map/ppermute | solution.py:268
